TPU v7x, 32 devices: a whole 2x2x4 slice. The times are simulated.
32 devices in a mesh: hi: 8 (over z, core), lo: 4 (over y, x).
Axes of the slice: x: 2, y: 2, z: 4, core: 2. Of those that a mesh axis runs over, the one named last changes fastest.
Arguments:
- amplitudes: float32 [2, 1048576], P(None, ('hi', 'lo')), may hold values from -6 to 6
- gate_mats: float32 [5, 2, 128, 128], replicated, may hold values from -0.375 to 0.375
- dev_gate: float32 [2, 2, 2], replicated, may hold values from -3 to 3
- qubit_order: int32 [15], replicated, may hold values from 0 to 14, each once
Outputs:
- final_state: float32 [2, 1048576], P(None, ('hi', 'lo'))
Inputs may be any that keep to these rules, and one draw needn't show every extreme that they name: `qubit_order`: each of the 15 positions appears exactly once.
All inputs are finite; a program needn't handle non-finite values.
Results may differ from a plain program's by a relative error of at most 0.000068.
Values sent between devices are 32-bit elements; how exact they have to be, the bound alone decides.
No kernel may reach another device: no remote copies, remote signals or barrier semaphores. Data moves between devices by JAX's collectives and lax.ppermute only.
A program may use at most 128 MiB of HBM per device.

v0:
```python
import jax
import jax.numpy as jnp
from jax import lax
from jax.sharding import PartitionSpec as P


def swapped(block, axis, stride):
    count = lax.axis_size(axis)
    route = []
    for low in range(count):
        high = low | 1 << stride
        if high != low and high < count:
            route += [(low, high), (high, low)]
    return lax.ppermute(block, axis, route)


def apply_matrix(matrix, values, pattern):
    mix_rr = jnp.einsum(pattern, matrix[0], values[0], precision=lax.Precision.HIGHEST)
    mix_ii = jnp.einsum(pattern, matrix[1], values[1], precision=lax.Precision.HIGHEST)
    mix_ri = jnp.einsum(pattern, matrix[0], values[1], precision=lax.Precision.HIGHEST)
    mix_ir = jnp.einsum(pattern, matrix[1], values[0], precision=lax.Precision.HIGHEST)
    return jnp.stack([mix_rr - mix_ii, mix_ri + mix_ir])


def low_gate(matrix, values):
    gate_width = matrix.shape[-1]
    shaped = values.reshape(2, -1, gate_width)
    return apply_matrix(matrix, shaped, "ab,mb->ma").reshape(values.shape)


def high_gate(matrix, values):
    gate_width = matrix.shape[-1]
    shaped = values.reshape(2, gate_width, -1)
    return apply_matrix(matrix, shaped, "ab,bm->am").reshape(values.shape)


def mix_pair(dev_gate, row_index, lower_pair, upper_pair):
    coef_0r = dev_gate[0, row_index, 0]
    coef_0i = dev_gate[1, row_index, 0]
    coef_1r = dev_gate[0, row_index, 1]
    coef_1i = dev_gate[1, row_index, 1]
    real_part = (
        coef_0r * lower_pair[0]
        - coef_0i * lower_pair[1]
        + (coef_1r * upper_pair[0] - coef_1i * upper_pair[1])
    )
    imag_part = (
        coef_0r * lower_pair[1]
        + coef_0i * lower_pair[0]
        + (coef_1r * upper_pair[1] + coef_1i * upper_pair[0])
    )
    return jnp.stack([real_part, imag_part])


def reorder_bits(state_now, qubit_order):
    amp_count = state_now.shape[1]
    positions = jnp.arange(amp_count, dtype=jnp.int32)
    source = jnp.zeros((amp_count,), jnp.int32)
    for position in range(qubit_order.shape[0]):
        source = source + jnp.left_shift(
            jnp.right_shift(positions, position) & 1, qubit_order[position]
        )
    return jnp.take(state_now, source, axis=1)


def on_device(amplitudes, gate_mats, dev_gate, qubit_order):
    gate_width = gate_mats.shape[-1]
    pair_bit = lax.axis_size("hi").bit_length() - 2
    top_bit = jnp.right_shift(lax.axis_index("hi"), pair_bit) & 1
    partner = swapped(amplitudes, "hi", pair_bit)
    lower_pair = jnp.where(top_bit == 0, amplitudes, partner)
    upper_pair = jnp.where(top_bit == 0, partner, amplitudes)
    state_now = mix_pair(dev_gate, top_bit, lower_pair, upper_pair)
    state_now = high_gate(gate_mats[0], state_now)
    state_now = low_gate(gate_mats[1], state_now)
    state_now = reorder_bits(state_now, qubit_order)
    groups = lax.axis_size("lo")
    blocks = state_now.reshape(2, groups, -1, gate_width)
    exchanged = lax.all_to_all(blocks, "lo", split_axis=1, concat_axis=1, tiled=True).reshape(2, -1)
    state_now = high_gate(gate_mats[2], exchanged)
    state_now = low_gate(gate_mats[3], state_now)
    state_now = high_gate(gate_mats[4], state_now)
    return state_now


def solution(mesh):
    return jax.shard_map(
        on_device,
        mesh=mesh,
        in_specs=(P(None, ("hi", "lo")), P(), P(), P()),
        out_specs=P(None, ("hi", "lo")),
        check_vma=False,
    )
```

profile of v0, /device:TPU:0, one launch (start us, length us, event | category | flops | bytes accessed | tf_op | source)
XLA Modules:
  0.0 191.2 jit_solution(3666460535472623201)
XLA Ops:
  0.0 4.0 %collective-permute-start = (f32[2,32768]{1,0:T(2,128)}, f32[2,32768]{1,0:T(2,128)S(1)}, u32[]{:S(2)}, u32[]{:S(2)}) collective-permute-start(f32[2,32768]{1,0:T(2,128)} %param.4), channel_id=1, source_target_pairs={{0,16},{16,0},{4,20},{20,4},{8,24},{24,8},{12,28},{28,12},{1,17},{... | collective-permute-start | bytes 786440 | tf_op jit(solution)/shard_map/ppermute | solution.py:14
  4.0 1.9 fusion.57
  5.9 11.4 %compare_select_fusion = s32[32768,1]{0,1:T(1,128)S(1)} fusion(s32[]{:T(128)} %bitcast.14, s32[]{:T(128)} %bitcast.13, s32[]{:T(128)} %bitcast.12, s32[]{:T(128)} %bitcast.11, s32[]{:T(128)} %bitcast.10, s32[]{:T(128)} %bitcast.9, s32[]{:T(128)} %bitcast.8, s32[]{:T(128)} %bitcast.7, s32[]{:T(128)} %bitcast.6, s32[]{:T(128)} %bitcast.5, s32[]{:T(128)} %bitcast.4, ...), kind=kLoop, calls=%fused_computation.17 | loop fusion | flops 2031616 | bytes 131132 | tf_op jit(solution)/shard_map/jit(_take)/jit(_where)/select_n | solution.py:63
  17.4 1.4 constant_dynamic-slice_fusion.3
  18.8 9.6 %compare_and_fusion = pred[4,64,128]{2,1,0:T(8,128)(4,1)S(1)} fusion(s32[]{:T(128)} %bitcast.14, s32[]{:T(128)} %bitcast.13, s32[]{:T(128)} %bitcast.12, s32[]{:T(128)} %bitcast.11, s32[]{:T(128)} %bitcast.10, s32[]{:T(128)} %bitcast.9, s32[]{:T(128)} %bitcast.8, s32[]{:T(128)} %bitcast.7, s32[]{:T(128)} %bitcast.6, s32[]{:T(128)} %bitcast.5, s32[]{:T(128)} %bitcast.4, ...), kind=kLoop, calls=%fused_computation.26 | loop fusion | flops 2260992 | bytes 32828 | tf_op jit(solution)/shard_map/jit(_take)/and | solution.py:63
  28.4 1.1 broadcast_select_fusion.1
  29.5 3.7 %add_reduce_fusion.1 = (f32[32768]{0:T(1024)S(1)}, f32[32768]{0:T(1024)S(1)}) fusion(f32[2,32768]{1,0:T(2,128)S(1)} %get-tuple-element.8, f32[2,32768]{1,0:T(2,128)S(1)} %get-tuple-element.7, f32[]{:T(128)} %bitcast.18, f32[]{:T(128)} %bitcast.17, f32[]{:T(128)} %bitcast.16, f32[]{:T(128)} %bitcast.15), kind=kLoop, calls=%fused_computation.25 | loop fusion | flops 458752 | bytes 786448 | tf_op jit(solution)/shard_map/add | solution.py:43
  33.3 1.2 fusion.34
  34.6 1.2 fusion.32
  35.8 1.2 fusion.5
  37.1 1.1 fusion.28
  38.3 1.2 fusion.4
  39.6 1.1 fusion.26
  40.8 1.1 convolution_subtract_fusion.3
  41.9 1.1 convolution_add_fusion.3
  43.3 8.4 %copy.18 = f32[2,32768]{0,1:T(8,128)} copy(f32[2,32768]{1,0:T(2,128)S(1)} %pad_maximum_fusion) | data formatting | bytes 524288 | tf_op jit(solution)/shard_map/stack | solution.py:22
  51.6 114.2 %gather_fusion = f32[32768,2]{1,0:T(8,128)} fusion(f32[2,32768]{0,1:T(8,128)} %copy.18, s32[32768]{0:T(1024)S(1)} %broadcast_clamp_fusion), kind=kCustom, calls=%fused_computation | custom fusion | bytes 655360 | tf_op jit(solution)/shard_map/jit(_take)/gather | solution.py:63
  165.8 10.0 %copy.19 = f32[2,4,64,128]{3,2,0,1:T(8,128)S(1)} copy(f32[2,4,64,128]{0,3,2,1:T(8,128)} %bitcast.121) | data formatting | bytes 524288 | tf_op jit(solution)/shard_map/jit(_take)/gather | solution.py:63
  175.8 9.2 %all_to_all.5 = f32[2,4,64,128]{3,2,0,1:T(8,128)S(1)} all-to-all(f32[2,4,64,128]{3,2,0,1:T(8,128)S(1)} %broadcast_select_fusion.2), channel_id=1, replica_groups=mesh['hi'=8,'lo'=4] {'lo'}, dimensions={1} | all-to-all | bytes 524288 | tf_op jit(solution)/shard_map/all_to_all | solution.py:79
  185.9 0.4 fusion.3
  186.7 0.4 fusion.2
  189.0 0.4 fusion.1
  189.6 0.4 fusion
  190.3 0.9 pad_maximum_fusion.1
  (33 shorter events, 4.1 us)
Async XLA Ops:
  0.0 28.4 %collective-permute-start = (f32[2,32768]{1,0:T(2,128)}, f32[2,32768]{1,0:T(2,128)S(1)}, u32[]{:S(2)}, u32[]{:S(2)}) collective-permute-start(f32[2,32768]{1,0:T(2,128)} %param.4), channel_id=1, source_target_pairs={{0,16},{16,0},{4,20},{20,4},{8,24},{24,8},{12,28},{28,12},{1,17},{... | collective-permute-start | bytes 786440 | tf_op jit(solution)/shard_map/ppermute | solution.py:14
  43.3 141.8 %copy-start = (f32[5,2,128,128]{3,2,1,0:T(8,128)S(1)}, f32[5,2,128,128]{3,2,1,0:T(8,128)}, u32[]{:S(2)}) copy-start(f32[5,2,128,128]{3,2,1,0:T(8,128)} %param.5) | copy-start | bytes 1966084
where the time goes:
time: 192 us; the launch traced here: 191 us
  local copies, waits for them, and re-layouts  137 us (71%)
  other arithmetic  27 us (14%)
  matrix products  13.6 us (7%)
  blocking collectives  9.23 us (5%)
  starting transfers between devices  4.04 us (2%)
    gather x2, local copies, waits for them, and re-layouts, reorder_bits(): return jnp.take(state_now, source, axis=1)  124 us
    select_n x2, other arithmetic, reorder_bits(): return jnp.take(state_now, source, axis=1)  11.4 us
    and x1, other arithmetic, reorder_bits(): return jnp.take(state_now, source, axis=1)  9.59 us
    all_to_all x1, blocking collectives, on_device(): lax.all_to_all(blocks, 'lo', split_axis=1, concat_axis=1, tiled=True)  9.23 us
    another operation x1, local copies, waits for them, and re-layouts, apply_matrix(): return jnp.stack([mix_rr - mix_ii, mix_ri + mix_ir])  8.36 us
    ppermute x1, starting transfers between devices, swapped(): return lax.ppermute(block, axis, route)  4.04 us
  transfers between devices with their start and end apart: 1, of which 0 were waited for; matrix products, arithmetic and copies ran while one was open for 13% of the time, Pallas kernels for 0%

commit v1 on v0

v1 whole, which is shorter than its diff:
```python
import functools

import jax
import jax.numpy as jnp
from jax import lax
from jax.experimental import pallas as pl
from jax.experimental.pallas import tpu as pltpu
from jax.sharding import PartitionSpec as P

WIDTH = 128
LANE_BITS = 7
ROW_BITS = 8
F32, BF16 = jnp.float32, jnp.bfloat16


def halves(value):
    high = value.astype(BF16)
    return high, (value - high.astype(F32)).astype(BF16)


def dot(left, right, transposed=False):
    return lax.dot_general(
        left, right, (((1,), (1 if transposed else 0,)), ((), ())), preferred_element_type=F32
    )


def dot3(left, right, transposed=False):
    (lh, ll), (rh, rl) = left, right
    return dot(lh, rl, transposed) + dot(ll, rh, transposed) + dot(lh, rh, transposed)


def block_matrix(real, imag):
    return jnp.concatenate(
        [jnp.concatenate([real, -imag], axis=1), jnp.concatenate([imag, real], axis=1)], axis=0
    )


def new_positions(lo_bits):
    kept = LANE_BITS - lo_bits
    return [8 + r for r in range(kept)] + [7] + [8 + r for r in range(kept, LANE_BITS)]


def plan_of(order, lo_bits):
    one, zero = jnp.int32(1), jnp.int32(0)
    middle = LANE_BITS - lo_bits
    row_of_lane = [l if l < middle else l + 1 for l in range(LANE_BITS)]
    wanted = [order[k] for k in new_positions(lo_bits)]
    crosses = [jnp.where(w < LANE_BITS, one, zero) for w in wanted]
    crosses_middle = crosses[middle]
    used, before = [], zero
    spare = zero
    for l in range(LANE_BITS):
        free = (one - crosses[row_of_lane[l]]) * crosses_middle * jnp.where(before == 0, one, zero)
        spare = spare + free * l
        used.append(crosses[row_of_lane[l]] + free)
        before = before + free
    key_lane, moved, stayed = [], zero, zero
    for l in range(LANE_BITS):
        key_lane.append(jnp.where(used[l] == 1, moved + 16, stayed))
        moved, stayed = moved + used[l], stayed + (one - used[l])
    key_new, moved, stayed = [], zero, zero
    for k in range(LANE_BITS):
        from_row = jnp.where(order[k] >= LANE_BITS, one, zero)
        key_new.append(jnp.where(from_row == 1, moved + 16, stayed))
        moved, stayed = moved + from_row, stayed + (one - from_row)
    match = []
    for l in range(LANE_BITS):
        total = zero
        for k in range(LANE_BITS):
            total = total + jnp.where(key_lane[l] == key_new[k], order[k] + 16 * k, zero)
        match.append(total)
    new_in_lane = [m >> 4 for m in match]
    lane_before, row_before = [], [None] * ROW_BITS
    middle_before = zero
    for l in range(LANE_BITS):
        r = row_of_lane[l]
        old = match[l] & 15
        at_spare = crosses_middle * jnp.where(spare == l, one, zero)
        lane_before.append(jnp.where(crosses[r] == 1, wanted[r], jnp.where(at_spare == 1, wanted[middle], old)))
        row_before[r] = jnp.where(crosses[r] == 1, old, wanted[r]) & 7
        middle_before = middle_before + at_spare * old
    row_before[middle] = jnp.where(crosses_middle == 1, middle_before, wanted[middle]) & 7
    return crosses, spare, row_before, lane_before, new_in_lane


def moved_bits(index, sources, targets):
    total = jnp.zeros_like(index)
    for source, target in zip(sources, targets, strict=True):
        total = total | (((index >> source) & 1) << target)
    return total


def one_hot(count, index):
    rows = lax.broadcasted_iota(jnp.int32, (count, index.shape[1]), 0)
    return jnp.where(rows == index, 1.0, 0.0).astype(F32).astype(BF16)


def bit_exchange(low, high, lane, crosses, lane_bit, shift):
    up = ((lane >> lane_bit) & 1) * crosses
    down = (1 - ((lane >> lane_bit) & 1)) * crosses
    return (
        jnp.where(up == 1, pltpu.roll(high, shift, 1), low),
        jnp.where(down == 1, pltpu.roll(low, WIDTH - shift, 1), high),
    )


def first_kernel(lo_bits, order_ref, x_ref, gates_ref, *refs):
    outs, (work, blocks) = refs[:-2], refs[-2:]
    parts = 1 << lo_bits
    order = [order_ref[k] for k in range(LANE_BITS + ROW_BITS)]
    crosses, spare, row_before, lane_before, _ = plan_of(order, lo_bits)
    middle = LANE_BITS - lo_bits
    pieces = [[x_ref[pl.ds(m * 2 + c, WIDTH, stride=4), :] for m in range(2)] for c in range(2)]
    state = jnp.concatenate([jnp.concatenate(row, axis=1) for row in pieces], axis=0)
    real, imag = halves(gates_ref[0, 0]), halves(gates_ref[0, 1])
    matrix = [block_matrix(real[i], imag[i]) for i in range(2)]
    state = dot3(matrix, halves(state))
    state = jnp.concatenate(
        [
            jnp.concatenate([state[c * WIDTH : (c + 1) * WIDTH, m * WIDTH : (m + 1) * WIDTH] for c in range(2)], axis=1)
            for m in range(2)
        ],
        axis=0,
    )
    index = lax.broadcasted_iota(jnp.int32, (1, 2 * WIDTH), 1)
    rows = one_hot(2 * WIDTH, moved_bits(index, row_before, range(ROW_BITS)))
    state = [dot(rows, half).astype(BF16) for half in halves(state)]
    index = lax.broadcasted_iota(jnp.int32, (1, WIDTH), 1)
    lanes = one_hot(WIDTH, moved_bits(index, lane_before, range(LANE_BITS)))
    real, imag = halves(gates_ref[1, 0]), halves(gates_ref[1, 1])
    matrix = [
        block_matrix(dot(lanes, real[i]).astype(BF16), dot(lanes, imag[i]).astype(BF16)) for i in range(2)
    ]
    state = dot3(state, matrix, transposed=True)
    for c in range(2):
        work[c] = state[:, c * WIDTH : (c + 1) * WIDTH]
    lane = lax.broadcasted_iota(jnp.int32, (8, WIDTH), 1)

    def exchange(values, row_bit, bit):
        if row_bit == middle:
            lane_bit, shift = spare, jnp.left_shift(jnp.int32(1), spare)
        else:
            lane_bit = row_bit if row_bit < middle else row_bit - 1
            shift = 1 << lane_bit
        for i in range(len(values)):
            if not i >> bit & 1:
                j = i | 1 << bit
                values[i], values[j] = bit_exchange(values[i], values[j], lane, crosses[row_bit], lane_bit, shift)

    for c in range(2):
        for group in range(4):
            places = [pl.ds(group * 64 + o, 8, stride=8) for o in range(8)]
            values = [work[c, place, :] for place in places]
            for row_bit in range(3):
                exchange(values, row_bit, row_bit)
            for place, value in zip(places, values, strict=True):
                work[c, place, :] = value
    me = lax.axis_index("lo")
    kept = WIDTH // parts
    for c in range(2):
        values = [work[c, pl.ds(8 * v, 8), :] for v in range(32)]
        for row_bit in range(3, ROW_BITS):
            exchange(values, row_bit, row_bit - 3)
        each = 32 // parts
        for part in range(parts):
            step = jnp.bitwise_xor(me, part)
            for v in range(each):
                m, h = divmod(8 * v, kept)
                blocks[step, c, m, pl.ds(h, 8), :] = values[part * each + v]
    at = 0
    for out in outs:
        out[...] = blocks[at : at + out.shape[0]]
        at += out.shape[0]


def mixed(coefs, own, other):
    own_r, own_i, other_r, other_i = coefs
    return (
        own_r * own[0] - own_i * own[1] + (other_r * other[0] - other_i * other[1]),
        own_r * own[1] + own_i * own[0] + (other_r * other[1] + other_i * other[0]),
    )


def coefs_of(gate_ref, side):
    other = 1 - side
    return gate_ref[0, side, side], gate_ref[1, side, side], gate_ref[0, side, other], gate_ref[1, side, other]


def side_of():
    return jnp.right_shift(lax.axis_index("hi"), lax.axis_size("hi").bit_length() - 2) & 1


def mix_kernel(gate_ref, own_ref, other_ref, out_ref):
    coefs = coefs_of(gate_ref, side_of())
    for b in range(own_ref.shape[0]):
        out_ref[b, 0], out_ref[b, 1] = mixed(coefs, own_ref.at[b], other_ref.at[b])


def weights_kernel(lo_bits, order_ref, gate2_ref, gate3_ref, gate4_ref, high_ref, low_ref):
    order = [order_ref[k] for k in range(LANE_BITS + ROW_BITS)]
    new_in_lane = plan_of(order, lo_bits)[4]
    index = lax.broadcasted_iota(jnp.int32, (1, WIDTH), 1)
    lanes = one_hot(WIDTH, moved_bits(index, range(LANE_BITS), new_in_lane))
    for g, ref in enumerate((gate2_ref, gate3_ref, gate4_ref)):
        real, imag = halves(ref[0, 0]), halves(ref[0, 1])
        for i, out in enumerate((high_ref, low_ref)):
            parts = real[i], imag[i]
            if g == 1:
                parts = [dot(part, lanes).astype(BF16) for part in parts]
            out[g] = block_matrix(*parts)


def last_kernel(groups, gate_ref, high_ref, low_ref, *refs):
    ins, (out_ref, state_ref) = refs[:-2], refs[-2:]
    me = lax.axis_index("lo")
    coefs = coefs_of(gate_ref, side_of())
    step = 0
    for kind, count in groups:
        if kind == "pair":
            own, other, ins = ins[0], ins[1], ins[2:]
        else:
            own, ins = ins[0], ins[1:]
        for b in range(count):
            kept = own.shape[3]
            source = pl.multiple_of(jnp.bitwise_xor(me, step) * kept, 8)
            parts = mixed(coefs, own.at[b], other.at[b]) if kind == "pair" else (own[b, 0], own[b, 1])
            for c in range(2):
                for m in range(2):
                    state_ref[c, m, pl.ds(source, kept), :] = parts[c][m]
            step += 1
    matrix = [(high_ref[g], low_ref[g]) for g in range(3)]
    state = jnp.concatenate(
        [jnp.concatenate([state_ref[c, m] for m in range(2)], axis=1) for c in range(2)], axis=0
    )

    def turned(value):
        return jnp.concatenate(
            [
                jnp.concatenate([value[i * WIDTH : (i + 1) * WIDTH, j * WIDTH : (j + 1) * WIDTH] for i in range(2)], axis=1)
                for j in range(2)
            ],
            axis=0,
        )

    state = dot3(matrix[0], halves(state))
    state = dot3(halves(turned(state)), matrix[1], transposed=True)
    state = dot3(matrix[2], halves(turned(state)))
    for c in range(2):
        for m in range(2):
            out_ref[pl.ds(m * 2 + c, WIDTH, stride=4), :] = state[c * WIDTH : (c + 1) * WIDTH, m * WIDTH : (m + 1) * WIDTH]


def swapped(block, axis, distance):
    count = lax.axis_size(axis)
    return lax.ppermute(block, axis, [(i, i ^ distance) for i in range(count)])


SMEM = pl.BlockSpec(memory_space=pltpu.SMEM)
VMEM = pl.BlockSpec(memory_space=pltpu.VMEM)


def on_device(amplitudes, gate_mats, dev_gate, qubit_order):
    parts = lax.axis_size("lo")
    lo_bits = parts.bit_length() - 1
    top = lax.axis_size("hi") // 2
    kept = WIDTH // parts
    rows = amplitudes.reshape(2, 256, WIDTH).transpose(1, 0, 2).reshape(512, WIDTH)

    def block(count):
        return jax.ShapeDtypeStruct((count, 2, 2, kept, WIDTH), F32)

    def gate_spec(g, count):
        return pl.BlockSpec((count, 2, WIDTH, WIDTH), lambda i: (g, 0, 0, 0))

    near = parts // 2
    first = pl.pallas_call(
        functools.partial(first_kernel, lo_bits),
        grid=(1,),
        out_shape=[block(near)] + [block(1)] * (parts - near),
        in_specs=[SMEM, VMEM, gate_spec(0, 2)],
        out_specs=[VMEM] * (1 + parts - near),
        scratch_shapes=[
            pltpu.VMEM((2, 256, WIDTH), F32),
            pltpu.VMEM((parts, 2, 2, kept, WIDTH), F32),
        ],
        name="first_gates",
    )(qubit_order, rows, gate_mats)
    near_own, far_own = first[0], first[1:]
    near_other = swapped(near_own, "hi", top)
    far_own = [swapped(far, "lo", near + i) for i, far in enumerate(far_own)]
    far_other = [swapped(far, "hi", top) for far in far_own]
    high, low = pl.pallas_call(
        functools.partial(weights_kernel, lo_bits),
        grid=(1,),
        out_shape=[jax.ShapeDtypeStruct((3, 256, 256), BF16)] * 2,
        in_specs=[SMEM] + [gate_spec(2 + g, 1) for g in range(3)],
        out_specs=[VMEM] * 2,
        name="gate_weights",
    )(qubit_order, gate_mats, gate_mats, gate_mats)
    near_mixed = pl.pallas_call(
        mix_kernel, out_shape=block(near), in_specs=[SMEM, VMEM, VMEM], out_specs=VMEM, name="mix_pair"
    )(dev_gate, near_own, near_other)
    arrived = [near_mixed[0:1]] + [swapped(near_mixed[k : k + 1], "lo", k) for k in range(1, near)]
    operands = arrived
    groups = [("mixed", 1)] * near
    for own, other in zip(far_own, far_other, strict=True):
        operands = operands + [own, other]
        groups = groups + [("pair", 1)]
    out = pl.pallas_call(
        functools.partial(last_kernel, tuple(groups)),
        out_shape=jax.ShapeDtypeStruct((512, WIDTH), F32),
        in_specs=[SMEM] + [VMEM] * (2 + len(operands)),
        out_specs=VMEM,
        scratch_shapes=[pltpu.VMEM((2, 2, WIDTH, WIDTH), F32)],
        name="last_gates",
    )(dev_gate, high, low, *operands)
    return out.reshape(256, 2, WIDTH).transpose(1, 0, 2).reshape(2, -1)


def solution(mesh):
    return jax.shard_map(
        on_device,
        mesh=mesh,
        in_specs=(P(None, ("hi", "lo")), P(), P(), P()),
        out_specs=P(None, ("hi", "lo")),
        check_vma=False,
    )
```

time: 192 us -> 26.6 us (0.14)
  local copies, waits for them, and re-layouts: 137 us -> 2.79 us
  other arithmetic: 27 us -> 0 us
  matrix products: 13.6 us -> 0 us
  Pallas kernels: 0 us -> 10.1 us
  blocking collectives: 9.23 us -> 0 us
  starting transfers between devices: 4.04 us -> 8.99 us
  waiting for transfers between devices: 0.01 us -> 4.48 us
    gather x2 -> x0, local copies, waits for them, and re-layouts: 124 us -> none  [reorder_bits(): return jnp.take(state_now, source, axis=1)]
    dot_general x20 -> x0, matrix products: 13.6 us -> none  [the longest x5 3.4 us: apply_matrix(): jnp.einsum(pattern, matrix[1], values[1], precision=lax.Precision.HIGHEST)]
    select_n x3 -> x0, other arithmetic: 12.6 us -> none  [the longest x2 11.4 us: reorder_bits(): return jnp.take(state_now, source, axis=1)]
    pallas_call x0 -> x4, Pallas kernels: none -> 10.1 us  [the longest x1 3.33 us: on_device(): pl.pallas_call(functools.partial(first_kernel, lo_bits), grid=(1,), out_s...]
    and x1 -> x0, other arithmetic: 9.59 us -> none  [reorder_bits(): return jnp.take(state_now, source, axis=1)]
    all_to_all x1 -> x0, blocking collectives: 9.23 us -> none  [on_device(): lax.all_to_all(blocks, 'lo', split_axis=1, concat_axis=1, tiled=True)]
    another operation x1 -> x0, local copies, waits for them, and re-layouts: 8.36 us -> none  [apply_matrix(): return jnp.stack([mix_rr - mix_ii, mix_ri + mix_ir])]
    ppermute x1 -> x6, starting transfers between devices: 4.04 us -> 8.99 us  [swapped(): return lax.ppermute(block, axis, [(i, i ^ distance) for i in range(count)])]
  transfers between devices with their start and end apart: 1 -> 6, of which waited for: 0 -> 3; matrix products, arithmetic and copies ran while one was open for 13% -> 6% of each run, Pallas kernels for 0% -> 15%
where the time goes in v1:
time: 26.6 us; the launch traced here: 26.4 us
  Pallas kernels  10.1 us (38%)
  starting transfers between devices  8.99 us (34%)
  waiting for transfers between devices  4.48 us (17%)
  local copies, waits for them, and re-layouts  2.79 us (10%)
    ppermute x6, starting transfers between devices, swapped(): return lax.ppermute(block, axis, [(i, i ^ distance) for i in range(count)])  8.99 us
    ppermute x6, waiting for transfers between devices, swapped(): return lax.ppermute(block, axis, [(i, i ^ distance) for i in range(count)])  4.48 us
    pallas_call x1, Pallas kernels, on_device(): pl.pallas_call(functools.partial(first_kernel, lo_bits), grid=(1,), out_s...  3.33 us
    pallas_call x1, Pallas kernels, on_device(): pl.pallas_call(functools.partial(last_kernel, tuple(groups)), out_shape=j...  2.86 us
    pallas_call x1, Pallas kernels, on_device(): pl.pallas_call(functools.partial(weights_kernel, lo_bits), grid=(1,), out...  2.22 us
    pallas_call x1, Pallas kernels, on_device(): pl.pallas_call(mix_kernel, out_shape=block(near), in_specs=[SMEM, VMEM, V...  1.67 us
    slice x1, local copies, waits for them, and re-layouts, on_device(): near_mixed[k:k + 1]  1.5 us
    unnamed x12, local copies, waits for them, and re-layouts  1.29 us
  transfers between devices with their start and end apart: 6, of which 3 were waited for; matrix products, arithmetic and copies ran while one was open for 6% of the time, Pallas kernels for 15%

profile of v1, /device:TPU:0, one launch (start us, length us, event | category | flops | bytes accessed | tf_op | source)
XLA Modules:
  0.0 26.4 jit_solution(4239849146429742361)
XLA Ops:
  0.0 3.3 %first_gates.1 = (f32[2,2,2,32,128]{4,3,2,1,0:T(8,128)}, f32[1,2,2,32,128]{4,3,2,1,0:T(8,128)}, f32[1,2,2,32,128]{4,3,2,1,0:T(8,128)}) custom-call(s32[15]{0:T(128)} %order_ref.3, f32[512,128]{1,0:T(8,128)} %bitcast.10, f32[5,2,128,128]{3,2,1,0:T(8,128)} %gates_ref.1), custom_call_target="tpu_custom_call" | custom-call | tf_op jit(solution)/shard_map/first_gates/pallas_call | solution.py:276
  3.3 4.0 %collective-permute-start = (f32[2,2,2,32,128]{4,3,2,1,0:T(8,128)}, f32[2,2,2,32,128]{4,3,2,1,0:T(8,128)S(1)}, u32[]{:S(2)}, u32[]{:S(2)}) collective-permute-start(f32[2,2,2,32,128]{4,3,2,1,0:T(8,128)} %get-tuple-element.12.own_ref), channel_id=1, source_target_pairs={{0,16},{4,20},{8,24},{12,28},{16,0},{20,4},{24,8},{28,12},{1,17},{... | collective-permute-start | bytes 393224 | tf_op jit(solution)/shard_map/ppermute | solution.py:255
  7.4 1.5 %collective-permute-start.2 = (f32[1,2,2,32,128]{4,3,2,1,0:T(8,128)}, f32[1,2,2,32,128]{4,3,2,1,0:T(8,128)S(1)}, u32[]{:S(2)}, u32[]{:S(2)}) collective-permute-start(f32[1,2,2,32,128]{4,3,2,1,0:T(8,128)} %get-tuple-element.13), channel_id=1, source_target_pairs={{0,2},{1,3},{2,0},{3,1},{4,6},{5,7},{6,4},{7,5},{8,10},{9,11},{10,... | collective-permute-start | bytes 196616 | tf_op jit(solution)/shard_map/ppermute | solution.py:255
  8.9 1.4 %collective-permute-start.4 = (f32[1,2,2,32,128]{4,3,2,1,0:T(8,128)}, f32[1,2,2,32,128]{4,3,2,1,0:T(8,128)S(1)}, u32[]{:S(2)}, u32[]{:S(2)}) collective-permute-start(f32[1,2,2,32,128]{4,3,2,1,0:T(8,128)} %get-tuple-element.14), channel_id=1, source_target_pairs={{0,3},{1,2},{2,1},{3,0},{4,7},{5,6},{6,5},{7,4},{8,11},{9,10},{10,... | collective-permute-start | bytes 196616 | tf_op jit(solution)/shard_map/ppermute | solution.py:255
  10.3 1.5 %collective-permute-done.2.refs_2_ = f32[1,2,2,32,128]{4,3,2,1,0:T(8,128)S(1)} collective-permute-done((f32[1,2,2,32,128]{4,3,2,1,0:T(8,128)}, f32[1,2,2,32,128]{4,3,2,1,0:T(8,128)S(1)}, u32[]{:S(2)}, u32[]{:S(2)}) %collective-permute-start.2) | collective-permute-done | bytes 65568 | tf_op jit(solution)/shard_map/ppermute | solution.py:255
  11.8 0.0 collective-permute-start.3
  11.8 2.4 %collective-permute-done.4.refs_4_ = f32[1,2,2,32,128]{4,3,2,1,0:T(8,128)S(1)} collective-permute-done((f32[1,2,2,32,128]{4,3,2,1,0:T(8,128)}, f32[1,2,2,32,128]{4,3,2,1,0:T(8,128)S(1)}, u32[]{:S(2)}, u32[]{:S(2)}) %collective-permute-start.4) | collective-permute-done | bytes 65568 | tf_op jit(solution)/shard_map/ppermute | solution.py:255
  14.3 0.5 %collective-permute-start.5 = (f32[1,2,2,32,128]{4,3,2,1,0:T(8,128)S(1)}, f32[1,2,2,32,128]{4,3,2,1,0:T(8,128)S(1)}, u32[]{:S(2)}, u32[]{:S(2)}) collective-permute-start(f32[1,2,2,32,128]{4,3,2,1,0:T(8,128)S(1)} %collective-permute-done.4.refs_4_), channel_id=1, source_target_pairs={{0,16},{4,20},{8,24},{12,28},{16,0},{20,4},{24,8},{28,12},{1,17},{... | collective-permute-start | bytes 196616 | tf_op jit(solution)/shard_map/ppermute | solution.py:255
  14.8 0.0 collective-permute-done.other_ref
  14.8 0.6 %copy-done = f32[2,2,2,32,128]{4,3,2,1,0:T(8,128)} copy-done((f32[2,2,2,32,128]{4,3,2,1,0:T(8,128)}, f32[2,2,2,32,128]{4,3,2,1,0:T(8,128)S(1)}, u32[]{:S(2)}) %copy-start) | copy-done | bytes 131096
  15.4 1.7 %mix_pair.1 = f32[2,2,2,32,128]{4,3,2,1,0:T(8,128)} custom-call(f32[2,2,2]{2,1,0:T(2,128)} %gate_ref.3, f32[2,2,2,32,128]{4,3,2,1,0:T(8,128)} %get-tuple-element.12.own_ref, f32[2,2,2,32,128]{4,3,2,1,0:T(8,128)} %copy-done), custom_call_target="tpu_custom_call" | custom-call | tf_op jit(solution)/shard_map/mix_pair/pallas_call | solution.py:300
  17.1 0.0 copy-done.1
  17.1 0.0 copy-done.2
  17.1 1.5 %fusion = (f32[1,2,2,32,128]{4,3,2,1,0:T(8,128)S(1)}, f32[1,2,2,32,128]{4,3,2,1,0:T(8,128)}) fusion(f32[2,2,2,32,128]{4,3,2,1,0:T(8,128)} %mix_pair.1), kind=kLoop, calls=%fused_computation | loop fusion | bytes 262144 | tf_op jit(solution)/shard_map/slice | solution.py:303
  18.6 1.5 %collective-permute-start.1 = (f32[1,2,2,32,128]{4,3,2,1,0:T(8,128)S(1)}, f32[1,2,2,32,128]{4,3,2,1,0:T(8,128)S(1)}, u32[]{:S(2)}, u32[]{:S(2)}) collective-permute-start(f32[1,2,2,32,128]{4,3,2,1,0:T(8,128)S(1)} %get-tuple-element.15), channel_id=1, source_target_pairs={{0,1},{1,0},{2,3},{3,2},{4,5},{5,4},{6,7},{7,6},{8,9},{9,8},{10,11... | collective-permute-start | bytes 196616 | tf_op jit(solution)/shard_map/ppermute | solution.py:255
  20.1 2.2 %gate_weights.1 = (bf16[3,256,256]{2,1,0:T(8,128)(2,1)}, bf16[3,256,256]{2,1,0:T(8,128)(2,1)}) custom-call(s32[15]{0:T(128)} %order_ref.3, f32[5,2,128,128]{3,2,1,0:T(8,128)} %gates_ref.1, f32[5,2,128,128]{3,2,1,0:T(8,128)} %gates_ref.1, f32[5,2,128,128]{3,2,1,0:T(8,128)} %gates_ref.1), custom_call_target="tpu_custom_call" | custom-call | tf_op jit(solution)/shard_map/gate_weights/pallas_call | solution.py:292
  22.3 0.0 collective-permute-done.3.refs_3_
  22.3 0.0 collective-permute-done.5.refs_5_
  22.3 0.0 copy-start.4
  22.3 0.5 %collective-permute-done.1.refs_1_ = f32[1,2,2,32,128]{4,3,2,1,0:T(8,128)S(1)} collective-permute-done((f32[1,2,2,32,128]{4,3,2,1,0:T(8,128)S(1)}, f32[1,2,2,32,128]{4,3,2,1,0:T(8,128)S(1)}, u32[]{:S(2)}, u32[]{:S(2)}) %collective-permute-start.1) | collective-permute-done | bytes 65568 | tf_op jit(solution)/shard_map/ppermute | solution.py:255
  22.9 0.1 copy-done.3
  22.9 0.0 copy-done.4
  23.0 0.5 %copy-done.5 = f32[1,2,2,32,128]{4,3,2,1,0:T(8,128)} copy-done((f32[1,2,2,32,128]{4,3,2,1,0:T(8,128)}, f32[1,2,2,32,128]{4,3,2,1,0:T(8,128)S(1)}, u32[]{:S(2)}) %copy-start.5) | copy-done | bytes 65560
  23.5 2.9 %last_gates.1 = f32[512,128]{1,0:T(8,128)} custom-call(f32[2,2,2]{2,1,0:T(2,128)} %gate_ref.3, bf16[3,256,256]{2,1,0:T(8,128)(2,1)} %get-tuple-element.10.high_ref, bf16[3,256,256]{2,1,0:T(8,128)(2,1)} %get-tuple-element.11.low_ref, f32[1,2,2,32,128]{4,3,2,1,0:T(8,128)} %get-tuple-element.16.refs_0_, f32[1,2,2,32,128]{4,3,2,1,0:T(8,128)} %copy-done.5, ...), custom_call_target="tpu_custom_call" | custom-call | tf_op jit(solution)/shard_map/last_gates/pallas_call | solution.py:309
  (5 shorter events, 0.0 us)
Async XLA Ops:
  3.3 11.4 %collective-permute-start = (f32[2,2,2,32,128]{4,3,2,1,0:T(8,128)}, f32[2,2,2,32,128]{4,3,2,1,0:T(8,128)S(1)}, u32[]{:S(2)}, u32[]{:S(2)}) collective-permute-start(f32[2,2,2,32,128]{4,3,2,1,0:T(8,128)} %get-tuple-element.12.own_ref), channel_id=1, source_target_pairs={{0,16},{4,20},{8,24},{12,28},{16,0},{20,4},{24,8},{28,12},{1,17},{... | collective-permute-start | bytes 393224 | tf_op jit(solution)/shard_map/ppermute | solution.py:255
  7.4 4.5 %collective-permute-start.2 = (f32[1,2,2,32,128]{4,3,2,1,0:T(8,128)}, f32[1,2,2,32,128]{4,3,2,1,0:T(8,128)S(1)}, u32[]{:S(2)}, u32[]{:S(2)}) collective-permute-start(f32[1,2,2,32,128]{4,3,2,1,0:T(8,128)} %get-tuple-element.13), channel_id=1, source_target_pairs={{0,2},{1,3},{2,0},{3,1},{4,6},{5,7},{6,4},{7,5},{8,10},{9,11},{10,... | collective-permute-start | bytes 196616 | tf_op jit(solution)/shard_map/ppermute | solution.py:255
  8.9 5.4 %collective-permute-start.4 = (f32[1,2,2,32,128]{4,3,2,1,0:T(8,128)}, f32[1,2,2,32,128]{4,3,2,1,0:T(8,128)S(1)}, u32[]{:S(2)}, u32[]{:S(2)}) collective-permute-start(f32[1,2,2,32,128]{4,3,2,1,0:T(8,128)} %get-tuple-element.14), channel_id=1, source_target_pairs={{0,3},{1,2},{2,1},{3,0},{4,7},{5,6},{6,5},{7,4},{8,11},{9,10},{10,... | collective-permute-start | bytes 196616 | tf_op jit(solution)/shard_map/ppermute | solution.py:255
  11.8 5.3 %copy-start.1 = (f32[1,2,2,32,128]{4,3,2,1,0:T(8,128)}, f32[1,2,2,32,128]{4,3,2,1,0:T(8,128)S(1)}, u32[]{:S(2)}) copy-start(f32[1,2,2,32,128]{4,3,2,1,0:T(8,128)S(1)} %collective-permute-done.2.refs_2_) | copy-start | bytes 196612
  11.8 10.5 %collective-permute-start.3 = (f32[1,2,2,32,128]{4,3,2,1,0:T(8,128)S(1)}, f32[1,2,2,32,128]{4,3,2,1,0:T(8,128)S(1)}, u32[]{:S(2)}, u32[]{:S(2)}) collective-permute-start(f32[1,2,2,32,128]{4,3,2,1,0:T(8,128)S(1)} %collective-permute-done.2.refs_2_), channel_id=1, source_target_pairs={{0,16},{4,20},{8,24},{12,28},{16,0},{20,4},{24,8},{28,12},{1,17},{... | collective-permute-start | bytes 196616 | tf_op jit(solution)/shard_map/ppermute | solution.py:255
  14.3 2.8 %copy-start.2 = (f32[1,2,2,32,128]{4,3,2,1,0:T(8,128)}, f32[1,2,2,32,128]{4,3,2,1,0:T(8,128)S(1)}, u32[]{:S(2)}) copy-start(f32[1,2,2,32,128]{4,3,2,1,0:T(8,128)S(1)} %collective-permute-done.4.refs_4_) | copy-start | bytes 196612
  14.3 8.1 %collective-permute-start.5 = (f32[1,2,2,32,128]{4,3,2,1,0:T(8,128)S(1)}, f32[1,2,2,32,128]{4,3,2,1,0:T(8,128)S(1)}, u32[]{:S(2)}, u32[]{:S(2)}) collective-permute-start(f32[1,2,2,32,128]{4,3,2,1,0:T(8,128)S(1)} %collective-permute-done.4.refs_4_), channel_id=1, source_target_pairs={{0,16},{4,20},{8,24},{12,28},{16,0},{20,4},{24,8},{28,12},{1,17},{... | collective-permute-start | bytes 196616 | tf_op jit(solution)/shard_map/ppermute | solution.py:255
  14.8 0.7 %copy-start = (f32[2,2,2,32,128]{4,3,2,1,0:T(8,128)}, f32[2,2,2,32,128]{4,3,2,1,0:T(8,128)S(1)}, u32[]{:S(2)}) copy-start(f32[2,2,2,32,128]{4,3,2,1,0:T(8,128)S(1)} %collective-permute-done.other_ref) | copy-start | bytes 393220
  18.6 4.3 %collective-permute-start.1 = (f32[1,2,2,32,128]{4,3,2,1,0:T(8,128)S(1)}, f32[1,2,2,32,128]{4,3,2,1,0:T(8,128)S(1)}, u32[]{:S(2)}, u32[]{:S(2)}) collective-permute-start(f32[1,2,2,32,128]{4,3,2,1,0:T(8,128)S(1)} %get-tuple-element.15), channel_id=1, source_target_pairs={{0,1},{1,0},{2,3},{3,2},{4,5},{5,4},{6,7},{7,6},{8,9},{9,8},{10,11... | collective-permute-start | bytes 196616 | tf_op jit(solution)/shard_map/ppermute | solution.py:255
  22.3 0.6 %copy-start.3 = (f32[1,2,2,32,128]{4,3,2,1,0:T(8,128)}, f32[1,2,2,32,128]{4,3,2,1,0:T(8,128)S(1)}, u32[]{:S(2)}) copy-start(f32[1,2,2,32,128]{4,3,2,1,0:T(8,128)S(1)} %collective-permute-done.3.refs_3_) | copy-start | bytes 196612
  22.3 0.6 %copy-start.4 = (f32[1,2,2,32,128]{4,3,2,1,0:T(8,128)}, f32[1,2,2,32,128]{4,3,2,1,0:T(8,128)S(1)}, u32[]{:S(2)}) copy-start(f32[1,2,2,32,128]{4,3,2,1,0:T(8,128)S(1)} %collective-permute-done.5.refs_5_) | copy-start | bytes 196612
  22.9 0.6 %copy-start.5 = (f32[1,2,2,32,128]{4,3,2,1,0:T(8,128)}, f32[1,2,2,32,128]{4,3,2,1,0:T(8,128)S(1)}, u32[]{:S(2)}) copy-start(f32[1,2,2,32,128]{4,3,2,1,0:T(8,128)S(1)} %collective-permute-done.1.refs_1_) | copy-start | bytes 196612

commit v2 on v1

v2 whole, which is shorter than its diff:
```python
import functools

import jax
import jax.numpy as jnp
from jax import lax
from jax.experimental import pallas as pl
from jax.experimental.pallas import tpu as pltpu
from jax.sharding import PartitionSpec as P

WIDTH = 128
LANE_BITS = 7
ROW_BITS = 8
F32, BF16 = jnp.float32, jnp.bfloat16


def halves(value):
    high = value.astype(BF16)
    return high, (value - high.astype(F32)).astype(BF16)


def dot(left, right, transposed=False):
    return lax.dot_general(
        left, right, (((1,), (1 if transposed else 0,)), ((), ())), preferred_element_type=F32
    )


def dot3(left, right, transposed=False):
    (lh, ll), (rh, rl) = left, right
    return dot(lh, rl, transposed) + dot(ll, rh, transposed) + dot(lh, rh, transposed)


def block_matrix(real, imag):
    return jnp.concatenate(
        [jnp.concatenate([real, -imag], axis=1), jnp.concatenate([imag, real], axis=1)], axis=0
    )


def new_positions(lo_bits):
    kept = LANE_BITS - lo_bits
    return [8 + r for r in range(kept)] + [7] + [8 + r for r in range(kept, LANE_BITS)]


def plan_of(order, lo_bits):
    one, zero = jnp.int32(1), jnp.int32(0)
    middle = LANE_BITS - lo_bits
    row_of_lane = [l if l < middle else l + 1 for l in range(LANE_BITS)]
    wanted = [order[k] for k in new_positions(lo_bits)]
    crosses = [jnp.where(w < LANE_BITS, one, zero) for w in wanted]
    crosses_middle = crosses[middle]
    used, before = [], zero
    spare = zero
    for l in range(LANE_BITS):
        free = (one - crosses[row_of_lane[l]]) * crosses_middle * jnp.where(before == 0, one, zero)
        spare = spare + free * l
        used.append(crosses[row_of_lane[l]] + free)
        before = before + free
    key_lane, moved, stayed = [], zero, zero
    for l in range(LANE_BITS):
        key_lane.append(jnp.where(used[l] == 1, moved + 16, stayed))
        moved, stayed = moved + used[l], stayed + (one - used[l])
    key_new, moved, stayed = [], zero, zero
    for k in range(LANE_BITS):
        from_row = jnp.where(order[k] >= LANE_BITS, one, zero)
        key_new.append(jnp.where(from_row == 1, moved + 16, stayed))
        moved, stayed = moved + from_row, stayed + (one - from_row)
    match = []
    for l in range(LANE_BITS):
        total = zero
        for k in range(LANE_BITS):
            total = total + jnp.where(key_lane[l] == key_new[k], order[k] + 16 * k, zero)
        match.append(total)
    new_in_lane = [m >> 4 for m in match]
    lane_before, row_before = [], [None] * ROW_BITS
    middle_before = zero
    for l in range(LANE_BITS):
        r = row_of_lane[l]
        old = match[l] & 15
        at_spare = crosses_middle * jnp.where(spare == l, one, zero)
        lane_before.append(jnp.where(crosses[r] == 1, wanted[r], jnp.where(at_spare == 1, wanted[middle], old)))
        row_before[r] = jnp.where(crosses[r] == 1, old, wanted[r]) & 7
        middle_before = middle_before + at_spare * old
    row_before[middle] = jnp.where(crosses_middle == 1, middle_before, wanted[middle]) & 7
    return crosses, spare, row_before, lane_before, new_in_lane


def moved_bits(index, sources, targets):
    total = jnp.zeros_like(index)
    for source, target in zip(sources, targets, strict=True):
        total = total | (((index >> source) & 1) << target)
    return total


def one_hot(count, index):
    rows = lax.broadcasted_iota(jnp.int32, (count, index.shape[1]), 0)
    return jnp.where(rows == index, 1.0, 0.0).astype(F32).astype(BF16)


def bit_exchange(low, high, lane, crosses, lane_bit, shift):
    up = ((lane >> lane_bit) & 1) * crosses
    down = (1 - ((lane >> lane_bit) & 1)) * crosses
    return (
        jnp.where(up == 1, pltpu.roll(high, shift, 1), low),
        jnp.where(down == 1, pltpu.roll(low, WIDTH - shift, 1), high),
    )


def first_kernel(lo_bits, order_hbm, gate_hbm, x_hbm, gates_hbm, *refs):
    outs, (order_ref, gate_ref, x_ref, gates_ref, work, blocks, sems) = refs[:-7], refs[-7:]
    outs, (coefs_out, lanes_out) = outs[:-2], outs[-2:]
    parts = 1 << lo_bits
    fetches = [
        pltpu.make_async_copy(order_hbm, order_ref, sems.at[0]),
        pltpu.make_async_copy(gates_hbm.at[pl.ds(0, 2)], gates_ref, sems.at[1]),
        pltpu.make_async_copy(x_hbm, x_ref, sems.at[2]),
        pltpu.make_async_copy(gate_hbm, gate_ref, sems.at[3]),
    ]
    for fetch in fetches:
        fetch.start()
    fetches[0].wait()
    order = [order_ref[k] for k in range(LANE_BITS + ROW_BITS)]
    crosses, spare, row_before, lane_before, new_in_lane = plan_of(order, lo_bits)
    middle = LANE_BITS - lo_bits
    index = lax.broadcasted_iota(jnp.int32, (1, 2 * WIDTH), 1)
    rows = one_hot(2 * WIDTH, moved_bits(index, row_before, range(ROW_BITS)))
    index = lax.broadcasted_iota(jnp.int32, (1, WIDTH), 1)
    lanes = one_hot(WIDTH, moved_bits(index, lane_before, range(LANE_BITS)))
    lanes_out[...] = jnp.broadcast_to(moved_bits(index, range(LANE_BITS), new_in_lane), lanes_out.shape)
    fetches[1].wait()
    real, imag = halves(gates_ref[0, 0]), halves(gates_ref[0, 1])
    matrix0 = [block_matrix(real[i], imag[i]) for i in range(2)]
    real, imag = halves(gates_ref[1, 0]), halves(gates_ref[1, 1])
    matrix1 = [
        block_matrix(dot(lanes, real[i]).astype(BF16), dot(lanes, imag[i]).astype(BF16)) for i in range(2)
    ]
    fetches[2].wait()
    pieces = [[x_ref[pl.ds(m * 2 + c, WIDTH, stride=4), :] for m in range(2)] for c in range(2)]
    state = jnp.concatenate([jnp.concatenate(row, axis=1) for row in pieces], axis=0)
    state = dot3(matrix0, halves(state))
    state = [dot(rows, half).astype(BF16) for half in halves(turned(state))]
    state = dot3(state, matrix1, transposed=True)
    for c in range(2):
        work[c] = state[:, c * WIDTH : (c + 1) * WIDTH]
    lane = lax.broadcasted_iota(jnp.int32, (8, WIDTH), 1)

    def exchange(values, row_bit, bit):
        if row_bit == middle:
            lane_bit, shift = spare, jnp.left_shift(jnp.int32(1), spare)
        else:
            lane_bit = row_bit if row_bit < middle else row_bit - 1
            shift = 1 << lane_bit
        for i in range(len(values)):
            if not i >> bit & 1:
                j = i | 1 << bit
                values[i], values[j] = bit_exchange(values[i], values[j], lane, crosses[row_bit], lane_bit, shift)

    for c in range(2):
        for group in range(4):
            places = [pl.ds(group * 64 + o, 8, stride=8) for o in range(8)]
            values = [work[c, place, :] for place in places]
            for row_bit in range(3):
                exchange(values, row_bit, row_bit)
            for place, value in zip(places, values, strict=True):
                work[c, place, :] = value
    me = lax.axis_index("lo")
    kept = WIDTH // parts
    for c in range(2):
        values = [work[c, pl.ds(8 * v, 8), :] for v in range(32)]
        for row_bit in range(3, ROW_BITS):
            exchange(values, row_bit, row_bit - 3)
        each = 32 // parts
        for part in range(parts):
            step = jnp.bitwise_xor(me, part)
            for v in range(each):
                m, h = divmod(8 * v, kept)
                blocks[step, c, m, pl.ds(h, 8), :] = values[part * each + v]
    near = outs[0].shape[0]
    outs[0][...] = blocks[:near]
    for step, out in enumerate(outs[1:]):
        out[...] = blocks[near + step]
    fetches[3].wait()
    side = jnp.right_shift(lax.axis_index("hi"), lax.axis_size("hi").bit_length() - 2) & 1
    for other in range(2):
        for c in range(2):
            coefs_out[2 * other + c] = jnp.full((8, WIDTH), gate_ref[c, side, side ^ other])


def turned(value):
    return jnp.concatenate(
        [
            jnp.concatenate([value[i * WIDTH : (i + 1) * WIDTH, j * WIDTH : (j + 1) * WIDTH] for i in range(2)], axis=1)
            for j in range(2)
        ],
        axis=0,
    )


def mixed(coefs_ref, own, other, m):
    rows = own.shape[-2]
    own_r, own_i, other_r, other_i = [jnp.concatenate([coefs_ref[i]] * (rows // 8), axis=0) for i in range(4)]
    return (
        own_r * own[0, m] - own_i * own[1, m] + (other_r * other[0, m] - other_i * other[1, m]),
        own_r * own[1, m] + own_i * own[0, m] + (other_r * other[1, m] + other_i * other[0, m]),
    )


def mix_kernel(coefs_ref, own_ref, other_ref, *outs):
    for k, out_ref in enumerate(outs):
        for m in range(2):
            out_ref[0, m], out_ref[1, m] = mixed(coefs_ref, own_ref.at[k + 1], other_ref.at[k + 1], m)


def weights_kernel(lanes_ref, gates_hbm, high_ref, low_ref, gates_ref, sems):
    fetches = [pltpu.make_async_copy(gates_hbm.at[2 + g], gates_ref.at[g], sems.at[g]) for g in range(3)]
    for fetch in fetches:
        fetch.start()
    lanes = one_hot(WIDTH, lanes_ref[0:1])
    for g, fetch in enumerate(fetches):
        fetch.wait()
        real, imag = halves(gates_ref[g, 0]), halves(gates_ref[g, 1])
        for i, out in enumerate((high_ref, low_ref)):
            parts = real[i], imag[i]
            if g == 1:
                parts = [dot(part, lanes).astype(BF16) for part in parts]
            out[g] = block_matrix(*parts)


def last_kernel(pairs, coefs_ref, high_ref, low_ref, *refs):
    ins, (out_hbm, state_ref, out_ref, sems) = refs[:-4], refs[-4:]
    ins = (ins[0].at[0], ins[1].at[0]) + ins[2:]
    me = lax.axis_index("lo")
    for step, pair in enumerate(pairs):
        own, ins = ins[0], ins[1:]
        kept = own.shape[-2]
        source = pl.multiple_of(jnp.bitwise_xor(me, step) * kept, 8)
        if pair:
            other, ins = ins[0], ins[1:]
        for m in range(2):
            values = mixed(coefs_ref, own, other, m) if pair else (own[0, m], own[1, m])
            for c in range(2):
                state_ref[c, m, pl.ds(source, kept), :] = values[c]
    state = jnp.concatenate(
        [jnp.concatenate([state_ref[c, m] for m in range(2)], axis=1) for c in range(2)], axis=0
    )
    state = dot3((high_ref[0], low_ref[0]), halves(state))
    state = dot3(halves(turned(state)), (high_ref[1], low_ref[1]), transposed=True)
    state = halves(turned(state))
    sends = []
    half = WIDTH // 2
    for i in range(2):
        matrix = [
            jnp.concatenate([ref[2, c * WIDTH + i * half : c * WIDTH + (i + 1) * half] for c in range(2)], axis=0)
            for ref in (high_ref, low_ref)
        ]
        result = dot3(matrix, state)
        for c in range(2):
            for m in range(2):
                out_ref[pl.ds(i * 256 + m * 2 + c, half, stride=4), :] = result[
                    c * half : (c + 1) * half, m * WIDTH : (m + 1) * WIDTH
                ]
        sends.append(
            pltpu.make_async_copy(out_ref.at[pl.ds(i * 256, 256)], out_hbm.at[pl.ds(i * 256, 256)], sems.at[i])
        )
        sends[-1].start()
    for send in sends:
        send.wait()


def swapped(block, axis, distance):
    count = lax.axis_size(axis)
    return lax.ppermute(block, axis, [(i, i ^ distance) for i in range(count)])


PARAMS = pltpu.CompilerParams(vmem_limit_bytes=8 << 20)
HBM = pl.BlockSpec(memory_space=pltpu.HBM)
VMEM = pl.BlockSpec(memory_space=pltpu.VMEM)


def in_hbm(value):
    return pltpu.with_memory_space_constraint(value, pltpu.HBM)


def on_device(amplitudes, gate_mats, dev_gate, qubit_order):
    parts = lax.axis_size("lo")
    lo_bits = parts.bit_length() - 1
    top = lax.axis_size("hi") // 2
    kept = WIDTH // parts
    rows = amplitudes.reshape(2, 256, WIDTH).transpose(1, 0, 2).reshape(512, WIDTH)
    block = pltpu.VMEM((2, 2, kept, WIDTH), F32)
    near = parts // 2
    near_own, *far_own, coefs, lanes = pl.pallas_call(
        functools.partial(first_kernel, lo_bits),
        out_shape=[pltpu.VMEM((near, 2, 2, kept, WIDTH), F32)]
        + [block] * (parts - near)
        + [pltpu.VMEM((4, 8, WIDTH), F32), pltpu.VMEM((8, WIDTH), jnp.int32)],
        in_specs=[HBM] * 4,
        out_specs=[VMEM] * (parts - near + 3),
        scratch_shapes=[
            pltpu.SMEM((LANE_BITS + ROW_BITS,), jnp.int32),
            pltpu.SMEM((2, 2, 2), F32),
            pltpu.VMEM((512, WIDTH), F32),
            pltpu.VMEM((2, 2, WIDTH, WIDTH), F32),
            pltpu.VMEM((2, 256, WIDTH), F32),
            pltpu.VMEM((parts, 2, 2, kept, WIDTH), F32),
            pltpu.SemaphoreType.DMA((4,)),
        ],
        compiler_params=PARAMS,
        name="first_gates",
    )(in_hbm(qubit_order), in_hbm(dev_gate), in_hbm(rows), in_hbm(gate_mats))
    near_other = swapped(near_own, "hi", top)
    far_own = [swapped(far, "lo", near + i) for i, far in enumerate(far_own)]
    far_other = [swapped(far, "hi", top) for far in far_own]
    weights = pltpu.VMEM((3, 256, 256), BF16)
    high, low = pl.pallas_call(
        weights_kernel,
        out_shape=[weights] * 2,
        in_specs=[VMEM, HBM],
        out_specs=[VMEM] * 2,
        scratch_shapes=[pltpu.VMEM((3, 2, WIDTH, WIDTH), F32), pltpu.SemaphoreType.DMA((3,))],
        compiler_params=PARAMS,
        name="gate_weights",
    )(lanes, in_hbm(gate_mats))
    mixes = pl.pallas_call(
        mix_kernel,
        out_shape=[block] * (near - 1),
        in_specs=[VMEM] * 3,
        out_specs=[VMEM] * (near - 1),
        compiler_params=PARAMS,
        name="mix_pair",
    )(coefs, near_own, near_other)
    operands = [near_own, near_other] + [swapped(mix, "lo", 1 + i) for i, mix in enumerate(mixes)]
    pairs = [True] + [False] * (near - 1) + [True] * (parts - near)
    for pair in zip(far_own, far_other, strict=True):
        operands += pair
    out = pl.pallas_call(
        functools.partial(last_kernel, tuple(pairs)),
        out_shape=jax.ShapeDtypeStruct((512, WIDTH), F32),
        in_specs=[VMEM] * (3 + len(operands)),
        out_specs=HBM,
        scratch_shapes=[
            pltpu.VMEM((2, 2, WIDTH, WIDTH), F32),
            pltpu.VMEM((512, WIDTH), F32),
            pltpu.SemaphoreType.DMA((2,)),
        ],
        compiler_params=PARAMS,
        name="last_gates",
    )(coefs, high, low, *operands)
    return out.reshape(256, 2, WIDTH).transpose(1, 0, 2).reshape(2, -1)


def solution(mesh):
    return jax.shard_map(
        on_device,
        mesh=mesh,
        in_specs=(P(None, ("hi", "lo")), P(), P(), P()),
        out_specs=P(None, ("hi", "lo")),
        check_vma=False,
    )
```

time: 26.6 us -> 20.7 us (0.78)
  Pallas kernels: 10.1 us -> 5.56 us
  local copies, waits for them, and re-layouts: 2.79 us -> 0 us
  waiting for transfers between devices: 4.48 us -> 5.78 us
    pallas_call x4, Pallas kernels: 10.1 us -> 5.56 us  [the longest x1 2.68 us: on_device(): pl.pallas_call(functools.partial(first_kernel, lo_bits), out_shape=[pltpu...]
    slice x1 -> x0, local copies, waits for them, and re-layouts: 1.5 us -> none  [on_device(): near_mixed[k:k + 1]]
    ppermute x6, waiting for transfers between devices: 4.48 us -> 5.78 us  [swapped(): return lax.ppermute(block, axis, [(i, i ^ distance) for i in range(count)])]
    unnamed x12 -> x0, local copies, waits for them, and re-layouts: 1.29 us -> none
  transfers between devices with their start and end apart: 6 -> 6, of which waited for: 3 -> 4; matrix products, arithmetic and copies ran while one was open for 6% -> 0% of each run, Pallas kernels for 15% -> 6%
where the time goes in v2:
time: 20.7 us; the launch traced here: 20.6 us
  starting transfers between devices  9.2 us (44%)
  waiting for transfers between devices  5.78 us (28%)
  Pallas kernels  5.56 us (27%)
    ppermute x6, starting transfers between devices, swapped(): return lax.ppermute(block, axis, [(i, i ^ distance) for i in range(count)])  9.2 us
    ppermute x6, waiting for transfers between devices, swapped(): return lax.ppermute(block, axis, [(i, i ^ distance) for i in range(count)])  5.78 us
    pallas_call x1, Pallas kernels, on_device(): pl.pallas_call(functools.partial(first_kernel, lo_bits), out_shape=[pltpu...  2.68 us
    pallas_call x1, Pallas kernels, on_device(): pl.pallas_call(functools.partial(last_kernel, tuple(pairs)), out_shape=ja...  1.67 us
    pallas_call x1, Pallas kernels, on_device(): pl.pallas_call(weights_kernel, out_shape=[weights] * 2, in_specs=[VMEM, H...  1.19 us
  transfers between devices with their start and end apart: 6, of which 4 were waited for; matrix products, arithmetic and copies ran while one was open for 0% of the time, Pallas kernels for 6%

profile of v2, /device:TPU:0, one launch (start us, length us, event | category | flops | bytes accessed | tf_op | source)
XLA Modules:
  0.0 20.6 jit_solution(4788567218749240988)
XLA Ops:
  0.0 2.7 %first_gates.1 = (f32[2,2,2,32,128]{4,3,2,1,0:T(8,128)S(1)}, f32[2,2,32,128]{3,2,1,0:T(8,128)S(1)}, f32[2,2,32,128]{3,2,1,0:T(8,128)S(1)}, f32[4,8,128]{2,1,0:T(8,128)S(1)}, s32[8,128]{1,0:T(8,128)S(1)}) custom-call(s32[15]{0:T(128)} %order_hbm.1, f32[2,2,2]{2,1,0:T(2,128)} %gate_hbm.1, f32[512,128]{1,0:T(8,128)} %bitcast.10, f32[5,2,128,128]{3,2,1,0:T(8,128)} %gates_hbm.3), custom_call_target="tpu_custom_call" | custom-call | tf_op jit(solution)/shard_map/first_gates/pallas_call | solution.py:290
  2.7 4.1 %collective-permute-start = (f32[2,2,2,32,128]{4,3,2,1,0:T(8,128)S(1)}, f32[2,2,2,32,128]{4,3,2,1,0:T(8,128)S(1)}, u32[]{:S(2)}, u32[]{:S(2)}) collective-permute-start(f32[2,2,2,32,128]{4,3,2,1,0:T(8,128)S(1)} %get-tuple-element.16.own_ref.refs_0_), channel_id=1, source_target_pairs={{0,16},{4,20},{8,24},{12,28},{16,0},{20,4},{24,8},{28,12},{1,17},{... | collective-permute-start | bytes 393224 | tf_op jit(solution)/shard_map/ppermute | solution.py:270
  6.8 1.5 %collective-permute-start.2 = (f32[2,2,32,128]{3,2,1,0:T(8,128)S(1)}, f32[2,2,32,128]{3,2,1,0:T(8,128)S(1)}, u32[]{:S(2)}, u32[]{:S(2)}) collective-permute-start(f32[2,2,32,128]{3,2,1,0:T(8,128)S(1)} %get-tuple-element.17), channel_id=1, source_target_pairs={{0,2},{1,3},{2,0},{3,1},{4,6},{5,7},{6,4},{7,5},{8,10},{9,11},{10,... | collective-permute-start | bytes 196616 | tf_op jit(solution)/shard_map/ppermute | solution.py:270
  8.3 1.4 %collective-permute-start.4 = (f32[2,2,32,128]{3,2,1,0:T(8,128)S(1)}, f32[2,2,32,128]{3,2,1,0:T(8,128)S(1)}, u32[]{:S(2)}, u32[]{:S(2)}) collective-permute-start(f32[2,2,32,128]{3,2,1,0:T(8,128)S(1)} %get-tuple-element.18), channel_id=1, source_target_pairs={{0,3},{1,2},{2,1},{3,0},{4,7},{5,6},{6,5},{7,4},{8,11},{9,10},{10,... | collective-permute-start | bytes 196616 | tf_op jit(solution)/shard_map/ppermute | solution.py:270
  9.7 1.3 %collective-permute-done.2.refs_3_ = f32[2,2,32,128]{3,2,1,0:T(8,128)S(1)} collective-permute-done((f32[2,2,32,128]{3,2,1,0:T(8,128)S(1)}, f32[2,2,32,128]{3,2,1,0:T(8,128)S(1)}, u32[]{:S(2)}, u32[]{:S(2)}) %collective-permute-start.2) | collective-permute-done | bytes 65568 | tf_op jit(solution)/shard_map/ppermute | solution.py:270
  11.1 0.1 collective-permute-start.3
  11.1 2.3 %collective-permute-done.4.refs_5_ = f32[2,2,32,128]{3,2,1,0:T(8,128)S(1)} collective-permute-done((f32[2,2,32,128]{3,2,1,0:T(8,128)S(1)}, f32[2,2,32,128]{3,2,1,0:T(8,128)S(1)}, u32[]{:S(2)}, u32[]{:S(2)}) %collective-permute-start.4) | collective-permute-done | bytes 65568 | tf_op jit(solution)/shard_map/ppermute | solution.py:270
  13.5 0.5 %collective-permute-start.5 = (f32[2,2,32,128]{3,2,1,0:T(8,128)S(1)}, f32[2,2,32,128]{3,2,1,0:T(8,128)S(1)}, u32[]{:S(2)}, u32[]{:S(2)}) collective-permute-start(f32[2,2,32,128]{3,2,1,0:T(8,128)S(1)} %collective-permute-done.4.refs_5_), channel_id=1, source_target_pairs={{0,16},{4,20},{8,24},{12,28},{16,0},{20,4},{24,8},{28,12},{1,17},{... | collective-permute-start | bytes 196616 | tf_op jit(solution)/shard_map/ppermute | solution.py:270
  14.0 0.0 collective-permute-done.other_ref.refs_1_
  14.0 1.6 %collective-permute-start.1 = (f32[2,2,32,128]{3,2,1,0:T(8,128)S(1)}, f32[2,2,32,128]{3,2,1,0:T(8,128)S(1)}, u32[]{:S(2)}, u32[]{:S(2)}) collective-permute-start(f32[2,2,32,128]{3,2,1,0:T(8,128)S(1)} %mix_pair.1), channel_id=1, source_target_pairs={{0,1},{1,0},{2,3},{3,2},{4,5},{5,4},{6,7},{7,6},{8,9},{9,8},{10,11... | collective-permute-start | bytes 196616 | tf_op jit(solution)/shard_map/ppermute | solution.py:270
  15.6 1.2 %gate_weights.1 = (bf16[3,256,256]{2,1,0:T(8,128)(2,1)S(1)}, bf16[3,256,256]{2,1,0:T(8,128)(2,1)S(1)}) custom-call(s32[8,128]{1,0:T(8,128)S(1)} %get-tuple-element.13.lanes_ref, f32[5,2,128,128]{3,2,1,0:T(8,128)} %gates_hbm.3), custom_call_target="tpu_custom_call" | custom-call | tf_op jit(solution)/shard_map/gate_weights/pallas_call | solution.py:313
  16.8 1.4 %collective-permute-done.3.refs_4_ = f32[2,2,32,128]{3,2,1,0:T(8,128)S(1)} collective-permute-done((f32[2,2,32,128]{3,2,1,0:T(8,128)S(1)}, f32[2,2,32,128]{3,2,1,0:T(8,128)S(1)}, u32[]{:S(2)}, u32[]{:S(2)}) %collective-permute-start.3) | collective-permute-done | bytes 65568 | tf_op jit(solution)/shard_map/ppermute | solution.py:270
  18.2 0.7 %collective-permute-done.5.refs_6_ = f32[2,2,32,128]{3,2,1,0:T(8,128)S(1)} collective-permute-done((f32[2,2,32,128]{3,2,1,0:T(8,128)S(1)}, f32[2,2,32,128]{3,2,1,0:T(8,128)S(1)}, u32[]{:S(2)}, u32[]{:S(2)}) %collective-permute-start.5) | collective-permute-done | bytes 65568 | tf_op jit(solution)/shard_map/ppermute | solution.py:270
  18.9 0.0 collective-permute-done.1.refs_2_
  18.9 1.7 %last_gates.1 = f32[512,128]{1,0:T(8,128)} custom-call(f32[4,8,128]{2,1,0:T(8,128)S(1)} %get-tuple-element.12.coefs_ref, bf16[3,256,256]{2,1,0:T(8,128)(2,1)S(1)} %get-tuple-element.14.high_ref, bf16[3,256,256]{2,1,0:T(8,128)(2,1)S(1)} %get-tuple-element.15.low_ref, f32[2,2,2,32,128]{4,3,2,1,0:T(8,128)S(1)} %get-tuple-element.16.own_ref.refs_0_, ...), custom_call_target="tpu_custom_call" | custom-call | tf_op jit(solution)/shard_map/last_gates/pallas_call | solution.py:334
  (1 shorter events, 0.0 us)
Async XLA Ops:
  2.7 11.3 %collective-permute-start = (f32[2,2,2,32,128]{4,3,2,1,0:T(8,128)S(1)}, f32[2,2,2,32,128]{4,3,2,1,0:T(8,128)S(1)}, u32[]{:S(2)}, u32[]{:S(2)}) collective-permute-start(f32[2,2,2,32,128]{4,3,2,1,0:T(8,128)S(1)} %get-tuple-element.16.own_ref.refs_0_), channel_id=1, source_target_pairs={{0,16},{4,20},{8,24},{12,28},{16,0},{20,4},{24,8},{28,12},{1,17},{... | collective-permute-start | bytes 393224 | tf_op jit(solution)/shard_map/ppermute | solution.py:270
  6.8 4.3 %collective-permute-start.2 = (f32[2,2,32,128]{3,2,1,0:T(8,128)S(1)}, f32[2,2,32,128]{3,2,1,0:T(8,128)S(1)}, u32[]{:S(2)}, u32[]{:S(2)}) collective-permute-start(f32[2,2,32,128]{3,2,1,0:T(8,128)S(1)} %get-tuple-element.17), channel_id=1, source_target_pairs={{0,2},{1,3},{2,0},{3,1},{4,6},{5,7},{6,4},{7,5},{8,10},{9,11},{10,... | collective-permute-start | bytes 196616 | tf_op jit(solution)/shard_map/ppermute | solution.py:270
  8.3 5.2 %collective-permute-start.4 = (f32[2,2,32,128]{3,2,1,0:T(8,128)S(1)}, f32[2,2,32,128]{3,2,1,0:T(8,128)S(1)}, u32[]{:S(2)}, u32[]{:S(2)}) collective-permute-start(f32[2,2,32,128]{3,2,1,0:T(8,128)S(1)} %get-tuple-element.18), channel_id=1, source_target_pairs={{0,3},{1,2},{2,1},{3,0},{4,7},{5,6},{6,5},{7,4},{8,11},{9,10},{10,... | collective-permute-start | bytes 196616 | tf_op jit(solution)/shard_map/ppermute | solution.py:270
  11.1 7.1 %collective-permute-start.3 = (f32[2,2,32,128]{3,2,1,0:T(8,128)S(1)}, f32[2,2,32,128]{3,2,1,0:T(8,128)S(1)}, u32[]{:S(2)}, u32[]{:S(2)}) collective-permute-start(f32[2,2,32,128]{3,2,1,0:T(8,128)S(1)} %collective-permute-done.2.refs_3_), channel_id=1, source_target_pairs={{0,16},{4,20},{8,24},{12,28},{16,0},{20,4},{24,8},{28,12},{1,17},{... | collective-permute-start | bytes 196616 | tf_op jit(solution)/shard_map/ppermute | solution.py:270
  13.5 5.4 %collective-permute-start.5 = (f32[2,2,32,128]{3,2,1,0:T(8,128)S(1)}, f32[2,2,32,128]{3,2,1,0:T(8,128)S(1)}, u32[]{:S(2)}, u32[]{:S(2)}) collective-permute-start(f32[2,2,32,128]{3,2,1,0:T(8,128)S(1)} %collective-permute-done.4.refs_5_), channel_id=1, source_target_pairs={{0,16},{4,20},{8,24},{12,28},{16,0},{20,4},{24,8},{28,12},{1,17},{... | collective-permute-start | bytes 196616 | tf_op jit(solution)/shard_map/ppermute | solution.py:270
  14.0 4.9 %collective-permute-start.1 = (f32[2,2,32,128]{3,2,1,0:T(8,128)S(1)}, f32[2,2,32,128]{3,2,1,0:T(8,128)S(1)}, u32[]{:S(2)}, u32[]{:S(2)}) collective-permute-start(f32[2,2,32,128]{3,2,1,0:T(8,128)S(1)} %mix_pair.1), channel_id=1, source_target_pairs={{0,1},{1,0},{2,3},{3,2},{4,5},{5,4},{6,7},{7,6},{8,9},{9,8},{10,11... | collective-permute-start | bytes 196616 | tf_op jit(solution)/shard_map/ppermute | solution.py:270

commit v3 on v2

v3 whole, which is shorter than its diff:
```python
import functools

import jax
import jax.numpy as jnp
from jax import lax
from jax.experimental import pallas as pl
from jax.experimental.pallas import tpu as pltpu
from jax.sharding import PartitionSpec as P

WIDTH = 128
LANE_BITS = 7
ROW_BITS = 8
F32, BF16 = jnp.float32, jnp.bfloat16


def halves(value):
    high = value.astype(BF16)
    return high, (value - high.astype(F32)).astype(BF16)


def dot(left, right, transposed=False):
    return lax.dot_general(
        left, right, (((1,), (1 if transposed else 0,)), ((), ())), preferred_element_type=F32
    )


def dot3(left, right, transposed=False):
    (lh, ll), (rh, rl) = left, right
    return dot(lh, rl, transposed) + dot(ll, rh, transposed) + dot(lh, rh, transposed)


def block_matrix(real, imag):
    return jnp.concatenate(
        [jnp.concatenate([real, -imag], axis=1), jnp.concatenate([imag, real], axis=1)], axis=0
    )


def new_positions(lo_bits):
    kept = LANE_BITS - lo_bits
    return [8 + r for r in range(kept)] + [7] + [8 + r for r in range(kept, LANE_BITS)]


def plan_of(order, lo_bits):
    one, zero = jnp.int32(1), jnp.int32(0)
    middle = LANE_BITS - lo_bits
    row_of_lane = [l if l < middle else l + 1 for l in range(LANE_BITS)]
    wanted = [order[k] for k in new_positions(lo_bits)]
    crosses = [jnp.where(w < LANE_BITS, one, zero) for w in wanted]
    crosses_middle = crosses[middle]
    used, before = [], zero
    spare = zero
    for l in range(LANE_BITS):
        free = (one - crosses[row_of_lane[l]]) * crosses_middle * jnp.where(before == 0, one, zero)
        spare = spare + free * l
        used.append(crosses[row_of_lane[l]] + free)
        before = before + free
    key_lane, moved, stayed = [], zero, zero
    for l in range(LANE_BITS):
        key_lane.append(jnp.where(used[l] == 1, moved + 16, stayed))
        moved, stayed = moved + used[l], stayed + (one - used[l])
    key_new, moved, stayed = [], zero, zero
    for k in range(LANE_BITS):
        from_row = jnp.where(order[k] >= LANE_BITS, one, zero)
        key_new.append(jnp.where(from_row == 1, moved + 16, stayed))
        moved, stayed = moved + from_row, stayed + (one - from_row)
    match = []
    for l in range(LANE_BITS):
        total = zero
        for k in range(LANE_BITS):
            total = total + jnp.where(key_lane[l] == key_new[k], order[k] + 16 * k, zero)
        match.append(total)
    new_in_lane = [m >> 4 for m in match]
    lane_before, row_before = [], [None] * ROW_BITS
    middle_before = zero
    for l in range(LANE_BITS):
        r = row_of_lane[l]
        old = match[l] & 15
        at_spare = crosses_middle * jnp.where(spare == l, one, zero)
        lane_before.append(jnp.where(crosses[r] == 1, wanted[r], jnp.where(at_spare == 1, wanted[middle], old)))
        row_before[r] = jnp.where(crosses[r] == 1, old, wanted[r]) & 7
        middle_before = middle_before + at_spare * old
    row_before[middle] = jnp.where(crosses_middle == 1, middle_before, wanted[middle]) & 7
    slots = [r if r < middle else r - 1 for r in range(ROW_BITS)]
    slots[middle] = spare
    return crosses, wanted, slots, row_before, lane_before, new_in_lane


def moved_bits(index, sources, targets):
    total = jnp.zeros_like(index)
    for source, target in zip(sources, targets, strict=True):
        total = total | (((index >> source) & 1) << target)
    return total


def one_hot(count, index):
    rows = lax.broadcasted_iota(jnp.int32, (count, index.shape[1]), 0)
    return jnp.where(rows == index, 1.0, 0.0).astype(F32).astype(BF16)


def crossed(values, before, after, index):
    values = list(values)

    def butterfly(masks):
        for bit, mask in enumerate(masks):
            for i in range(len(values)):
                if not i >> bit & 1:
                    low, high = values[i], values[i | 1 << bit]
                    values[i] = jnp.where(mask, high, low)
                    values[i | 1 << bit] = jnp.where(mask, low, high)

    butterfly(before)
    for i, lanes in enumerate(index):
        values[i] = jnp.take_along_axis(values[i], lanes, axis=1, mode="promise_in_bounds")
    butterfly(after)
    return values


def masks_of(lane, crosses, bits):
    return [((lane >> bit) & 1) * cross == 1 for cross, bit in zip(crosses, bits, strict=True)]


def lanes_of(lane, crosses, bits):
    moves = [cross << bit for cross, bit in zip(crosses, bits, strict=True)]
    offsets = [jnp.int32(0)]
    for move in moves:
        offsets += [offset | move for offset in offsets]
    return [jnp.bitwise_xor(lane, offset) for offset in offsets]


def first_kernel(lo_bits, order_hbm, gate_hbm, x_hbm, gates_hbm, *refs):
    outs, (order_ref, gate_ref, x_ref, gates_ref, work, sems) = refs[:-6], refs[-6:]
    outs, (coefs_out, lanes_out) = outs[:-2], outs[-2:]
    parts = 1 << lo_bits
    fetches = [
        pltpu.make_async_copy(order_hbm, order_ref, sems.at[0]),
        pltpu.make_async_copy(gates_hbm.at[pl.ds(0, 2)], gates_ref, sems.at[1]),
        pltpu.make_async_copy(x_hbm, x_ref, sems.at[2]),
        pltpu.make_async_copy(gate_hbm, gate_ref, sems.at[3]),
    ]
    for fetch in fetches:
        fetch.start()
    fetches[0].wait()
    order = [order_ref[k] for k in range(LANE_BITS + ROW_BITS)]
    crosses, wanted, slots, row_before, lane_before, new_in_lane = plan_of(order, lo_bits)
    index = lax.broadcasted_iota(jnp.int32, (1, 2 * WIDTH), 1)
    rows = one_hot(2 * WIDTH, moved_bits(index, row_before, range(ROW_BITS)))
    lane = lax.broadcasted_iota(jnp.int32, (8, WIDTH), 1)
    lanes_out[...] = moved_bits(lane, range(LANE_BITS), new_in_lane)
    old_lane = moved_bits(lane, range(LANE_BITS), lane_before)
    fetches[1].wait()
    real, imag = halves(gates_ref[0, 0]), halves(gates_ref[0, 1])
    matrix0 = [block_matrix(real[i], imag[i]) for i in range(2)]
    real, imag = halves(gates_ref[1, 0]), halves(gates_ref[1, 1])
    matrix1 = [block_matrix(real[i], imag[i]) for i in range(2)]
    fetches[2].wait()
    pieces = [[x_ref[pl.ds(m * 2 + c, WIDTH, stride=4), :] for m in range(2)] for c in range(2)]
    state = jnp.concatenate([jnp.concatenate(row, axis=1) for row in pieces], axis=0)
    state = dot3(matrix0, halves(state))
    state = [dot(rows, half).astype(BF16) for half in halves(turned(state))]
    state = dot3(state, matrix1, transposed=True)
    before, after = masks_of(lane, crosses[3:], wanted[3:]), masks_of(lane, crosses[3:], slots[3:])
    index = lanes_of(old_lane, crosses[3:], wanted[3:])
    for c in range(2):
        values = [state[8 * v : 8 * v + 8, c * WIDTH : (c + 1) * WIDTH] for v in range(32)]
        for v, value in enumerate(crossed(values, before, after, index)):
            work[c, pl.ds(8 * v, 8), :] = value
    masks = masks_of(lane, crosses[:3], slots[:3])
    index = lanes_of(lane, crosses[:3], slots[:3])
    for c in range(2):
        for group in range(4):
            places = [pl.ds(group * 64 + o, 8, stride=8) for o in range(8)]
            values = crossed([work[c, place, :] for place in places], masks, masks, index)
            for place, value in zip(places, values, strict=True):
                work[c, place, :] = value
    me = lax.axis_index("lo")
    count = 2 * WIDTH // parts
    near = outs[0].shape[0]
    for step in range(parts):
        out = outs[0].at[step] if step < near else outs[1 + step - near]
        source = pl.multiple_of(jnp.bitwise_xor(me, step) * count, 8)
        for c in range(2):
            out[c] = work[c, pl.ds(source, count), :]
    fetches[3].wait()
    side = jnp.right_shift(lax.axis_index("hi"), lax.axis_size("hi").bit_length() - 2) & 1
    for other in range(2):
        for c in range(2):
            coefs_out[2 * other + c] = jnp.full((8, WIDTH), gate_ref[c, side, side ^ other])


def turned(value):
    return jnp.concatenate(
        [
            jnp.concatenate([value[i * WIDTH : (i + 1) * WIDTH, j * WIDTH : (j + 1) * WIDTH] for i in range(2)], axis=1)
            for j in range(2)
        ],
        axis=0,
    )


def mixed(coefs_ref, own, other):
    own_r, own_i, other_r, other_i = [jnp.concatenate([coefs_ref[i]] * (own.shape[-2] // 8), axis=0) for i in range(4)]
    return (
        own_r * own[0] - own_i * own[1] + (other_r * other[0] - other_i * other[1]),
        own_r * own[1] + own_i * own[0] + (other_r * other[1] + other_i * other[0]),
    )


def mix_kernel(coefs_ref, own_ref, other_ref, *outs):
    for k, out_ref in enumerate(outs):
        out_ref[0], out_ref[1] = mixed(coefs_ref, own_ref.at[k + 1], other_ref.at[k + 1])


def weights_kernel(lo_bits, lanes_ref, gates_hbm, high_ref, low_ref, gates_ref, sems):
    fetches = [pltpu.make_async_copy(gates_hbm.at[2 + g], gates_ref.at[g], sems.at[g]) for g in range(3)]
    for fetch in fetches:
        fetch.start()
    lanes = one_hot(WIDTH, lanes_ref[0:1])
    me = lax.axis_index("lo")
    rows = one_hot(WIDTH, jnp.bitwise_xor(lax.broadcasted_iota(jnp.int32, (1, WIDTH), 1), me * (WIDTH >> lo_bits)))
    for fetch in fetches:
        fetch.wait()
    first = [[dot(part, rows).astype(BF16) for part in halves(gates_ref[0, c])] for c in range(2)]
    last = [halves(gates_ref[2, c]) for c in range(2)]
    real = halves(dot3(last[0], first[0]) - dot3(last[1], first[1]))
    imag = halves(dot3(last[0], first[1]) + dot3(last[1], first[0]))
    for i, out in enumerate((high_ref, low_ref)):
        out[0] = block_matrix(*[dot(halves(gates_ref[1, c])[i], lanes).astype(BF16) for c in range(2)])
        out[1] = block_matrix(real[i], imag[i])


def low_gate(high_ref, low_ref, values):
    state = jnp.concatenate([jnp.concatenate(value, axis=1) for value in values], axis=0)
    return dot3(halves(state), (high_ref[0], low_ref[0]), transposed=True)


def early_kernel(coefs_ref, high_ref, low_ref, near_own_ref, near_other_ref, *refs):
    ins, out_ref = refs[:-1], refs[-1]
    values = [mixed(coefs_ref, near_own_ref.at[0], near_other_ref.at[0])]
    values += [mixed(coefs_ref, own, other) for own, other in zip(ins[0::2], ins[1::2], strict=True)]
    state = low_gate(high_ref, low_ref, values)
    out_ref[...] = state


def last_kernel(near, coefs_ref, high_ref, low_ref, early_ref, own_ref, other_ref, *refs):
    ins, (out_hbm, out_ref, sems) = refs[:-3], refs[-3:]
    values = [(ref[0], ref[1]) for ref in ins] + [mixed(coefs_ref, own_ref, other_ref)]
    state = low_gate(high_ref, low_ref, values)
    count = values[0][0].shape[0]
    kept = count // 2
    blocks = [early_ref[i * count : (i + 1) * count] for i in range(early_ref.shape[0] // count)]
    late = [state[i * count : (i + 1) * count] for i in range(len(values))]
    blocks = blocks[:1] + late[:-1] + blocks[1:] + late[-1:]
    state = jnp.concatenate(
        [
            jnp.concatenate(
                [
                    jnp.concatenate([block[m * kept : (m + 1) * kept, c * WIDTH : (c + 1) * WIDTH] for block in blocks], axis=0)
                    for m in range(2)
                ],
                axis=1,
            )
            for c in range(2)
        ],
        axis=0,
    )
    state = halves(state)
    sends = []
    half = WIDTH // 2
    for i in range(2):
        matrix = [
            jnp.concatenate([ref[1, c * WIDTH + i * half : c * WIDTH + (i + 1) * half] for c in range(2)], axis=0)
            for ref in (high_ref, low_ref)
        ]
        result = dot3(matrix, state)
        for c in range(2):
            for m in range(2):
                out_ref[pl.ds(i * 256 + m * 2 + c, half, stride=4), :] = result[
                    c * half : (c + 1) * half, m * WIDTH : (m + 1) * WIDTH
                ]
        sends.append(
            pltpu.make_async_copy(out_ref.at[pl.ds(i * 256, 256)], out_hbm.at[pl.ds(i * 256, 256)], sems.at[i])
        )
        sends[-1].start()
    for send in sends:
        send.wait()


def swapped(block, axis, distance):
    count = lax.axis_size(axis)
    return lax.ppermute(block, axis, [(i, i ^ distance) for i in range(count)])


PARAMS = pltpu.CompilerParams(vmem_limit_bytes=8 << 20)
HBM = pl.BlockSpec(memory_space=pltpu.HBM)
VMEM = pl.BlockSpec(memory_space=pltpu.VMEM)


def in_hbm(value):
    return pltpu.with_memory_space_constraint(value, pltpu.HBM)


def on_device(amplitudes, gate_mats, dev_gate, qubit_order):
    parts = lax.axis_size("lo")
    lo_bits = parts.bit_length() - 1
    top = lax.axis_size("hi") // 2
    kept = WIDTH // parts
    rows = amplitudes.reshape(2, 256, WIDTH).transpose(1, 0, 2).reshape(512, WIDTH)
    block = pltpu.VMEM((2, 2 * kept, WIDTH), F32)
    near = parts // 2
    near_own, *far_own, coefs, lanes = pl.pallas_call(
        functools.partial(first_kernel, lo_bits),
        out_shape=[pltpu.VMEM((near, 2, 2 * kept, WIDTH), F32)]
        + [block] * (parts - near)
        + [pltpu.VMEM((4, 8, WIDTH), F32), pltpu.VMEM((8, WIDTH), jnp.int32)],
        in_specs=[HBM] * 4,
        out_specs=[VMEM] * (parts - near + 3),
        scratch_shapes=[
            pltpu.SMEM((LANE_BITS + ROW_BITS,), jnp.int32),
            pltpu.SMEM((2, 2, 2), F32),
            pltpu.VMEM((512, WIDTH), F32),
            pltpu.VMEM((2, 2, WIDTH, WIDTH), F32),
            pltpu.VMEM((2, 256, WIDTH), F32),
            pltpu.SemaphoreType.DMA((4,)),
        ],
        compiler_params=PARAMS,
        name="first_gates",
    )(in_hbm(qubit_order), in_hbm(dev_gate), in_hbm(rows), in_hbm(gate_mats))
    near_other = swapped(near_own, "hi", top)
    far_own = [swapped(far, "lo", near + i) for i, far in enumerate(far_own)]
    far_other = [swapped(far, "hi", top) for far in far_own]
    weights = pltpu.VMEM((2, 256, 256), BF16)
    high, low = pl.pallas_call(
        functools.partial(weights_kernel, lo_bits),
        out_shape=[weights] * 2,
        in_specs=[VMEM, HBM],
        out_specs=[VMEM] * 2,
        scratch_shapes=[pltpu.VMEM((3, 2, WIDTH, WIDTH), F32), pltpu.SemaphoreType.DMA((3,))],
        compiler_params=PARAMS,
        name="gate_weights",
    )(lanes, in_hbm(gate_mats))
    mixes = pl.pallas_call(
        mix_kernel,
        out_shape=[block] * (near - 1),
        in_specs=[VMEM] * 3,
        out_specs=[VMEM] * (near - 1),
        compiler_params=PARAMS,
        name="mix_pair",
    )(coefs, near_own, near_other)
    mixes = [swapped(mix, "lo", 1 + i) for i, mix in enumerate(mixes)]
    pairs = [value for pair in zip(far_own[:-1], far_other[:-1], strict=True) for value in pair]
    early = pl.pallas_call(
        early_kernel,
        out_shape=pltpu.VMEM(((parts - near) * 2 * kept, 2 * WIDTH), F32),
        in_specs=[VMEM] * (5 + len(pairs)),
        out_specs=VMEM,
        compiler_params=PARAMS,
        name="early_gate",
    )(coefs, high, low, near_own, near_other, *pairs)
    out = pl.pallas_call(
        functools.partial(last_kernel, near),
        out_shape=jax.ShapeDtypeStruct((512, WIDTH), F32),
        in_specs=[VMEM] * (6 + len(mixes)),
        out_specs=HBM,
        scratch_shapes=[pltpu.VMEM((512, WIDTH), F32), pltpu.SemaphoreType.DMA((2,))],
        compiler_params=PARAMS,
        name="last_gates",
    )(coefs, high, low, early, far_own[-1], far_other[-1], *mixes)
    return out.reshape(256, 2, WIDTH).transpose(1, 0, 2).reshape(2, -1)


def solution(mesh):
    return jax.shard_map(
        on_device,
        mesh=mesh,
        in_specs=(P(None, ("hi", "lo")), P(), P(), P()),
        out_specs=P(None, ("hi", "lo")),
        check_vma=False,
    )
```

time: 20.7 us -> 20.1 us (0.971)
  waiting for transfers between devices: 5.78 us -> 5.2 us
    ppermute x6, waiting for transfers between devices: 5.78 us -> 5.2 us  [swapped(): return lax.ppermute(block, axis, [(i, i ^ distance) for i in range(count)])]
    pallas_call x1, Pallas kernels: 2.68 us -> 2.36 us  [on_device(): pl.pallas_call(functools.partial(first_kernel, lo_bits), out_shape=[pltpu...]
    pallas_call x2 -> x3, Pallas kernels: 2.87 us -> 3.15 us  [the longest x1 1.5 us: on_device(): pl.pallas_call(functools.partial(weights_kernel, lo_bits), out_shape=[wei...]
  transfers between devices with their start and end apart: 6 -> 6, of which waited for: 4 -> 4; matrix products, arithmetic and copies ran while one was open for 0% -> 0% of each run, Pallas kernels for 6% -> 9%
where the time goes in v3:
time: 20.1 us; the launch traced here: 20 us
  starting transfers between devices  9.2 us (46%)
  Pallas kernels  5.53 us (28%)
  waiting for transfers between devices  5.2 us (26%)
    ppermute x6, starting transfers between devices, swapped(): return lax.ppermute(block, axis, [(i, i ^ distance) for i in range(count)])  9.2 us
    ppermute x6, waiting for transfers between devices, swapped(): return lax.ppermute(block, axis, [(i, i ^ distance) for i in range(count)])  5.2 us
    pallas_call x1, Pallas kernels, on_device(): pl.pallas_call(functools.partial(first_kernel, lo_bits), out_shape=[pltpu...  2.36 us
    pallas_call x1, Pallas kernels, on_device(): pl.pallas_call(functools.partial(weights_kernel, lo_bits), out_shape=[wei...  1.5 us
    pallas_call x1, Pallas kernels, on_device(): pl.pallas_call(functools.partial(last_kernel, near), out_shape=jax.ShapeD...  1.37 us
  transfers between devices with their start and end apart: 6, of which 4 were waited for; matrix products, arithmetic and copies ran while one was open for 0% of the time, Pallas kernels for 9%

profile of v3, /device:TPU:0, one launch (start us, length us, event | category | flops | bytes accessed | tf_op | source)
XLA Modules:
  0.0 20.0 jit_solution(13481812353422952563)
XLA Ops:
  0.0 2.4 %first_gates.1 = (f32[2,2,64,128]{3,2,1,0:T(8,128)S(1)}, f32[2,64,128]{2,1,0:T(8,128)S(1)}, f32[2,64,128]{2,1,0:T(8,128)S(1)}, f32[4,8,128]{2,1,0:T(8,128)S(1)}, s32[8,128]{1,0:T(8,128)S(1)}) custom-call(s32[15]{0:T(128)} %order_hbm.1, f32[2,2,2]{2,1,0:T(2,128)} %gate_hbm.1, f32[512,128]{1,0:T(8,128)} %bitcast.10, f32[5,2,128,128]{3,2,1,0:T(8,128)} %gates_hbm.3), custom_call_target="tpu_custom_call" | custom-call | tf_op jit(solution)/shard_map/first_gates/pallas_call | solution.py:310
  2.4 4.1 %collective-permute-start = (f32[2,2,64,128]{3,2,1,0:T(8,128)S(1)}, f32[2,2,64,128]{3,2,1,0:T(8,128)S(1)}, u32[]{:S(2)}, u32[]{:S(2)}) collective-permute-start(f32[2,2,64,128]{3,2,1,0:T(8,128)S(1)} %get-tuple-element.16.near_own_ref.own_ref), channel_id=1, source_target_pairs={{0,16},{4,20},{8,24},{12,28},{16,0},{20,4},{24,8},{28,12},{1,17},{... | collective-permute-start | bytes 393224 | tf_op jit(solution)/shard_map/ppermute | solution.py:290
  6.5 1.5 %collective-permute-start.1 = (f32[2,64,128]{2,1,0:T(8,128)S(1)}, f32[2,64,128]{2,1,0:T(8,128)S(1)}, u32[]{:S(2)}, u32[]{:S(2)}) collective-permute-start(f32[2,64,128]{2,1,0:T(8,128)S(1)} %get-tuple-element.17), channel_id=1, source_target_pairs={{0,2},{1,3},{2,0},{3,1},{4,6},{5,7},{6,4},{7,5},{8,10},{9,11},{10,... | collective-permute-start | bytes 196616 | tf_op jit(solution)/shard_map/ppermute | solution.py:290
  8.0 1.4 %collective-permute-start.3 = (f32[2,64,128]{2,1,0:T(8,128)S(1)}, f32[2,64,128]{2,1,0:T(8,128)S(1)}, u32[]{:S(2)}, u32[]{:S(2)}) collective-permute-start(f32[2,64,128]{2,1,0:T(8,128)S(1)} %get-tuple-element.18), channel_id=1, source_target_pairs={{0,3},{1,2},{2,1},{3,0},{4,7},{5,6},{6,5},{7,4},{8,11},{9,10},{10,... | collective-permute-start | bytes 196616 | tf_op jit(solution)/shard_map/ppermute | solution.py:290
  9.4 1.3 %collective-permute-done.1.refs_0_ = f32[2,64,128]{2,1,0:T(8,128)S(1)} collective-permute-done((f32[2,64,128]{2,1,0:T(8,128)S(1)}, f32[2,64,128]{2,1,0:T(8,128)S(1)}, u32[]{:S(2)}, u32[]{:S(2)}) %collective-permute-start.1) | collective-permute-done | bytes 65568 | tf_op jit(solution)/shard_map/ppermute | solution.py:290
  10.7 0.1 collective-permute-start.2
  10.8 2.3 %collective-permute-done.3.own_ref = f32[2,64,128]{2,1,0:T(8,128)S(1)} collective-permute-done((f32[2,64,128]{2,1,0:T(8,128)S(1)}, f32[2,64,128]{2,1,0:T(8,128)S(1)}, u32[]{:S(2)}, u32[]{:S(2)}) %collective-permute-start.3) | collective-permute-done | bytes 65568 | tf_op jit(solution)/shard_map/ppermute | solution.py:290
  13.2 0.5 %collective-permute-start.4 = (f32[2,64,128]{2,1,0:T(8,128)S(1)}, f32[2,64,128]{2,1,0:T(8,128)S(1)}, u32[]{:S(2)}, u32[]{:S(2)}) collective-permute-start(f32[2,64,128]{2,1,0:T(8,128)S(1)} %collective-permute-done.3.own_ref), channel_id=1, source_target_pairs={{0,16},{4,20},{8,24},{12,28},{16,0},{20,4},{24,8},{28,12},{1,17},{... | collective-permute-start | bytes 196616 | tf_op jit(solution)/shard_map/ppermute | solution.py:290
  13.7 0.0 collective-permute-done.near_other_ref.other_ref
  13.7 1.6 %collective-permute-start.5 = (f32[2,64,128]{2,1,0:T(8,128)S(1)}, f32[2,64,128]{2,1,0:T(8,128)S(1)}, u32[]{:S(2)}, u32[]{:S(2)}) collective-permute-start(f32[2,64,128]{2,1,0:T(8,128)S(1)} %mix_pair.1), channel_id=1, source_target_pairs={{0,1},{1,0},{2,3},{3,2},{4,5},{5,4},{6,7},{7,6},{8,9},{9,8},{10,11... | collective-permute-start | bytes 196616 | tf_op jit(solution)/shard_map/ppermute | solution.py:290
  15.3 1.5 %gate_weights.1 = (bf16[2,256,256]{2,1,0:T(8,128)(2,1)S(1)}, bf16[2,256,256]{2,1,0:T(8,128)(2,1)S(1)}) custom-call(s32[8,128]{1,0:T(8,128)S(1)} %get-tuple-element.13.lanes_ref, f32[5,2,128,128]{3,2,1,0:T(8,128)} %gates_hbm.3), custom_call_target="tpu_custom_call" | custom-call | tf_op jit(solution)/shard_map/gate_weights/pallas_call | solution.py:332
  16.8 1.1 %collective-permute-done.2.refs_1_ = f32[2,64,128]{2,1,0:T(8,128)S(1)} collective-permute-done((f32[2,64,128]{2,1,0:T(8,128)S(1)}, f32[2,64,128]{2,1,0:T(8,128)S(1)}, u32[]{:S(2)}, u32[]{:S(2)}) %collective-permute-start.2) | collective-permute-done | bytes 65568 | tf_op jit(solution)/shard_map/ppermute | solution.py:290
  17.9 0.3 %early_gate.1.early_ref = f32[128,256]{1,0:T(8,128)S(1)} custom-call(f32[4,8,128]{2,1,0:T(8,128)S(1)} %get-tuple-element.12.coefs_ref, bf16[2,256,256]{2,1,0:T(8,128)(2,1)S(1)} %get-tuple-element.14.high_ref, bf16[2,256,256]{2,1,0:T(8,128)(2,1)S(1)} %get-tuple-element.15.low_ref, f32[2,2,64,128]{3,2,1,0:T(8,128)S(1)} %get-tuple-element.16.near_own_ref.own_ref, ...), custom_call_target="tpu_custom_call" | custom-call | tf_op jit(solution)/shard_map/early_gate/pallas_call | solution.py:351
  18.2 0.4 %collective-permute-done.4.other_ref = f32[2,64,128]{2,1,0:T(8,128)S(1)} collective-permute-done((f32[2,64,128]{2,1,0:T(8,128)S(1)}, f32[2,64,128]{2,1,0:T(8,128)S(1)}, u32[]{:S(2)}, u32[]{:S(2)}) %collective-permute-start.4) | collective-permute-done | bytes 65568 | tf_op jit(solution)/shard_map/ppermute | solution.py:290
  18.6 0.0 collective-permute-done.5.refs_0_
  18.6 1.4 %last_gates.1 = f32[512,128]{1,0:T(8,128)} custom-call(f32[4,8,128]{2,1,0:T(8,128)S(1)} %get-tuple-element.12.coefs_ref, bf16[2,256,256]{2,1,0:T(8,128)(2,1)S(1)} %get-tuple-element.14.high_ref, bf16[2,256,256]{2,1,0:T(8,128)(2,1)S(1)} %get-tuple-element.15.low_ref, f32[128,256]{1,0:T(8,128)S(1)} %early_gate.1.early_ref, ...), custom_call_target="tpu_custom_call" | custom-call | tf_op jit(solution)/shard_map/last_gates/pallas_call | solution.py:359
  (1 shorter events, 0.0 us)
Async XLA Ops:
  2.4 11.3 %collective-permute-start = (f32[2,2,64,128]{3,2,1,0:T(8,128)S(1)}, f32[2,2,64,128]{3,2,1,0:T(8,128)S(1)}, u32[]{:S(2)}, u32[]{:S(2)}) collective-permute-start(f32[2,2,64,128]{3,2,1,0:T(8,128)S(1)} %get-tuple-element.16.near_own_ref.own_ref), channel_id=1, source_target_pairs={{0,16},{4,20},{8,24},{12,28},{16,0},{20,4},{24,8},{28,12},{1,17},{... | collective-permute-start | bytes 393224 | tf_op jit(solution)/shard_map/ppermute | solution.py:290
  6.5 4.3 %collective-permute-start.1 = (f32[2,64,128]{2,1,0:T(8,128)S(1)}, f32[2,64,128]{2,1,0:T(8,128)S(1)}, u32[]{:S(2)}, u32[]{:S(2)}) collective-permute-start(f32[2,64,128]{2,1,0:T(8,128)S(1)} %get-tuple-element.17), channel_id=1, source_target_pairs={{0,2},{1,3},{2,0},{3,1},{4,6},{5,7},{6,4},{7,5},{8,10},{9,11},{10,... | collective-permute-start | bytes 196616 | tf_op jit(solution)/shard_map/ppermute | solution.py:290
  8.0 5.2 %collective-permute-start.3 = (f32[2,64,128]{2,1,0:T(8,128)S(1)}, f32[2,64,128]{2,1,0:T(8,128)S(1)}, u32[]{:S(2)}, u32[]{:S(2)}) collective-permute-start(f32[2,64,128]{2,1,0:T(8,128)S(1)} %get-tuple-element.18), channel_id=1, source_target_pairs={{0,3},{1,2},{2,1},{3,0},{4,7},{5,6},{6,5},{7,4},{8,11},{9,10},{10,... | collective-permute-start | bytes 196616 | tf_op jit(solution)/shard_map/ppermute | solution.py:290
  10.7 7.1 %collective-permute-start.2 = (f32[2,64,128]{2,1,0:T(8,128)S(1)}, f32[2,64,128]{2,1,0:T(8,128)S(1)}, u32[]{:S(2)}, u32[]{:S(2)}) collective-permute-start(f32[2,64,128]{2,1,0:T(8,128)S(1)} %collective-permute-done.1.refs_0_), channel_id=1, source_target_pairs={{0,16},{4,20},{8,24},{12,28},{16,0},{20,4},{24,8},{28,12},{1,17},{... | collective-permute-start | bytes 196616 | tf_op jit(solution)/shard_map/ppermute | solution.py:290
  13.2 5.4 %collective-permute-start.4 = (f32[2,64,128]{2,1,0:T(8,128)S(1)}, f32[2,64,128]{2,1,0:T(8,128)S(1)}, u32[]{:S(2)}, u32[]{:S(2)}) collective-permute-start(f32[2,64,128]{2,1,0:T(8,128)S(1)} %collective-permute-done.3.own_ref), channel_id=1, source_target_pairs={{0,16},{4,20},{8,24},{12,28},{16,0},{20,4},{24,8},{28,12},{1,17},{... | collective-permute-start | bytes 196616 | tf_op jit(solution)/shard_map/ppermute | solution.py:290
  13.7 4.9 %collective-permute-start.5 = (f32[2,64,128]{2,1,0:T(8,128)S(1)}, f32[2,64,128]{2,1,0:T(8,128)S(1)}, u32[]{:S(2)}, u32[]{:S(2)}) collective-permute-start(f32[2,64,128]{2,1,0:T(8,128)S(1)} %mix_pair.1), channel_id=1, source_target_pairs={{0,1},{1,0},{2,3},{3,2},{4,5},{5,4},{6,7},{7,6},{8,9},{9,8},{10,11... | collective-permute-start | bytes 196616 | tf_op jit(solution)/shard_map/ppermute | solution.py:290

commit v4 on v3

--- a/solution.py
+++ b/solution.py
@@ -210,73 +210,95 @@
         out_ref[0], out_ref[1] = mixed(coefs_ref, own_ref.at[k + 1], other_ref.at[k + 1])
 
 
-def weights_kernel(lo_bits, lanes_ref, gates_hbm, high_ref, low_ref, gates_ref, sems):
+def arrival(parts):
+    near = parts // 2
+    return [0, *range(near, parts - 1)], [*range(1, near), parts - 1]
+
+
+def weights_kernel(lo_bits, lanes_ref, gates_hbm, low_gate_ref, early_ref, late_ref, gates_ref, sems):
     fetches = [pltpu.make_async_copy(gates_hbm.at[2 + g], gates_ref.at[g], sems.at[g]) for g in range(3)]
     for fetch in fetches:
         fetch.start()
     lanes = one_hot(WIDTH, lanes_ref[0:1])
+    parts = 1 << lo_bits
+    kept = WIDTH // parts
     me = lax.axis_index("lo")
-    rows = one_hot(WIDTH, jnp.bitwise_xor(lax.broadcasted_iota(jnp.int32, (1, WIDTH), 1), me * (WIDTH >> lo_bits)))
+    index = lax.broadcasted_iota(jnp.int32, (1, WIDTH), 1)
+    source = index % kept
+    early, late = arrival(parts)
+    for place, step in enumerate(early + late):
+        source = source + jnp.where(index // kept == place, jnp.bitwise_xor(me, step) * kept, 0)
+    rows = one_hot(WIDTH, source)
     for fetch in fetches:
         fetch.wait()
-    first = [[dot(part, rows).astype(BF16) for part in halves(gates_ref[0, c])] for c in range(2)]
-    last = [halves(gates_ref[2, c]) for c in range(2)]
-    real = halves(dot3(last[0], first[0]) - dot3(last[1], first[1]))
-    imag = halves(dot3(last[0], first[1]) + dot3(last[1], first[0]))
-    for i, out in enumerate((high_ref, low_ref)):
-        out[0] = block_matrix(*[dot(halves(gates_ref[1, c])[i], lanes).astype(BF16) for c in range(2)])
-        out[1] = block_matrix(real[i], imag[i])
-
-
-def low_gate(high_ref, low_ref, values):
+
+    def exact(left, right):
+        return lax.dot_general(
+            left, right, (((1,), (0,)), ((), ())), precision=lax.Precision.HIGHEST, preferred_element_type=F32
+        )
+
+    first, last = [gates_ref[0, c] for c in range(2)], [gates_ref[2, c] for c in range(2)]
+    real = halves(exact(last[0], first[0]) - exact(last[1], first[1]))
+    imag = halves(exact(last[0], first[1]) + exact(last[1], first[0]))
+    half = len(early) * kept
+    for i in range(2):
+        real3, imag3 = [dot(halves(gates_ref[1, c])[i], lanes).T for c in range(2)]
+        low_gate_ref[i] = block_matrix(real3, -imag3).astype(BF16)
+        both = [dot(part[i], rows) for part in (real, imag)]
+        early_ref[i] = block_matrix(*[part[:, :half] for part in both]).astype(BF16)
+        late_ref[i] = block_matrix(*[part[:, half:] for part in both]).astype(BF16)
+
+
+def low_gate(matrix_ref, values):
     state = jnp.concatenate([jnp.concatenate(value, axis=1) for value in values], axis=0)
-    return dot3(halves(state), (high_ref[0], low_ref[0]), transposed=True)
-
-
-def early_kernel(coefs_ref, high_ref, low_ref, near_own_ref, near_other_ref, *refs):
-    ins, out_ref = refs[:-1], refs[-1]
-    values = [mixed(coefs_ref, near_own_ref.at[0], near_other_ref.at[0])]
-    values += [mixed(coefs_ref, own, other) for own, other in zip(ins[0::2], ins[1::2], strict=True)]
-    state = low_gate(high_ref, low_ref, values)
-    out_ref[...] = state
-
-
-def last_kernel(near, coefs_ref, high_ref, low_ref, early_ref, own_ref, other_ref, *refs):
-    ins, (out_hbm, out_ref, sems) = refs[:-3], refs[-3:]
-    values = [(ref[0], ref[1]) for ref in ins] + [mixed(coefs_ref, own_ref, other_ref)]
-    state = low_gate(high_ref, low_ref, values)
-    count = values[0][0].shape[0]
+    state = dot3(halves(state), (matrix_ref[0], matrix_ref[1]))
+    count = state.shape[0] // len(values)
     kept = count // 2
-    blocks = [early_ref[i * count : (i + 1) * count] for i in range(early_ref.shape[0] // count)]
-    late = [state[i * count : (i + 1) * count] for i in range(len(values))]
-    blocks = blocks[:1] + late[:-1] + blocks[1:] + late[-1:]
-    state = jnp.concatenate(
+    return jnp.concatenate(
         [
             jnp.concatenate(
                 [
-                    jnp.concatenate([block[m * kept : (m + 1) * kept, c * WIDTH : (c + 1) * WIDTH] for block in blocks], axis=0)
+                    state[i * count + m * kept : i * count + (m + 1) * kept, c * WIDTH : (c + 1) * WIDTH]
                     for m in range(2)
                 ],
                 axis=1,
             )
             for c in range(2)
+            for i in range(len(values))
         ],
         axis=0,
     )
-    state = halves(state)
+
+
+def early_kernel(coefs_ref, low_gate_ref, high_gate_ref, near_own_ref, near_other_ref, *refs):
+    ins, out_ref = refs[:-1], refs[-1]
+    values = [mixed(coefs_ref, near_own_ref.at[0], near_other_ref.at[0])]
+    values += [mixed(coefs_ref, own, other) for own, other in zip(ins[0::2], ins[1::2], strict=True)]
+    out_ref[...] = dot3((high_gate_ref[0], high_gate_ref[1]), halves(low_gate(low_gate_ref, values)))
+
+
+def last_kernel(coefs_ref, low_gate_ref, high_gate_ref, early_ref, own_ref, other_ref, *refs):
+    ins, (out_hbm, out_ref, sems) = refs[:-3], refs[-3:]
+    values = [(ref[0], ref[1]) for ref in ins] + [mixed(coefs_ref, own_ref, other_ref)]
+    high, low = halves(low_gate(low_gate_ref, values))
+    state = jnp.concatenate([low, high, high], axis=0)
     sends = []
     half = WIDTH // 2
     for i in range(2):
         matrix = [
-            jnp.concatenate([ref[1, c * WIDTH + i * half : c * WIDTH + (i + 1) * half] for c in range(2)], axis=0)
-            for ref in (high_ref, low_ref)
+            jnp.concatenate(
+                [high_gate_ref[j, c * WIDTH + i * half : c * WIDTH + (i + 1) * half] for c in range(2)], axis=0
+            )
+            for j in (0, 1, 0)
         ]
-        result = dot3(matrix, state)
+        result = dot(jnp.concatenate(matrix, axis=1), state)
         for c in range(2):
             for m in range(2):
-                out_ref[pl.ds(i * 256 + m * 2 + c, half, stride=4), :] = result[
-                    c * half : (c + 1) * half, m * WIDTH : (m + 1) * WIDTH
-                ]
+                at = c * WIDTH + i * half
+                out_ref[pl.ds(i * 256 + m * 2 + c, half, stride=4), :] = (
+                    early_ref[at : at + half, m * WIDTH : (m + 1) * WIDTH]
+                    + result[c * half : (c + 1) * half, m * WIDTH : (m + 1) * WIDTH]
+                )
         sends.append(
             pltpu.make_async_copy(out_ref.at[pl.ds(i * 256, 256)], out_hbm.at[pl.ds(i * 256, 256)], sems.at[i])
         )
@@ -328,12 +350,12 @@
     near_other = swapped(near_own, "hi", top)
     far_own = [swapped(far, "lo", near + i) for i, far in enumerate(far_own)]
     far_other = [swapped(far, "hi", top) for far in far_own]
-    weights = pltpu.VMEM((2, 256, 256), BF16)
-    high, low = pl.pallas_call(
+    counts = [2 * kept * len(steps) for steps in arrival(parts)]
+    low_weights, early_weights, late_weights = pl.pallas_call(
         functools.partial(weights_kernel, lo_bits),
-        out_shape=[weights] * 2,
+        out_shape=[pltpu.VMEM((2, 256, count), BF16) for count in (256, *counts)],
         in_specs=[VMEM, HBM],
-        out_specs=[VMEM] * 2,
+        out_specs=[VMEM] * 3,
         scratch_shapes=[pltpu.VMEM((3, 2, WIDTH, WIDTH), F32), pltpu.SemaphoreType.DMA((3,))],
         compiler_params=PARAMS,
         name="gate_weights",
@@ -350,21 +372,21 @@
     pairs = [value for pair in zip(far_own[:-1], far_other[:-1], strict=True) for value in pair]
     early = pl.pallas_call(
         early_kernel,
-        out_shape=pltpu.VMEM(((parts - near) * 2 * kept, 2 * WIDTH), F32),
+        out_shape=pltpu.VMEM((256, 256), F32),
         in_specs=[VMEM] * (5 + len(pairs)),
         out_specs=VMEM,
         compiler_params=PARAMS,
         name="early_gate",
-    )(coefs, high, low, near_own, near_other, *pairs)
+    )(coefs, low_weights, early_weights, near_own, near_other, *pairs)
     out = pl.pallas_call(
-        functools.partial(last_kernel, near),
+        last_kernel,
         out_shape=jax.ShapeDtypeStruct((512, WIDTH), F32),
         in_specs=[VMEM] * (6 + len(mixes)),
         out_specs=HBM,
         scratch_shapes=[pltpu.VMEM((512, WIDTH), F32), pltpu.SemaphoreType.DMA((2,))],
         compiler_params=PARAMS,
         name="last_gates",
-    )(coefs, high, low, early, far_own[-1], far_other[-1], *mixes)
+    )(coefs, low_weights, late_weights, early, far_own[-1], far_other[-1], *mixes)
     return out.reshape(256, 2, WIDTH).transpose(1, 0, 2).reshape(2, -1)
 
 

time: 20.1 us -> 19.9 us (0.990)
  waiting for transfers between devices: 5.2 us -> 4.64 us
  Pallas kernels: 5.53 us -> 5.91 us
    ppermute x6, waiting for transfers between devices: 5.2 us -> 4.64 us  [swapped(): return lax.ppermute(block, axis, [(i, i ^ distance) for i in range(count)])]
    pallas_call x3, Pallas kernels: 3.15 us -> 3.53 us  [the longest x1 1.8 us: on_device(): pl.pallas_call(functools.partial(weights_kernel, lo_bits), out_shape=[plt...]
  transfers between devices with their start and end apart: 6 -> 6, of which waited for: 4 -> 4; matrix products, arithmetic and copies ran while one was open for 0% -> 0% of each run, Pallas kernels for 9% -> 12%
where the time goes in v4:
time: 19.9 us; the launch traced here: 19.8 us
  starting transfers between devices  9.2 us (46%)
  Pallas kernels  5.91 us (30%)
  waiting for transfers between devices  4.64 us (23%)
    ppermute x6, starting transfers between devices, swapped(): return lax.ppermute(block, axis, [(i, i ^ distance) for i in range(count)])  9.2 us
    ppermute x6, waiting for transfers between devices, swapped(): return lax.ppermute(block, axis, [(i, i ^ distance) for i in range(count)])  4.64 us
    pallas_call x1, Pallas kernels, on_device(): pl.pallas_call(functools.partial(first_kernel, lo_bits), out_shape=[pltpu...  2.36 us
    pallas_call x1, Pallas kernels, on_device(): pl.pallas_call(functools.partial(weights_kernel, lo_bits), out_shape=[plt...  1.8 us
    pallas_call x1, Pallas kernels, on_device(): pl.pallas_call(last_kernel, out_shape=jax.ShapeDtypeStruct((512, WIDTH),...  1.19 us
    pallas_call x1, Pallas kernels, on_device(): pl.pallas_call(early_kernel, out_shape=pltpu.VMEM((256, 256), F32), in_sp...  0.53 us
  transfers between devices with their start and end apart: 6, of which 4 were waited for; matrix products, arithmetic and copies ran while one was open for 0% of the time, Pallas kernels for 12%

profile of v4, /device:TPU:0, one launch (start us, length us, event | category | flops | bytes accessed | tf_op | source)
XLA Modules:
  0.0 19.8 jit_solution(10548828729027057919)
XLA Ops:
  0.0 2.4 %first_gates.1 = (f32[2,2,64,128]{3,2,1,0:T(8,128)S(1)}, f32[2,64,128]{2,1,0:T(8,128)S(1)}, f32[2,64,128]{2,1,0:T(8,128)S(1)}, f32[4,8,128]{2,1,0:T(8,128)S(1)}, s32[8,128]{1,0:T(8,128)S(1)}) custom-call(s32[15]{0:T(128)} %order_hbm.1, f32[2,2,2]{2,1,0:T(2,128)} %gate_hbm.1, f32[512,128]{1,0:T(8,128)} %bitcast.10, f32[5,2,128,128]{3,2,1,0:T(8,128)} %gates_hbm.3), custom_call_target="tpu_custom_call" | custom-call | tf_op jit(solution)/shard_map/first_gates/pallas_call | solution.py:332
  2.4 4.1 %collective-permute-start = (f32[2,2,64,128]{3,2,1,0:T(8,128)S(1)}, f32[2,2,64,128]{3,2,1,0:T(8,128)S(1)}, u32[]{:S(2)}, u32[]{:S(2)}) collective-permute-start(f32[2,2,64,128]{3,2,1,0:T(8,128)S(1)} %get-tuple-element.18.near_own_ref.own_ref), channel_id=1, source_target_pairs={{0,16},{4,20},{8,24},{12,28},{16,0},{20,4},{24,8},{28,12},{1,17},{... | collective-permute-start | bytes 393224 | tf_op jit(solution)/shard_map/ppermute | solution.py:312
  6.5 1.5 %collective-permute-start.1 = (f32[2,64,128]{2,1,0:T(8,128)S(1)}, f32[2,64,128]{2,1,0:T(8,128)S(1)}, u32[]{:S(2)}, u32[]{:S(2)}) collective-permute-start(f32[2,64,128]{2,1,0:T(8,128)S(1)} %get-tuple-element.19), channel_id=1, source_target_pairs={{0,2},{1,3},{2,0},{3,1},{4,6},{5,7},{6,4},{7,5},{8,10},{9,11},{10,... | collective-permute-start | bytes 196616 | tf_op jit(solution)/shard_map/ppermute | solution.py:312
  8.0 1.4 %collective-permute-start.3 = (f32[2,64,128]{2,1,0:T(8,128)S(1)}, f32[2,64,128]{2,1,0:T(8,128)S(1)}, u32[]{:S(2)}, u32[]{:S(2)}) collective-permute-start(f32[2,64,128]{2,1,0:T(8,128)S(1)} %get-tuple-element.20), channel_id=1, source_target_pairs={{0,3},{1,2},{2,1},{3,0},{4,7},{5,6},{6,5},{7,4},{8,11},{9,10},{10,... | collective-permute-start | bytes 196616 | tf_op jit(solution)/shard_map/ppermute | solution.py:312
  9.4 1.3 %collective-permute-done.1.refs_0_ = f32[2,64,128]{2,1,0:T(8,128)S(1)} collective-permute-done((f32[2,64,128]{2,1,0:T(8,128)S(1)}, f32[2,64,128]{2,1,0:T(8,128)S(1)}, u32[]{:S(2)}, u32[]{:S(2)}) %collective-permute-start.1) | collective-permute-done | bytes 65568 | tf_op jit(solution)/shard_map/ppermute | solution.py:312
  10.7 0.1 collective-permute-start.2
  10.8 2.3 %collective-permute-done.3.own_ref = f32[2,64,128]{2,1,0:T(8,128)S(1)} collective-permute-done((f32[2,64,128]{2,1,0:T(8,128)S(1)}, f32[2,64,128]{2,1,0:T(8,128)S(1)}, u32[]{:S(2)}, u32[]{:S(2)}) %collective-permute-start.3) | collective-permute-done | bytes 65568 | tf_op jit(solution)/shard_map/ppermute | solution.py:312
  13.2 0.5 %collective-permute-start.4 = (f32[2,64,128]{2,1,0:T(8,128)S(1)}, f32[2,64,128]{2,1,0:T(8,128)S(1)}, u32[]{:S(2)}, u32[]{:S(2)}) collective-permute-start(f32[2,64,128]{2,1,0:T(8,128)S(1)} %collective-permute-done.3.own_ref), channel_id=1, source_target_pairs={{0,16},{4,20},{8,24},{12,28},{16,0},{20,4},{24,8},{28,12},{1,17},{... | collective-permute-start | bytes 196616 | tf_op jit(solution)/shard_map/ppermute | solution.py:312
  13.7 0.0 collective-permute-done.near_other_ref.other_ref
  13.7 1.6 %collective-permute-start.5 = (f32[2,64,128]{2,1,0:T(8,128)S(1)}, f32[2,64,128]{2,1,0:T(8,128)S(1)}, u32[]{:S(2)}, u32[]{:S(2)}) collective-permute-start(f32[2,64,128]{2,1,0:T(8,128)S(1)} %mix_pair.1), channel_id=1, source_target_pairs={{0,1},{1,0},{2,3},{3,2},{4,5},{5,4},{6,7},{7,6},{8,9},{9,8},{10,11... | collective-permute-start | bytes 196616 | tf_op jit(solution)/shard_map/ppermute | solution.py:312
  15.3 1.8 %gate_weights.1 = (bf16[2,256,256]{2,1,0:T(8,128)(2,1)S(1)}, bf16[2,256,128]{2,1,0:T(8,128)(2,1)S(1)}, bf16[2,256,128]{2,1,0:T(8,128)(2,1)S(1)}) custom-call(s32[8,128]{1,0:T(8,128)S(1)} %get-tuple-element.14.lanes_ref, f32[5,2,128,128]{3,2,1,0:T(8,128)} %gates_hbm.3), custom_call_target="tpu_custom_call" | custom-call | tf_op jit(solution)/shard_map/gate_weights/pallas_call | solution.py:354
  17.1 0.8 %collective-permute-done.2.refs_1_ = f32[2,64,128]{2,1,0:T(8,128)S(1)} collective-permute-done((f32[2,64,128]{2,1,0:T(8,128)S(1)}, f32[2,64,128]{2,1,0:T(8,128)S(1)}, u32[]{:S(2)}, u32[]{:S(2)}) %collective-permute-start.2) | collective-permute-done | bytes 65568 | tf_op jit(solution)/shard_map/ppermute | solution.py:312
  17.9 0.5 %early_gate.1.early_ref = f32[256,256]{1,0:T(8,128)S(1)} custom-call(f32[4,8,128]{2,1,0:T(8,128)S(1)} %get-tuple-element.13.coefs_ref, bf16[2,256,256]{2,1,0:T(8,128)(2,1)S(1)} %get-tuple-element.15.low_gate_ref, bf16[2,256,128]{2,1,0:T(8,128)(2,1)S(1)} %get-tuple-element.17.high_gate_ref, f32[2,2,64,128]{3,2,1,0:T(8,128)S(1)} %get-tuple-element.18.near_own_ref.own_ref, ...), custom_call_target="tpu_custom_call" | custom-call | tf_op jit(solution)/shard_map/early_gate/pallas_call | solution.py:373
  18.4 0.2 collective-permute-done.4.other_ref
  18.6 0.0 collective-permute-done.5.refs_0_
  18.6 1.2 %last_gates.1 = f32[512,128]{1,0:T(8,128)} custom-call(f32[4,8,128]{2,1,0:T(8,128)S(1)} %get-tuple-element.13.coefs_ref, bf16[2,256,256]{2,1,0:T(8,128)(2,1)S(1)} %get-tuple-element.15.low_gate_ref, bf16[2,256,128]{2,1,0:T(8,128)(2,1)S(1)} %get-tuple-element.16.high_gate_ref, f32[256,256]{1,0:T(8,128)S(1)} %early_gate.1.early_ref, ...), custom_call_target="tpu_custom_call" | custom-call | tf_op jit(solution)/shard_map/last_gates/pallas_call | solution.py:381
  (1 shorter events, 0.0 us)
Async XLA Ops:
  2.4 11.3 %collective-permute-start = (f32[2,2,64,128]{3,2,1,0:T(8,128)S(1)}, f32[2,2,64,128]{3,2,1,0:T(8,128)S(1)}, u32[]{:S(2)}, u32[]{:S(2)}) collective-permute-start(f32[2,2,64,128]{3,2,1,0:T(8,128)S(1)} %get-tuple-element.18.near_own_ref.own_ref), channel_id=1, source_target_pairs={{0,16},{4,20},{8,24},{12,28},{16,0},{20,4},{24,8},{28,12},{1,17},{... | collective-permute-start | bytes 393224 | tf_op jit(solution)/shard_map/ppermute | solution.py:312
  6.5 4.3 %collective-permute-start.1 = (f32[2,64,128]{2,1,0:T(8,128)S(1)}, f32[2,64,128]{2,1,0:T(8,128)S(1)}, u32[]{:S(2)}, u32[]{:S(2)}) collective-permute-start(f32[2,64,128]{2,1,0:T(8,128)S(1)} %get-tuple-element.19), channel_id=1, source_target_pairs={{0,2},{1,3},{2,0},{3,1},{4,6},{5,7},{6,4},{7,5},{8,10},{9,11},{10,... | collective-permute-start | bytes 196616 | tf_op jit(solution)/shard_map/ppermute | solution.py:312
  8.0 5.2 %collective-permute-start.3 = (f32[2,64,128]{2,1,0:T(8,128)S(1)}, f32[2,64,128]{2,1,0:T(8,128)S(1)}, u32[]{:S(2)}, u32[]{:S(2)}) collective-permute-start(f32[2,64,128]{2,1,0:T(8,128)S(1)} %get-tuple-element.20), channel_id=1, source_target_pairs={{0,3},{1,2},{2,1},{3,0},{4,7},{5,6},{6,5},{7,4},{8,11},{9,10},{10,... | collective-permute-start | bytes 196616 | tf_op jit(solution)/shard_map/ppermute | solution.py:312
  10.7 7.1 %collective-permute-start.2 = (f32[2,64,128]{2,1,0:T(8,128)S(1)}, f32[2,64,128]{2,1,0:T(8,128)S(1)}, u32[]{:S(2)}, u32[]{:S(2)}) collective-permute-start(f32[2,64,128]{2,1,0:T(8,128)S(1)} %collective-permute-done.1.refs_0_), channel_id=1, source_target_pairs={{0,16},{4,20},{8,24},{12,28},{16,0},{20,4},{24,8},{28,12},{1,17},{... | collective-permute-start | bytes 196616 | tf_op jit(solution)/shard_map/ppermute | solution.py:312
  13.2 5.4 %collective-permute-start.4 = (f32[2,64,128]{2,1,0:T(8,128)S(1)}, f32[2,64,128]{2,1,0:T(8,128)S(1)}, u32[]{:S(2)}, u32[]{:S(2)}) collective-permute-start(f32[2,64,128]{2,1,0:T(8,128)S(1)} %collective-permute-done.3.own_ref), channel_id=1, source_target_pairs={{0,16},{4,20},{8,24},{12,28},{16,0},{20,4},{24,8},{28,12},{1,17},{... | collective-permute-start | bytes 196616 | tf_op jit(solution)/shard_map/ppermute | solution.py:312
  13.7 4.9 %collective-permute-start.5 = (f32[2,64,128]{2,1,0:T(8,128)S(1)}, f32[2,64,128]{2,1,0:T(8,128)S(1)}, u32[]{:S(2)}, u32[]{:S(2)}) collective-permute-start(f32[2,64,128]{2,1,0:T(8,128)S(1)} %mix_pair.1), channel_id=1, source_target_pairs={{0,1},{1,0},{2,3},{3,2},{4,5},{5,4},{6,7},{7,6},{8,9},{9,8},{10,11... | collective-permute-start | bytes 196616 | tf_op jit(solution)/shard_map/ppermute | solution.py:312

commit v5 on v4

--- a/solution.py
+++ b/solution.py
@@ -205,9 +205,10 @@
     )
 
 
-def mix_kernel(coefs_ref, own_ref, other_ref, *outs):
-    for k, out_ref in enumerate(outs):
-        out_ref[0], out_ref[1] = mixed(coefs_ref, own_ref.at[k + 1], other_ref.at[k + 1])
+def mix_kernel(coefs_ref, matrix_ref, own_ref, other_ref, *outs):
+    values = [mixed(coefs_ref, own_ref.at[k + 1], other_ref.at[k + 1]) for k in range(len(outs))]
+    for out_ref, value in zip(outs, low_gate(matrix_ref, values), strict=True):
+        out_ref[0], out_ref[1] = value
 
 
 def arrival(parts):
@@ -215,11 +216,20 @@
     return [0, *range(near, parts - 1)], [*range(1, near), parts - 1]
 
 
-def weights_kernel(lo_bits, lanes_ref, gates_hbm, low_gate_ref, early_ref, late_ref, gates_ref, sems):
-    fetches = [pltpu.make_async_copy(gates_hbm.at[2 + g], gates_ref.at[g], sems.at[g]) for g in range(3)]
+def low_weights_kernel(lanes_ref, gates_hbm, out_ref, gate_ref, sem):
+    fetch = pltpu.make_async_copy(gates_hbm.at[3], gate_ref, sem)
+    fetch.start()
+    lanes = one_hot(WIDTH, lanes_ref[0:1])
+    fetch.wait()
+    for i in range(2):
+        real, imag = [dot(halves(gate_ref[c])[i], lanes).T for c in range(2)]
+        out_ref[i] = block_matrix(real, -imag).astype(BF16)
+
+
+def high_weights_kernel(lo_bits, gates_hbm, early_ref, late_ref, gates_ref, sems):
+    fetches = [pltpu.make_async_copy(gates_hbm.at[2 + 2 * g], gates_ref.at[g], sems.at[g]) for g in range(2)]
     for fetch in fetches:
         fetch.start()
-    lanes = one_hot(WIDTH, lanes_ref[0:1])
     parts = 1 << lo_bits
     kept = WIDTH // parts
     me = lax.axis_index("lo")
@@ -237,13 +247,11 @@
             left, right, (((1,), (0,)), ((), ())), precision=lax.Precision.HIGHEST, preferred_element_type=F32
         )
 
-    first, last = [gates_ref[0, c] for c in range(2)], [gates_ref[2, c] for c in range(2)]
+    first, last = [[gates_ref[g, c] for c in range(2)] for g in range(2)]
     real = halves(exact(last[0], first[0]) - exact(last[1], first[1]))
     imag = halves(exact(last[0], first[1]) + exact(last[1], first[0]))
     half = len(early) * kept
     for i in range(2):
-        real3, imag3 = [dot(halves(gates_ref[1, c])[i], lanes).T for c in range(2)]
-        low_gate_ref[i] = block_matrix(real3, -imag3).astype(BF16)
         both = [dot(part[i], rows) for part in (real, imag)]
         early_ref[i] = block_matrix(*[part[:, :half] for part in both]).astype(BF16)
         late_ref[i] = block_matrix(*[part[:, half:] for part in both]).astype(BF16)
@@ -253,34 +261,43 @@
     state = jnp.concatenate([jnp.concatenate(value, axis=1) for value in values], axis=0)
     state = dot3(halves(state), (matrix_ref[0], matrix_ref[1]))
     count = state.shape[0] // len(values)
-    kept = count // 2
+    return [
+        [state[i * count : (i + 1) * count, c * WIDTH : (c + 1) * WIDTH] for c in range(2)] for i in range(len(values))
+    ]
+
+
+def for_high(values):
+    kept = values[0][0].shape[0] // 2
     return jnp.concatenate(
         [
-            jnp.concatenate(
-                [
-                    state[i * count + m * kept : i * count + (m + 1) * kept, c * WIDTH : (c + 1) * WIDTH]
-                    for m in range(2)
-                ],
-                axis=1,
-            )
+            jnp.concatenate([value[c][m * kept : (m + 1) * kept] for m in range(2)], axis=1)
             for c in range(2)
-            for i in range(len(values))
+            for value in values
         ],
         axis=0,
     )
+
+
+def copy_kernel(in_ref, out_ref):
+    out_ref[...] = in_ref[...]
+
+
+def low_kernel(matrix_ref, in_ref, out_ref):
+    (value,) = low_gate(matrix_ref, [(in_ref[0], in_ref[1])])
+    out_ref[0], out_ref[1] = value
 
 
 def early_kernel(coefs_ref, low_gate_ref, high_gate_ref, near_own_ref, near_other_ref, *refs):
     ins, out_ref = refs[:-1], refs[-1]
     values = [mixed(coefs_ref, near_own_ref.at[0], near_other_ref.at[0])]
     values += [mixed(coefs_ref, own, other) for own, other in zip(ins[0::2], ins[1::2], strict=True)]
-    out_ref[...] = dot3((high_gate_ref[0], high_gate_ref[1]), halves(low_gate(low_gate_ref, values)))
-
-
-def last_kernel(coefs_ref, low_gate_ref, high_gate_ref, early_ref, own_ref, other_ref, *refs):
+    out_ref[...] = dot3((high_gate_ref[0], high_gate_ref[1]), halves(for_high(low_gate(low_gate_ref, values))))
+
+
+def last_kernel(coefs_ref, high_gate_ref, early_ref, own_ref, other_ref, *refs):
     ins, (out_hbm, out_ref, sems) = refs[:-3], refs[-3:]
     values = [(ref[0], ref[1]) for ref in ins] + [mixed(coefs_ref, own_ref, other_ref)]
-    high, low = halves(low_gate(low_gate_ref, values))
+    high, low = halves(for_high(values))
     state = jnp.concatenate([low, high, high], axis=0)
     sends = []
     half = WIDTH // 2
@@ -349,25 +366,40 @@
     )(in_hbm(qubit_order), in_hbm(dev_gate), in_hbm(rows), in_hbm(gate_mats))
     near_other = swapped(near_own, "hi", top)
     far_own = [swapped(far, "lo", near + i) for i, far in enumerate(far_own)]
+    counts = [2 * kept * len(steps) for steps in arrival(parts)]
+    low_weights = pl.pallas_call(
+        low_weights_kernel,
+        out_shape=pltpu.VMEM((2, 256, 256), BF16),
+        in_specs=[VMEM, HBM],
+        out_specs=VMEM,
+        scratch_shapes=[pltpu.VMEM((2, WIDTH, WIDTH), F32), pltpu.SemaphoreType.DMA],
+        compiler_params=PARAMS,
+        name="low_weights",
+    )(lanes, in_hbm(gate_mats))
+    early_weights, late_weights = pl.pallas_call(
+        functools.partial(high_weights_kernel, lo_bits),
+        out_shape=[pltpu.VMEM((2, 256, count), BF16) for count in counts],
+        in_specs=[HBM],
+        out_specs=[VMEM] * 2,
+        scratch_shapes=[pltpu.VMEM((2, 2, WIDTH, WIDTH), F32), pltpu.SemaphoreType.DMA((2,))],
+        compiler_params=PARAMS,
+        name="high_weights",
+    )(in_hbm(gate_mats))
+    far_own[-1] = pl.pallas_call(
+        low_kernel, out_shape=block, in_specs=[VMEM] * 2, out_specs=VMEM, compiler_params=PARAMS, name="low_gate"
+    )(low_weights, far_own[-1])
     far_other = [swapped(far, "hi", top) for far in far_own]
-    counts = [2 * kept * len(steps) for steps in arrival(parts)]
-    low_weights, early_weights, late_weights = pl.pallas_call(
-        functools.partial(weights_kernel, lo_bits),
-        out_shape=[pltpu.VMEM((2, 256, count), BF16) for count in (256, *counts)],
-        in_specs=[VMEM, HBM],
-        out_specs=[VMEM] * 3,
-        scratch_shapes=[pltpu.VMEM((3, 2, WIDTH, WIDTH), F32), pltpu.SemaphoreType.DMA((3,))],
-        compiler_params=PARAMS,
-        name="gate_weights",
-    )(lanes, in_hbm(gate_mats))
+    far_other[0] = pl.pallas_call(
+        copy_kernel, out_shape=block, in_specs=[VMEM], out_specs=VMEM, compiler_params=PARAMS, name="arrived"
+    )(far_other[0])
     mixes = pl.pallas_call(
         mix_kernel,
         out_shape=[block] * (near - 1),
-        in_specs=[VMEM] * 3,
+        in_specs=[VMEM] * 4,
         out_specs=[VMEM] * (near - 1),
         compiler_params=PARAMS,
         name="mix_pair",
-    )(coefs, near_own, near_other)
+    )(coefs, low_weights, near_own, near_other)
     mixes = [swapped(mix, "lo", 1 + i) for i, mix in enumerate(mixes)]
     pairs = [value for pair in zip(far_own[:-1], far_other[:-1], strict=True) for value in pair]
     early = pl.pallas_call(
@@ -381,12 +413,12 @@
     out = pl.pallas_call(
         last_kernel,
         out_shape=jax.ShapeDtypeStruct((512, WIDTH), F32),
-        in_specs=[VMEM] * (6 + len(mixes)),
+        in_specs=[VMEM] * (5 + len(mixes)),
         out_specs=HBM,
         scratch_shapes=[pltpu.VMEM((512, WIDTH), F32), pltpu.SemaphoreType.DMA((2,))],
         compiler_params=PARAMS,
         name="last_gates",
-    )(coefs, low_weights, late_weights, early, far_own[-1], far_other[-1], *mixes)
+    )(coefs, late_weights, early, far_own[-1], far_other[-1], *mixes)
     return out.reshape(256, 2, WIDTH).transpose(1, 0, 2).reshape(2, -1)
 
 

time: 19.9 us -> 19.8 us (level)
  waiting for transfers between devices: 4.64 us -> 3.08 us
  Pallas kernels: 5.91 us -> 7.05 us
  starting transfers between devices: 9.2 us -> 9.5 us
    ppermute x6, waiting for transfers between devices: 4.64 us -> 3.08 us  [swapped(): return lax.ppermute(block, axis, [(i, i ^ distance) for i in range(count)])]
    pallas_call x1 -> x4, Pallas kernels: 1.8 us -> 3 us  [the longest x1 1.61 us: on_device(): pl.pallas_call(functools.partial(high_weights_kernel, lo_bits), out_shape...]
    ppermute x6, starting transfers between devices: 9.2 us -> 9.5 us  [swapped(): return lax.ppermute(block, axis, [(i, i ^ distance) for i in range(count)])]
    pallas_call x1, Pallas kernels: 1.19 us -> 0.96 us  [on_device(): pl.pallas_call(last_kernel, out_shape=jax.ShapeDtypeStruct((512, WIDTH),...]
  transfers between devices with their start and end apart: 6 -> 6, of which waited for: 4 -> 4; matrix products, arithmetic and copies ran while one was open for 0% -> 0% of each run, Pallas kernels for 12% -> 19%
where the time goes in v5:
time: 19.8 us; the launch traced here: 19.7 us
  starting transfers between devices  9.5 us (48%)
  Pallas kernels  7.05 us (36%)
  waiting for transfers between devices  3.08 us (16%)
    ppermute x6, starting transfers between devices, swapped(): return lax.ppermute(block, axis, [(i, i ^ distance) for i in range(count)])  9.5 us
    ppermute x6, waiting for transfers between devices, swapped(): return lax.ppermute(block, axis, [(i, i ^ distance) for i in range(count)])  3.08 us
    pallas_call x1, Pallas kernels, on_device(): pl.pallas_call(functools.partial(first_kernel, lo_bits), out_shape=[pltpu...  2.36 us
    pallas_call x1, Pallas kernels, on_device(): pl.pallas_call(functools.partial(high_weights_kernel, lo_bits), out_shape...  1.61 us
    pallas_call x1, Pallas kernels, on_device(): pl.pallas_call(low_weights_kernel, out_shape=pltpu.VMEM((2, 256, 256), BF...  1.21 us
    pallas_call x1, Pallas kernels, on_device(): pl.pallas_call(last_kernel, out_shape=jax.ShapeDtypeStruct((512, WIDTH),...  0.96 us
    pallas_call x1, Pallas kernels, on_device(): pl.pallas_call(early_kernel, out_shape=pltpu.VMEM((256, 256), F32), in_sp...  0.53 us
  transfers between devices with their start and end apart: 6, of which 4 were waited for; matrix products, arithmetic and copies ran while one was open for 0% of the time, Pallas kernels for 19%

profile of v5, /device:TPU:0, one launch (start us, length us, event | category | flops | bytes accessed | tf_op | source)
XLA Modules:
  0.0 19.7 jit_solution(9799444518656006219)
XLA Ops:
  0.0 2.4 %first_gates.1 = (f32[2,2,64,128]{3,2,1,0:T(8,128)S(1)}, f32[2,64,128]{2,1,0:T(8,128)S(1)}, f32[2,64,128]{2,1,0:T(8,128)S(1)}, f32[4,8,128]{2,1,0:T(8,128)S(1)}, s32[8,128]{1,0:T(8,128)S(1)}) custom-call(s32[15]{0:T(128)} %order_hbm.1, f32[2,2,2]{2,1,0:T(2,128)} %gate_hbm.1, f32[512,128]{1,0:T(8,128)} %bitcast.10, f32[5,2,128,128]{3,2,1,0:T(8,128)} %gates_hbm.5), custom_call_target="tpu_custom_call" | custom-call | tf_op jit(solution)/shard_map/first_gates/pallas_call | solution.py:349
  2.4 4.1 %collective-permute-start = (f32[2,2,64,128]{3,2,1,0:T(8,128)S(1)}, f32[2,2,64,128]{3,2,1,0:T(8,128)S(1)}, u32[]{:S(2)}, u32[]{:S(2)}) collective-permute-start(f32[2,2,64,128]{3,2,1,0:T(8,128)S(1)} %get-tuple-element.16.near_own_ref.own_ref), channel_id=1, source_target_pairs={{0,16},{4,20},{8,24},{12,28},{16,0},{20,4},{24,8},{28,12},{1,17},{... | collective-permute-start | bytes 393224 | tf_op jit(solution)/shard_map/ppermute | solution.py:329
  6.5 1.5 %collective-permute-start.1 = (f32[2,64,128]{2,1,0:T(8,128)S(1)}, f32[2,64,128]{2,1,0:T(8,128)S(1)}, u32[]{:S(2)}, u32[]{:S(2)}) collective-permute-start(f32[2,64,128]{2,1,0:T(8,128)S(1)} %get-tuple-element.17), channel_id=1, source_target_pairs={{0,2},{1,3},{2,0},{3,1},{4,6},{5,7},{6,4},{7,5},{8,10},{9,11},{10,... | collective-permute-start | bytes 196616 | tf_op jit(solution)/shard_map/ppermute | solution.py:329
  8.0 1.4 %collective-permute-start.3 = (f32[2,64,128]{2,1,0:T(8,128)S(1)}, f32[2,64,128]{2,1,0:T(8,128)S(1)}, u32[]{:S(2)}, u32[]{:S(2)}) collective-permute-start(f32[2,64,128]{2,1,0:T(8,128)S(1)} %get-tuple-element.18), channel_id=1, source_target_pairs={{0,3},{1,2},{2,1},{3,0},{4,7},{5,6},{6,5},{7,4},{8,11},{9,10},{10,... | collective-permute-start | bytes 196616 | tf_op jit(solution)/shard_map/ppermute | solution.py:329
  9.4 1.2 %low_weights.1.low_gate_ref.matrix_ref = bf16[2,256,256]{2,1,0:T(8,128)(2,1)S(1)} custom-call(s32[8,128]{1,0:T(8,128)S(1)} %get-tuple-element.14.lanes_ref, f32[5,2,128,128]{3,2,1,0:T(8,128)} %gates_hbm.5), custom_call_target="tpu_custom_call" | custom-call | tf_op jit(solution)/shard_map/low_weights/pallas_call | solution.py:370
  10.6 0.1 collective-permute-done.1.refs_0_
  10.7 0.3 %collective-permute-start.2 = (f32[2,64,128]{2,1,0:T(8,128)S(1)}, f32[2,64,128]{2,1,0:T(8,128)S(1)}, u32[]{:S(2)}, u32[]{:S(2)}) collective-permute-start(f32[2,64,128]{2,1,0:T(8,128)S(1)} %collective-permute-done.1.refs_0_), channel_id=1, source_target_pairs={{0,16},{4,20},{8,24},{12,28},{16,0},{20,4},{24,8},{28,12},{1,17},{... | collective-permute-start | bytes 196616 | tf_op jit(solution)/shard_map/ppermute | solution.py:329
  11.1 2.1 %collective-permute-done.3.in_ref = f32[2,64,128]{2,1,0:T(8,128)S(1)} collective-permute-done((f32[2,64,128]{2,1,0:T(8,128)S(1)}, f32[2,64,128]{2,1,0:T(8,128)S(1)}, u32[]{:S(2)}, u32[]{:S(2)}) %collective-permute-start.3) | collective-permute-done | bytes 65568 | tf_op jit(solution)/shard_map/ppermute | solution.py:329
  13.2 0.2 low_gate.1.own_ref
  13.3 0.6 %collective-permute-start.4 = (f32[2,64,128]{2,1,0:T(8,128)S(1)}, f32[2,64,128]{2,1,0:T(8,128)S(1)}, u32[]{:S(2)}, u32[]{:S(2)}) collective-permute-start(f32[2,64,128]{2,1,0:T(8,128)S(1)} %low_gate.1.own_ref), channel_id=1, source_target_pairs={{0,16},{4,20},{8,24},{12,28},{16,0},{20,4},{24,8},{28,12},{1,17},{... | collective-permute-start | bytes 196616 | tf_op jit(solution)/shard_map/ppermute | solution.py:329
  13.9 0.0 collective-permute-done.near_other_ref.other_ref
  13.9 0.2 mix_pair.1
  14.1 1.6 %collective-permute-start.5 = (f32[2,64,128]{2,1,0:T(8,128)S(1)}, f32[2,64,128]{2,1,0:T(8,128)S(1)}, u32[]{:S(2)}, u32[]{:S(2)}) collective-permute-start(f32[2,64,128]{2,1,0:T(8,128)S(1)} %mix_pair.1), channel_id=1, source_target_pairs={{0,1},{1,0},{2,3},{3,2},{4,5},{5,4},{6,7},{7,6},{8,9},{9,8},{10,11... | collective-permute-start | bytes 196616 | tf_op jit(solution)/shard_map/ppermute | solution.py:329
  15.7 1.6 %high_weights.1 = (bf16[2,256,128]{2,1,0:T(8,128)(2,1)S(1)}, bf16[2,256,128]{2,1,0:T(8,128)(2,1)S(1)}) custom-call(f32[5,2,128,128]{3,2,1,0:T(8,128)} %gates_hbm.5), custom_call_target="tpu_custom_call" | custom-call | tf_op jit(solution)/shard_map/high_weights/pallas_call | solution.py:379
  17.3 0.6 %collective-permute-done.2.in_ref = f32[2,64,128]{2,1,0:T(8,128)S(1)} collective-permute-done((f32[2,64,128]{2,1,0:T(8,128)S(1)}, f32[2,64,128]{2,1,0:T(8,128)S(1)}, u32[]{:S(2)}, u32[]{:S(2)}) %collective-permute-start.2) | collective-permute-done | bytes 65568 | tf_op jit(solution)/shard_map/ppermute | solution.py:329
  17.9 0.5 %early_gate.1.early_ref = f32[256,256]{1,0:T(8,128)S(1)} custom-call(f32[4,8,128]{2,1,0:T(8,128)S(1)} %get-tuple-element.12.coefs_ref, bf16[2,256,256]{2,1,0:T(8,128)(2,1)S(1)} %low_weights.1.low_gate_ref.matrix_ref, bf16[2,256,128]{2,1,0:T(8,128)(2,1)S(1)} %get-tuple-element.15.high_gate_ref, f32[2,2,64,128]{3,2,1,0:T(8,128)S(1)} %get-tuple-element.16.near_own_ref.own_ref, ...), custom_call_target="tpu_custom_call" | custom-call | tf_op jit(solution)/shard_map/early_gate/pallas_call | solution.py:405
  18.4 0.3 %collective-permute-done.4.other_ref = f32[2,64,128]{2,1,0:T(8,128)S(1)} collective-permute-done((f32[2,64,128]{2,1,0:T(8,128)S(1)}, f32[2,64,128]{2,1,0:T(8,128)S(1)}, u32[]{:S(2)}, u32[]{:S(2)}) %collective-permute-start.4) | collective-permute-done | bytes 65568 | tf_op jit(solution)/shard_map/ppermute | solution.py:329
  18.7 0.0 collective-permute-done.5.refs_0_
  18.7 1.0 %last_gates.1 = f32[512,128]{1,0:T(8,128)} custom-call(f32[4,8,128]{2,1,0:T(8,128)S(1)} %get-tuple-element.12.coefs_ref, bf16[2,256,128]{2,1,0:T(8,128)(2,1)S(1)} %get-tuple-element.13.high_gate_ref, f32[256,256]{1,0:T(8,128)S(1)} %early_gate.1.early_ref, f32[2,64,128]{2,1,0:T(8,128)S(1)} %low_gate.1.own_ref, ...), custom_call_target="tpu_custom_call" | custom-call | tf_op jit(solution)/shard_map/last_gates/pallas_call | solution.py:413
  (1 shorter events, 0.0 us)
Async XLA Ops:
  2.4 11.6 %collective-permute-start = (f32[2,2,64,128]{3,2,1,0:T(8,128)S(1)}, f32[2,2,64,128]{3,2,1,0:T(8,128)S(1)}, u32[]{:S(2)}, u32[]{:S(2)}) collective-permute-start(f32[2,2,64,128]{3,2,1,0:T(8,128)S(1)} %get-tuple-element.16.near_own_ref.own_ref), channel_id=1, source_target_pairs={{0,16},{4,20},{8,24},{12,28},{16,0},{20,4},{24,8},{28,12},{1,17},{... | collective-permute-start | bytes 393224 | tf_op jit(solution)/shard_map/ppermute | solution.py:329
  6.5 4.3 %collective-permute-start.1 = (f32[2,64,128]{2,1,0:T(8,128)S(1)}, f32[2,64,128]{2,1,0:T(8,128)S(1)}, u32[]{:S(2)}, u32[]{:S(2)}) collective-permute-start(f32[2,64,128]{2,1,0:T(8,128)S(1)} %get-tuple-element.17), channel_id=1, source_target_pairs={{0,2},{1,3},{2,0},{3,1},{4,6},{5,7},{6,4},{7,5},{8,10},{9,11},{10,... | collective-permute-start | bytes 196616 | tf_op jit(solution)/shard_map/ppermute | solution.py:329
  8.0 5.2 %collective-permute-start.3 = (f32[2,64,128]{2,1,0:T(8,128)S(1)}, f32[2,64,128]{2,1,0:T(8,128)S(1)}, u32[]{:S(2)}, u32[]{:S(2)}) collective-permute-start(f32[2,64,128]{2,1,0:T(8,128)S(1)} %get-tuple-element.18), channel_id=1, source_target_pairs={{0,3},{1,2},{2,1},{3,0},{4,7},{5,6},{6,5},{7,4},{8,11},{9,10},{10,... | collective-permute-start | bytes 196616 | tf_op jit(solution)/shard_map/ppermute | solution.py:329
  10.7 7.1 %collective-permute-start.2 = (f32[2,64,128]{2,1,0:T(8,128)S(1)}, f32[2,64,128]{2,1,0:T(8,128)S(1)}, u32[]{:S(2)}, u32[]{:S(2)}) collective-permute-start(f32[2,64,128]{2,1,0:T(8,128)S(1)} %collective-permute-done.1.refs_0_), channel_id=1, source_target_pairs={{0,16},{4,20},{8,24},{12,28},{16,0},{20,4},{24,8},{28,12},{1,17},{... | collective-permute-start | bytes 196616 | tf_op jit(solution)/shard_map/ppermute | solution.py:329
  13.3 5.4 %collective-permute-start.4 = (f32[2,64,128]{2,1,0:T(8,128)S(1)}, f32[2,64,128]{2,1,0:T(8,128)S(1)}, u32[]{:S(2)}, u32[]{:S(2)}) collective-permute-start(f32[2,64,128]{2,1,0:T(8,128)S(1)} %low_gate.1.own_ref), channel_id=1, source_target_pairs={{0,16},{4,20},{8,24},{12,28},{16,0},{20,4},{24,8},{28,12},{1,17},{... | collective-permute-start | bytes 196616 | tf_op jit(solution)/shard_map/ppermute | solution.py:329
  14.1 4.6 %collective-permute-start.5 = (f32[2,64,128]{2,1,0:T(8,128)S(1)}, f32[2,64,128]{2,1,0:T(8,128)S(1)}, u32[]{:S(2)}, u32[]{:S(2)}) collective-permute-start(f32[2,64,128]{2,1,0:T(8,128)S(1)} %mix_pair.1), channel_id=1, source_target_pairs={{0,1},{1,0},{2,3},{3,2},{4,5},{5,4},{6,7},{7,6},{8,9},{9,8},{10,11... | collective-permute-start | bytes 196616 | tf_op jit(solution)/shard_map/ppermute | solution.py:329

commit v6 on v5

--- a/solution.py
+++ b/solution.py
@@ -85,6 +85,22 @@
     return crosses, wanted, slots, row_before, lane_before, new_in_lane
 
 
+def middle_high(plan):
+    crosses, wanted, slots, row_before = plan
+    place = jnp.int32(3)
+    for r in range(3):
+        place = jnp.where(row_before[r] == LANE_BITS, r, place)
+
+    def exchanged(values):
+        values = [jnp.int32(value) for value in values]
+        moved = values[3]
+        for r in range(3):
+            moved = jnp.where(place == r, values[r], moved)
+        return [jnp.where(place == r, values[3], values[r]) for r in range(3)] + [moved] + values[4:]
+
+    return *(exchanged(values) for values in (crosses, wanted, slots, row_before)), place
+
+
 def moved_bits(index, sources, targets):
     total = jnp.zeros_like(index)
     for source, target in zip(sources, targets, strict=True):
@@ -129,7 +145,7 @@
 
 def first_kernel(lo_bits, order_hbm, gate_hbm, x_hbm, gates_hbm, *refs):
     outs, (order_ref, gate_ref, x_ref, gates_ref, work, sems) = refs[:-6], refs[-6:]
-    outs, (coefs_out, lanes_out) = outs[:-2], outs[-2:]
+    outs, (coefs_out, orders_out) = outs[:-2], outs[-2:]
     parts = 1 << lo_bits
     fetches = [
         pltpu.make_async_copy(order_hbm, order_ref, sems.at[0]),
@@ -141,22 +157,59 @@
         fetch.start()
     fetches[0].wait()
     order = [order_ref[k] for k in range(LANE_BITS + ROW_BITS)]
-    crosses, wanted, slots, row_before, lane_before, new_in_lane = plan_of(order, lo_bits)
-    index = lax.broadcasted_iota(jnp.int32, (1, 2 * WIDTH), 1)
-    rows = one_hot(2 * WIDTH, moved_bits(index, row_before, range(ROW_BITS)))
+    *plan, lane_before, new_in_lane = plan_of(order, lo_bits)
+    folded = lo_bits + 3 < LANE_BITS
+    place = jnp.int32(3)
+    if folded:
+        *plan, place = middle_high(plan)
+    crosses, wanted, slots, row_before = plan
     lane = lax.broadcasted_iota(jnp.int32, (8, WIDTH), 1)
-    lanes_out[...] = moved_bits(lane, range(LANE_BITS), new_in_lane)
+    orders_out[0] = moved_bits(lane, range(LANE_BITS), new_in_lane)
+    turn = [jnp.where(place == r, 3, r) for r in range(3)] + [place] + [*range(4, LANE_BITS)]
+    orders_out[1] = moved_bits(lane, range(LANE_BITS), turn)
+    if folded:
+        middle = jnp.int32(0)
+        for r in range(ROW_BITS):
+            middle = jnp.where(row_before[r] == LANE_BITS, r, middle)
+        after_middle = [jnp.where(middle < r, 1, 0) for r in range(ROW_BITS)]
+        index = lax.broadcasted_iota(jnp.int32, (1, WIDTH), 1)
+        rows = one_hot(WIDTH, moved_bits(index, row_before, [r - after_middle[r] for r in range(ROW_BITS)]))
+        offsets = [jnp.int32(0)]
+        for r in range(3, ROW_BITS):
+            stride = jnp.where(middle == r, WIDTH, jnp.left_shift(1, r - after_middle[r]))
+            offsets += [offset + stride for offset in offsets]
+    else:
+        index = lax.broadcasted_iota(jnp.int32, (1, 2 * WIDTH), 1)
+        rows = one_hot(2 * WIDTH, moved_bits(index, row_before, range(ROW_BITS)))
     old_lane = moved_bits(lane, range(LANE_BITS), lane_before)
     fetches[1].wait()
+    fetches[2].wait()
+    fetches[3].wait()
     real, imag = halves(gates_ref[0, 0]), halves(gates_ref[0, 1])
+    if folded:
+        both = [dot(rows, jnp.concatenate([real[i], imag[i]], axis=1)).astype(BF16) for i in range(2)]
+        real, imag = [[half[:, c * WIDTH : (c + 1) * WIDTH] for half in both] for c in range(2)]
     matrix0 = [block_matrix(real[i], imag[i]) for i in range(2)]
     real, imag = halves(gates_ref[1, 0]), halves(gates_ref[1, 1])
     matrix1 = [block_matrix(real[i], imag[i]) for i in range(2)]
-    fetches[2].wait()
     pieces = [[x_ref[pl.ds(m * 2 + c, WIDTH, stride=4), :] for m in range(2)] for c in range(2)]
     state = jnp.concatenate([jnp.concatenate(row, axis=1) for row in pieces], axis=0)
     state = dot3(matrix0, halves(state))
-    state = [dot(rows, half).astype(BF16) for half in halves(turned(state))]
+    if folded:
+        for c in range(2):
+            for m in range(2):
+                work[c, m * WIDTH : (m + 1) * WIDTH] = state[c * WIDTH : (c + 1) * WIDTH, m * WIDTH : (m + 1) * WIDTH]
+        state = halves(
+            jnp.concatenate(
+                [
+                    jnp.concatenate([work[c, pl.ds(pl.multiple_of(offset, 8), 8), :] for offset in offsets], axis=0)
+                    for c in range(2)
+                ],
+                axis=1,
+            )
+        )
+    else:
+        state = [dot(rows, half).astype(BF16) for half in halves(turned(state))]
     state = dot3(state, matrix1, transposed=True)
     before, after = masks_of(lane, crosses[3:], wanted[3:]), masks_of(lane, crosses[3:], slots[3:])
     index = lanes_of(old_lane, crosses[3:], wanted[3:])
@@ -180,7 +233,6 @@
         source = pl.multiple_of(jnp.bitwise_xor(me, step) * count, 8)
         for c in range(2):
             out[c] = work[c, pl.ds(source, count), :]
-    fetches[3].wait()
     side = jnp.right_shift(lax.axis_index("hi"), lax.axis_size("hi").bit_length() - 2) & 1
     for other in range(2):
         for c in range(2):
@@ -216,17 +268,17 @@
     return [0, *range(near, parts - 1)], [*range(1, near), parts - 1]
 
 
-def low_weights_kernel(lanes_ref, gates_hbm, out_ref, gate_ref, sem):
+def low_weights_kernel(orders_ref, gates_hbm, out_ref, gate_ref, sem):
     fetch = pltpu.make_async_copy(gates_hbm.at[3], gate_ref, sem)
     fetch.start()
-    lanes = one_hot(WIDTH, lanes_ref[0:1])
+    lanes = one_hot(WIDTH, orders_ref[0, 0:1])
     fetch.wait()
     for i in range(2):
         real, imag = [dot(halves(gate_ref[c])[i], lanes).T for c in range(2)]
         out_ref[i] = block_matrix(real, -imag).astype(BF16)
 
 
-def high_weights_kernel(lo_bits, gates_hbm, early_ref, late_ref, gates_ref, sems):
+def high_weights_kernel(lo_bits, orders_ref, gates_hbm, early_ref, late_ref, gates_ref, sems):
     fetches = [pltpu.make_async_copy(gates_hbm.at[2 + 2 * g], gates_ref.at[g], sems.at[g]) for g in range(2)]
     for fetch in fetches:
         fetch.start()
@@ -234,7 +286,7 @@
     kept = WIDTH // parts
     me = lax.axis_index("lo")
     index = lax.broadcasted_iota(jnp.int32, (1, WIDTH), 1)
-    source = index % kept
+    source = orders_ref[1, 0:1] % kept
     early, late = arrival(parts)
     for place, step in enumerate(early + late):
         source = source + jnp.where(index // kept == place, jnp.bitwise_xor(me, step) * kept, 0)
@@ -346,11 +398,11 @@
     rows = amplitudes.reshape(2, 256, WIDTH).transpose(1, 0, 2).reshape(512, WIDTH)
     block = pltpu.VMEM((2, 2 * kept, WIDTH), F32)
     near = parts // 2
-    near_own, *far_own, coefs, lanes = pl.pallas_call(
+    near_own, *far_own, coefs, orders = pl.pallas_call(
         functools.partial(first_kernel, lo_bits),
         out_shape=[pltpu.VMEM((near, 2, 2 * kept, WIDTH), F32)]
         + [block] * (parts - near)
-        + [pltpu.VMEM((4, 8, WIDTH), F32), pltpu.VMEM((8, WIDTH), jnp.int32)],
+        + [pltpu.VMEM((4, 8, WIDTH), F32), pltpu.VMEM((2, 8, WIDTH), jnp.int32)],
         in_specs=[HBM] * 4,
         out_specs=[VMEM] * (parts - near + 3),
         scratch_shapes=[
@@ -375,16 +427,16 @@
         scratch_shapes=[pltpu.VMEM((2, WIDTH, WIDTH), F32), pltpu.SemaphoreType.DMA],
         compiler_params=PARAMS,
         name="low_weights",
-    )(lanes, in_hbm(gate_mats))
+    )(orders, in_hbm(gate_mats))
     early_weights, late_weights = pl.pallas_call(
         functools.partial(high_weights_kernel, lo_bits),
         out_shape=[pltpu.VMEM((2, 256, count), BF16) for count in counts],
-        in_specs=[HBM],
+        in_specs=[VMEM, HBM],
         out_specs=[VMEM] * 2,
         scratch_shapes=[pltpu.VMEM((2, 2, WIDTH, WIDTH), F32), pltpu.SemaphoreType.DMA((2,))],
         compiler_params=PARAMS,
         name="high_weights",
-    )(in_hbm(gate_mats))
+    )(orders, in_hbm(gate_mats))
     far_own[-1] = pl.pallas_call(
         low_kernel, out_shape=block, in_specs=[VMEM] * 2, out_specs=VMEM, compiler_params=PARAMS, name="low_gate"
     )(low_weights, far_own[-1])

time: 19.8 us -> 19.8 us (level)
  no operation moved by 1% of the time
where the time goes in v6:
time: 19.8 us; the launch traced here: 19.6 us
  starting transfers between devices  9.5 us (48%)
  Pallas kernels  6.99 us (35%)
  waiting for transfers between devices  3.08 us (16%)
    ppermute x6, starting transfers between devices, swapped(): return lax.ppermute(block, axis, [(i, i ^ distance) for i in range(count)])  9.5 us
    ppermute x6, waiting for transfers between devices, swapped(): return lax.ppermute(block, axis, [(i, i ^ distance) for i in range(count)])  3.08 us
    pallas_call x1, Pallas kernels, on_device(): pl.pallas_call(functools.partial(first_kernel, lo_bits), out_shape=[pltpu...  2.31 us
    pallas_call x1, Pallas kernels, on_device(): pl.pallas_call(functools.partial(high_weights_kernel, lo_bits), out_shape...  1.61 us
    pallas_call x1, Pallas kernels, on_device(): pl.pallas_call(low_weights_kernel, out_shape=pltpu.VMEM((2, 256, 256), BF...  1.21 us
    pallas_call x1, Pallas kernels, on_device(): pl.pallas_call(last_kernel, out_shape=jax.ShapeDtypeStruct((512, WIDTH),...  0.96 us
    pallas_call x1, Pallas kernels, on_device(): pl.pallas_call(early_kernel, out_shape=pltpu.VMEM((256, 256), F32), in_sp...  0.53 us
  transfers between devices with their start and end apart: 6, of which 4 were waited for; matrix products, arithmetic and copies ran while one was open for 0% of the time, Pallas kernels for 19%

profile of v6, /device:TPU:0, one launch (start us, length us, event | category | flops | bytes accessed | tf_op | source)
XLA Modules:
  0.0 19.6 jit_solution(10611909168458642630)
XLA Ops:
  0.0 2.3 %first_gates.1 = (f32[2,2,64,128]{3,2,1,0:T(8,128)S(1)}, f32[2,64,128]{2,1,0:T(8,128)S(1)}, f32[2,64,128]{2,1,0:T(8,128)S(1)}, f32[4,8,128]{2,1,0:T(8,128)S(1)}, s32[2,8,128]{2,1,0:T(8,128)S(1)}) custom-call(s32[15]{0:T(128)} %order_hbm.1, f32[2,2,2]{2,1,0:T(2,128)} %gate_hbm.1, f32[512,128]{1,0:T(8,128)} %bitcast.10, f32[5,2,128,128]{3,2,1,0:T(8,128)} %gates_hbm.5), custom_call_target="tpu_custom_call" | custom-call | tf_op jit(solution)/shard_map/first_gates/pallas_call | solution.py:401
  2.3 4.1 %collective-permute-start = (f32[2,2,64,128]{3,2,1,0:T(8,128)S(1)}, f32[2,2,64,128]{3,2,1,0:T(8,128)S(1)}, u32[]{:S(2)}, u32[]{:S(2)}) collective-permute-start(f32[2,2,64,128]{3,2,1,0:T(8,128)S(1)} %get-tuple-element.16.near_own_ref.own_ref), channel_id=1, source_target_pairs={{0,16},{4,20},{8,24},{12,28},{16,0},{20,4},{24,8},{28,12},{1,17},{... | collective-permute-start | bytes 393224 | tf_op jit(solution)/shard_map/ppermute | solution.py:381
  6.4 1.5 %collective-permute-start.1 = (f32[2,64,128]{2,1,0:T(8,128)S(1)}, f32[2,64,128]{2,1,0:T(8,128)S(1)}, u32[]{:S(2)}, u32[]{:S(2)}) collective-permute-start(f32[2,64,128]{2,1,0:T(8,128)S(1)} %get-tuple-element.17), channel_id=1, source_target_pairs={{0,2},{1,3},{2,0},{3,1},{4,6},{5,7},{6,4},{7,5},{8,10},{9,11},{10,... | collective-permute-start | bytes 196616 | tf_op jit(solution)/shard_map/ppermute | solution.py:381
  7.9 1.4 %collective-permute-start.3 = (f32[2,64,128]{2,1,0:T(8,128)S(1)}, f32[2,64,128]{2,1,0:T(8,128)S(1)}, u32[]{:S(2)}, u32[]{:S(2)}) collective-permute-start(f32[2,64,128]{2,1,0:T(8,128)S(1)} %get-tuple-element.18), channel_id=1, source_target_pairs={{0,3},{1,2},{2,1},{3,0},{4,7},{5,6},{6,5},{7,4},{8,11},{9,10},{10,... | collective-permute-start | bytes 196616 | tf_op jit(solution)/shard_map/ppermute | solution.py:381
  9.4 1.2 %low_weights.1.low_gate_ref.matrix_ref = bf16[2,256,256]{2,1,0:T(8,128)(2,1)S(1)} custom-call(s32[2,8,128]{2,1,0:T(8,128)S(1)} %get-tuple-element.13.orders_ref, f32[5,2,128,128]{3,2,1,0:T(8,128)} %gates_hbm.5), custom_call_target="tpu_custom_call" | custom-call | tf_op jit(solution)/shard_map/low_weights/pallas_call | solution.py:422
  10.6 0.1 collective-permute-done.1.refs_0_
  10.7 0.3 %collective-permute-start.2 = (f32[2,64,128]{2,1,0:T(8,128)S(1)}, f32[2,64,128]{2,1,0:T(8,128)S(1)}, u32[]{:S(2)}, u32[]{:S(2)}) collective-permute-start(f32[2,64,128]{2,1,0:T(8,128)S(1)} %collective-permute-done.1.refs_0_), channel_id=1, source_target_pairs={{0,16},{4,20},{8,24},{12,28},{16,0},{20,4},{24,8},{28,12},{1,17},{... | collective-permute-start | bytes 196616 | tf_op jit(solution)/shard_map/ppermute | solution.py:381
  11.0 2.1 %collective-permute-done.3.in_ref = f32[2,64,128]{2,1,0:T(8,128)S(1)} collective-permute-done((f32[2,64,128]{2,1,0:T(8,128)S(1)}, f32[2,64,128]{2,1,0:T(8,128)S(1)}, u32[]{:S(2)}, u32[]{:S(2)}) %collective-permute-start.3) | collective-permute-done | bytes 65568 | tf_op jit(solution)/shard_map/ppermute | solution.py:381
  13.1 0.2 low_gate.1.own_ref
  13.3 0.6 %collective-permute-start.4 = (f32[2,64,128]{2,1,0:T(8,128)S(1)}, f32[2,64,128]{2,1,0:T(8,128)S(1)}, u32[]{:S(2)}, u32[]{:S(2)}) collective-permute-start(f32[2,64,128]{2,1,0:T(8,128)S(1)} %low_gate.1.own_ref), channel_id=1, source_target_pairs={{0,16},{4,20},{8,24},{12,28},{16,0},{20,4},{24,8},{28,12},{1,17},{... | collective-permute-start | bytes 196616 | tf_op jit(solution)/shard_map/ppermute | solution.py:381
  13.9 0.0 collective-permute-done.near_other_ref.other_ref
  13.9 0.2 mix_pair.1
  14.1 1.6 %collective-permute-start.5 = (f32[2,64,128]{2,1,0:T(8,128)S(1)}, f32[2,64,128]{2,1,0:T(8,128)S(1)}, u32[]{:S(2)}, u32[]{:S(2)}) collective-permute-start(f32[2,64,128]{2,1,0:T(8,128)S(1)} %mix_pair.1), channel_id=1, source_target_pairs={{0,1},{1,0},{2,3},{3,2},{4,5},{5,4},{6,7},{7,6},{8,9},{9,8},{10,11... | collective-permute-start | bytes 196616 | tf_op jit(solution)/shard_map/ppermute | solution.py:381
  15.6 1.6 %high_weights.1 = (bf16[2,256,128]{2,1,0:T(8,128)(2,1)S(1)}, bf16[2,256,128]{2,1,0:T(8,128)(2,1)S(1)}) custom-call(s32[2,8,128]{2,1,0:T(8,128)S(1)} %get-tuple-element.13.orders_ref, f32[5,2,128,128]{3,2,1,0:T(8,128)} %gates_hbm.5), custom_call_target="tpu_custom_call" | custom-call | tf_op jit(solution)/shard_map/high_weights/pallas_call | solution.py:431
  17.2 0.6 %collective-permute-done.2.in_ref = f32[2,64,128]{2,1,0:T(8,128)S(1)} collective-permute-done((f32[2,64,128]{2,1,0:T(8,128)S(1)}, f32[2,64,128]{2,1,0:T(8,128)S(1)}, u32[]{:S(2)}, u32[]{:S(2)}) %collective-permute-start.2) | collective-permute-done | bytes 65568 | tf_op jit(solution)/shard_map/ppermute | solution.py:381
  17.8 0.5 %early_gate.1.early_ref = f32[256,256]{1,0:T(8,128)S(1)} custom-call(f32[4,8,128]{2,1,0:T(8,128)S(1)} %get-tuple-element.12.coefs_ref, bf16[2,256,256]{2,1,0:T(8,128)(2,1)S(1)} %low_weights.1.low_gate_ref.matrix_ref, bf16[2,256,128]{2,1,0:T(8,128)(2,1)S(1)} %get-tuple-element.15.high_gate_ref, f32[2,2,64,128]{3,2,1,0:T(8,128)S(1)} %get-tuple-element.16.near_own_ref.own_ref, ...), custom_call_target="tpu_custom_call" | custom-call | tf_op jit(solution)/shard_map/early_gate/pallas_call | solution.py:457
  18.4 0.3 %collective-permute-done.4.other_ref = f32[2,64,128]{2,1,0:T(8,128)S(1)} collective-permute-done((f32[2,64,128]{2,1,0:T(8,128)S(1)}, f32[2,64,128]{2,1,0:T(8,128)S(1)}, u32[]{:S(2)}, u32[]{:S(2)}) %collective-permute-start.4) | collective-permute-done | bytes 65568 | tf_op jit(solution)/shard_map/ppermute | solution.py:381
  18.7 0.0 collective-permute-done.5.refs_0_
  18.7 1.0 %last_gates.1 = f32[512,128]{1,0:T(8,128)} custom-call(f32[4,8,128]{2,1,0:T(8,128)S(1)} %get-tuple-element.12.coefs_ref, bf16[2,256,128]{2,1,0:T(8,128)(2,1)S(1)} %get-tuple-element.14.high_gate_ref, f32[256,256]{1,0:T(8,128)S(1)} %early_gate.1.early_ref, f32[2,64,128]{2,1,0:T(8,128)S(1)} %low_gate.1.own_ref, ...), custom_call_target="tpu_custom_call" | custom-call | tf_op jit(solution)/shard_map/last_gates/pallas_call | solution.py:465
  (1 shorter events, 0.0 us)
Async XLA Ops:
  2.3 11.6 %collective-permute-start = (f32[2,2,64,128]{3,2,1,0:T(8,128)S(1)}, f32[2,2,64,128]{3,2,1,0:T(8,128)S(1)}, u32[]{:S(2)}, u32[]{:S(2)}) collective-permute-start(f32[2,2,64,128]{3,2,1,0:T(8,128)S(1)} %get-tuple-element.16.near_own_ref.own_ref), channel_id=1, source_target_pairs={{0,16},{4,20},{8,24},{12,28},{16,0},{20,4},{24,8},{28,12},{1,17},{... | collective-permute-start | bytes 393224 | tf_op jit(solution)/shard_map/ppermute | solution.py:381
  6.4 4.3 %collective-permute-start.1 = (f32[2,64,128]{2,1,0:T(8,128)S(1)}, f32[2,64,128]{2,1,0:T(8,128)S(1)}, u32[]{:S(2)}, u32[]{:S(2)}) collective-permute-start(f32[2,64,128]{2,1,0:T(8,128)S(1)} %get-tuple-element.17), channel_id=1, source_target_pairs={{0,2},{1,3},{2,0},{3,1},{4,6},{5,7},{6,4},{7,5},{8,10},{9,11},{10,... | collective-permute-start | bytes 196616 | tf_op jit(solution)/shard_map/ppermute | solution.py:381
  7.9 5.2 %collective-permute-start.3 = (f32[2,64,128]{2,1,0:T(8,128)S(1)}, f32[2,64,128]{2,1,0:T(8,128)S(1)}, u32[]{:S(2)}, u32[]{:S(2)}) collective-permute-start(f32[2,64,128]{2,1,0:T(8,128)S(1)} %get-tuple-element.18), channel_id=1, source_target_pairs={{0,3},{1,2},{2,1},{3,0},{4,7},{5,6},{6,5},{7,4},{8,11},{9,10},{10,... | collective-permute-start | bytes 196616 | tf_op jit(solution)/shard_map/ppermute | solution.py:381
  10.7 7.1 %collective-permute-start.2 = (f32[2,64,128]{2,1,0:T(8,128)S(1)}, f32[2,64,128]{2,1,0:T(8,128)S(1)}, u32[]{:S(2)}, u32[]{:S(2)}) collective-permute-start(f32[2,64,128]{2,1,0:T(8,128)S(1)} %collective-permute-done.1.refs_0_), channel_id=1, source_target_pairs={{0,16},{4,20},{8,24},{12,28},{16,0},{20,4},{24,8},{28,12},{1,17},{... | collective-permute-start | bytes 196616 | tf_op jit(solution)/shard_map/ppermute | solution.py:381
  13.3 5.4 %collective-permute-start.4 = (f32[2,64,128]{2,1,0:T(8,128)S(1)}, f32[2,64,128]{2,1,0:T(8,128)S(1)}, u32[]{:S(2)}, u32[]{:S(2)}) collective-permute-start(f32[2,64,128]{2,1,0:T(8,128)S(1)} %low_gate.1.own_ref), channel_id=1, source_target_pairs={{0,16},{4,20},{8,24},{12,28},{16,0},{20,4},{24,8},{28,12},{1,17},{... | collective-permute-start | bytes 196616 | tf_op jit(solution)/shard_map/ppermute | solution.py:381
  14.1 4.6 %collective-permute-start.5 = (f32[2,64,128]{2,1,0:T(8,128)S(1)}, f32[2,64,128]{2,1,0:T(8,128)S(1)}, u32[]{:S(2)}, u32[]{:S(2)}) collective-permute-start(f32[2,64,128]{2,1,0:T(8,128)S(1)} %mix_pair.1), channel_id=1, source_target_pairs={{0,1},{1,0},{2,3},{3,2},{4,5},{5,4},{6,7},{7,6},{8,9},{9,8},{10,11... | collective-permute-start | bytes 196616 | tf_op jit(solution)/shard_map/ppermute | solution.py:381

commit v7 on v6

--- a/solution.py
+++ b/solution.py
@@ -143,15 +143,14 @@
     return [jnp.bitwise_xor(lane, offset) for offset in offsets]
 
 
-def first_kernel(lo_bits, order_hbm, gate_hbm, x_hbm, gates_hbm, *refs):
-    outs, (order_ref, gate_ref, x_ref, gates_ref, work, sems) = refs[:-6], refs[-6:]
-    outs, (coefs_out, orders_out) = outs[:-2], outs[-2:]
+def first_kernel(lo_bits, order_hbm, x_hbm, gates_hbm, *refs):
+    outs, (order_ref, x_ref, gates_ref, work, sems) = refs[:-5], refs[-5:]
+    outs, orders_out = outs[:-1], outs[-1]
     parts = 1 << lo_bits
     fetches = [
         pltpu.make_async_copy(order_hbm, order_ref, sems.at[0]),
         pltpu.make_async_copy(gates_hbm.at[pl.ds(0, 2)], gates_ref, sems.at[1]),
         pltpu.make_async_copy(x_hbm, x_ref, sems.at[2]),
-        pltpu.make_async_copy(gate_hbm, gate_ref, sems.at[3]),
     ]
     for fetch in fetches:
         fetch.start()
@@ -184,7 +183,6 @@
     old_lane = moved_bits(lane, range(LANE_BITS), lane_before)
     fetches[1].wait()
     fetches[2].wait()
-    fetches[3].wait()
     real, imag = halves(gates_ref[0, 0]), halves(gates_ref[0, 1])
     if folded:
         both = [dot(rows, jnp.concatenate([real[i], imag[i]], axis=1)).astype(BF16) for i in range(2)]
@@ -233,10 +231,6 @@
         source = pl.multiple_of(jnp.bitwise_xor(me, step) * count, 8)
         for c in range(2):
             out[c] = work[c, pl.ds(source, count), :]
-    side = jnp.right_shift(lax.axis_index("hi"), lax.axis_size("hi").bit_length() - 2) & 1
-    for other in range(2):
-        for c in range(2):
-            coefs_out[2 * other + c] = jnp.full((8, WIDTH), gate_ref[c, side, side ^ other])
 
 
 def turned(value):
@@ -268,13 +262,22 @@
     return [0, *range(near, parts - 1)], [*range(1, near), parts - 1]
 
 
-def low_weights_kernel(orders_ref, gates_hbm, out_ref, gate_ref, sem):
-    fetch = pltpu.make_async_copy(gates_hbm.at[3], gate_ref, sem)
-    fetch.start()
+def low_weights_kernel(orders_ref, gate_hbm, gates_hbm, out_ref, coefs_out, mats_ref, gate_ref, sems):
+    fetches = [
+        pltpu.make_async_copy(gates_hbm.at[3], mats_ref, sems.at[0]),
+        pltpu.make_async_copy(gate_hbm, gate_ref, sems.at[1]),
+    ]
+    for fetch in fetches:
+        fetch.start()
     lanes = one_hot(WIDTH, orders_ref[0, 0:1])
-    fetch.wait()
+    for fetch in fetches:
+        fetch.wait()
+    side = jnp.right_shift(lax.axis_index("hi"), lax.axis_size("hi").bit_length() - 2) & 1
+    for other in range(2):
+        for c in range(2):
+            coefs_out[2 * other + c] = jnp.full((8, WIDTH), gate_ref[c, side, side ^ other])
     for i in range(2):
-        real, imag = [dot(halves(gate_ref[c])[i], lanes).T for c in range(2)]
+        real, imag = [dot(halves(mats_ref[c])[i], lanes).T for c in range(2)]
         out_ref[i] = block_matrix(real, -imag).astype(BF16)
 
 
@@ -398,36 +401,35 @@
     rows = amplitudes.reshape(2, 256, WIDTH).transpose(1, 0, 2).reshape(512, WIDTH)
     block = pltpu.VMEM((2, 2 * kept, WIDTH), F32)
     near = parts // 2
-    near_own, *far_own, coefs, orders = pl.pallas_call(
+    near_own, *far_own, orders = pl.pallas_call(
         functools.partial(first_kernel, lo_bits),
         out_shape=[pltpu.VMEM((near, 2, 2 * kept, WIDTH), F32)]
         + [block] * (parts - near)
-        + [pltpu.VMEM((4, 8, WIDTH), F32), pltpu.VMEM((2, 8, WIDTH), jnp.int32)],
-        in_specs=[HBM] * 4,
-        out_specs=[VMEM] * (parts - near + 3),
+        + [pltpu.VMEM((2, 8, WIDTH), jnp.int32)],
+        in_specs=[HBM] * 3,
+        out_specs=[VMEM] * (parts - near + 2),
         scratch_shapes=[
             pltpu.SMEM((LANE_BITS + ROW_BITS,), jnp.int32),
-            pltpu.SMEM((2, 2, 2), F32),
             pltpu.VMEM((512, WIDTH), F32),
             pltpu.VMEM((2, 2, WIDTH, WIDTH), F32),
             pltpu.VMEM((2, 256, WIDTH), F32),
-            pltpu.SemaphoreType.DMA((4,)),
+            pltpu.SemaphoreType.DMA((3,)),
         ],
         compiler_params=PARAMS,
         name="first_gates",
-    )(in_hbm(qubit_order), in_hbm(dev_gate), in_hbm(rows), in_hbm(gate_mats))
+    )(in_hbm(qubit_order), in_hbm(rows), in_hbm(gate_mats))
     near_other = swapped(near_own, "hi", top)
     far_own = [swapped(far, "lo", near + i) for i, far in enumerate(far_own)]
     counts = [2 * kept * len(steps) for steps in arrival(parts)]
-    low_weights = pl.pallas_call(
+    low_weights, coefs = pl.pallas_call(
         low_weights_kernel,
-        out_shape=pltpu.VMEM((2, 256, 256), BF16),
-        in_specs=[VMEM, HBM],
-        out_specs=VMEM,
-        scratch_shapes=[pltpu.VMEM((2, WIDTH, WIDTH), F32), pltpu.SemaphoreType.DMA],
+        out_shape=[pltpu.VMEM((2, 256, 256), BF16), pltpu.VMEM((4, 8, WIDTH), F32)],
+        in_specs=[VMEM, HBM, HBM],
+        out_specs=[VMEM] * 2,
+        scratch_shapes=[pltpu.VMEM((2, WIDTH, WIDTH), F32), pltpu.SMEM((2, 2, 2), F32), pltpu.SemaphoreType.DMA((2,))],
         compiler_params=PARAMS,
         name="low_weights",
-    )(orders, in_hbm(gate_mats))
+    )(orders, in_hbm(dev_gate), in_hbm(gate_mats))
     early_weights, late_weights = pl.pallas_call(
         functools.partial(high_weights_kernel, lo_bits),
         out_shape=[pltpu.VMEM((2, 256, count), BF16) for count in counts],

time: 19.8 us -> 19.8 us (level)
  no operation moved by 1% of the time
where the time goes in v7:
time: 19.8 us; the launch traced here: 19.6 us
  starting transfers between devices  9.53 us (48%)
  Pallas kernels  7.01 us (35%)
  waiting for transfers between devices  3.03 us (15%)
    ppermute x6, starting transfers between devices, swapped(): return lax.ppermute(block, axis, [(i, i ^ distance) for i in range(count)])  9.53 us
    ppermute x6, waiting for transfers between devices, swapped(): return lax.ppermute(block, axis, [(i, i ^ distance) for i in range(count)])  3.03 us
    pallas_call x1, Pallas kernels, on_device(): pl.pallas_call(functools.partial(first_kernel, lo_bits), out_shape=[pltpu...  2.29 us
    pallas_call x1, Pallas kernels, on_device(): pl.pallas_call(functools.partial(high_weights_kernel, lo_bits), out_shape...  1.61 us
    pallas_call x1, Pallas kernels, on_device(): pl.pallas_call(low_weights_kernel, out_shape=[pltpu.VMEM((2, 256, 256), B...  1.23 us
    pallas_call x1, Pallas kernels, on_device(): pl.pallas_call(last_kernel, out_shape=jax.ShapeDtypeStruct((512, WIDTH),...  0.97 us
    pallas_call x1, Pallas kernels, on_device(): pl.pallas_call(early_kernel, out_shape=pltpu.VMEM((256, 256), F32), in_sp...  0.53 us
  transfers between devices with their start and end apart: 6, of which 4 were waited for; matrix products, arithmetic and copies ran while one was open for 0% of the time, Pallas kernels for 19%

profile of v7, /device:TPU:0, one launch (start us, length us, event | category | flops | bytes accessed | tf_op | source)
XLA Modules:
  0.0 19.6 jit_solution(18333482853768282886)
XLA Ops:
  0.0 2.3 %first_gates.1 = (f32[2,2,64,128]{3,2,1,0:T(8,128)S(1)}, f32[2,64,128]{2,1,0:T(8,128)S(1)}, f32[2,64,128]{2,1,0:T(8,128)S(1)}, s32[2,8,128]{2,1,0:T(8,128)S(1)}) custom-call(s32[15]{0:T(128)} %order_hbm.1, f32[512,128]{1,0:T(8,128)} %bitcast.10, f32[5,2,128,128]{3,2,1,0:T(8,128)} %gates_hbm.5), custom_call_target="tpu_custom_call" | custom-call | tf_op jit(solution)/shard_map/first_gates/pallas_call | solution.py:404
  2.3 4.1 %collective-permute-start = (f32[2,2,64,128]{3,2,1,0:T(8,128)S(1)}, f32[2,2,64,128]{3,2,1,0:T(8,128)S(1)}, u32[]{:S(2)}, u32[]{:S(2)}) collective-permute-start(f32[2,2,64,128]{3,2,1,0:T(8,128)S(1)} %get-tuple-element.18.near_own_ref.own_ref), channel_id=1, source_target_pairs={{0,16},{4,20},{8,24},{12,28},{16,0},{20,4},{24,8},{28,12},{1,17},{... | collective-permute-start | bytes 393224 | tf_op jit(solution)/shard_map/ppermute | solution.py:384
  6.4 1.5 %collective-permute-start.1 = (f32[2,64,128]{2,1,0:T(8,128)S(1)}, f32[2,64,128]{2,1,0:T(8,128)S(1)}, u32[]{:S(2)}, u32[]{:S(2)}) collective-permute-start(f32[2,64,128]{2,1,0:T(8,128)S(1)} %get-tuple-element.19), channel_id=1, source_target_pairs={{0,2},{1,3},{2,0},{3,1},{4,6},{5,7},{6,4},{7,5},{8,10},{9,11},{10,... | collective-permute-start | bytes 196616 | tf_op jit(solution)/shard_map/ppermute | solution.py:384
  7.9 1.4 %collective-permute-start.3 = (f32[2,64,128]{2,1,0:T(8,128)S(1)}, f32[2,64,128]{2,1,0:T(8,128)S(1)}, u32[]{:S(2)}, u32[]{:S(2)}) collective-permute-start(f32[2,64,128]{2,1,0:T(8,128)S(1)} %get-tuple-element.20), channel_id=1, source_target_pairs={{0,3},{1,2},{2,1},{3,0},{4,7},{5,6},{6,5},{7,4},{8,11},{9,10},{10,... | collective-permute-start | bytes 196616 | tf_op jit(solution)/shard_map/ppermute | solution.py:384
  9.4 1.2 %low_weights.1 = (bf16[2,256,256]{2,1,0:T(8,128)(2,1)S(1)}, f32[4,8,128]{2,1,0:T(8,128)S(1)}) custom-call(s32[2,8,128]{2,1,0:T(8,128)S(1)} %get-tuple-element.13.orders_ref, f32[2,2,2]{2,1,0:T(2,128)} %gate_hbm.1, f32[5,2,128,128]{3,2,1,0:T(8,128)} %gates_hbm.5), custom_call_target="tpu_custom_call" | custom-call | tf_op jit(solution)/shard_map/low_weights/pallas_call | solution.py:424
  10.6 0.1 collective-permute-done.1.refs_0_
  10.7 0.3 %collective-permute-start.2 = (f32[2,64,128]{2,1,0:T(8,128)S(1)}, f32[2,64,128]{2,1,0:T(8,128)S(1)}, u32[]{:S(2)}, u32[]{:S(2)}) collective-permute-start(f32[2,64,128]{2,1,0:T(8,128)S(1)} %collective-permute-done.1.refs_0_), channel_id=1, source_target_pairs={{0,16},{4,20},{8,24},{12,28},{16,0},{20,4},{24,8},{28,12},{1,17},{... | collective-permute-start | bytes 196616 | tf_op jit(solution)/shard_map/ppermute | solution.py:384
  11.0 2.1 %collective-permute-done.3.in_ref = f32[2,64,128]{2,1,0:T(8,128)S(1)} collective-permute-done((f32[2,64,128]{2,1,0:T(8,128)S(1)}, f32[2,64,128]{2,1,0:T(8,128)S(1)}, u32[]{:S(2)}, u32[]{:S(2)}) %collective-permute-start.3) | collective-permute-done | bytes 65568 | tf_op jit(solution)/shard_map/ppermute | solution.py:384
  13.1 0.2 low_gate.1.own_ref
  13.3 0.6 %collective-permute-start.4 = (f32[2,64,128]{2,1,0:T(8,128)S(1)}, f32[2,64,128]{2,1,0:T(8,128)S(1)}, u32[]{:S(2)}, u32[]{:S(2)}) collective-permute-start(f32[2,64,128]{2,1,0:T(8,128)S(1)} %low_gate.1.own_ref), channel_id=1, source_target_pairs={{0,16},{4,20},{8,24},{12,28},{16,0},{20,4},{24,8},{28,12},{1,17},{... | collective-permute-start | bytes 196616 | tf_op jit(solution)/shard_map/ppermute | solution.py:384
  13.9 0.0 collective-permute-done.near_other_ref.other_ref
  13.9 0.2 mix_pair.1
  14.0 1.6 %collective-permute-start.5 = (f32[2,64,128]{2,1,0:T(8,128)S(1)}, f32[2,64,128]{2,1,0:T(8,128)S(1)}, u32[]{:S(2)}, u32[]{:S(2)}) collective-permute-start(f32[2,64,128]{2,1,0:T(8,128)S(1)} %mix_pair.1), channel_id=1, source_target_pairs={{0,1},{1,0},{2,3},{3,2},{4,5},{5,4},{6,7},{7,6},{8,9},{9,8},{10,11... | collective-permute-start | bytes 196616 | tf_op jit(solution)/shard_map/ppermute | solution.py:384
  15.6 1.6 %high_weights.1 = (bf16[2,256,128]{2,1,0:T(8,128)(2,1)S(1)}, bf16[2,256,128]{2,1,0:T(8,128)(2,1)S(1)}) custom-call(s32[2,8,128]{2,1,0:T(8,128)S(1)} %get-tuple-element.13.orders_ref, f32[5,2,128,128]{3,2,1,0:T(8,128)} %gates_hbm.5), custom_call_target="tpu_custom_call" | custom-call | tf_op jit(solution)/shard_map/high_weights/pallas_call | solution.py:433
  17.2 0.6 %collective-permute-done.2.in_ref = f32[2,64,128]{2,1,0:T(8,128)S(1)} collective-permute-done((f32[2,64,128]{2,1,0:T(8,128)S(1)}, f32[2,64,128]{2,1,0:T(8,128)S(1)}, u32[]{:S(2)}, u32[]{:S(2)}) %collective-permute-start.2) | collective-permute-done | bytes 65568 | tf_op jit(solution)/shard_map/ppermute | solution.py:384
  17.8 0.5 %early_gate.1.early_ref = f32[256,256]{1,0:T(8,128)S(1)} custom-call(f32[4,8,128]{2,1,0:T(8,128)S(1)} %get-tuple-element.14.coefs_ref, bf16[2,256,256]{2,1,0:T(8,128)(2,1)S(1)} %get-tuple-element.16.low_gate_ref.matrix_ref, bf16[2,256,128]{2,1,0:T(8,128)(2,1)S(1)} %get-tuple-element.17.high_gate_ref, ...), custom_call_target="tpu_custom_call" | custom-call | tf_op jit(solution)/shard_map/early_gate/pallas_call | solution.py:459
  18.4 0.3 %collective-permute-done.4.other_ref = f32[2,64,128]{2,1,0:T(8,128)S(1)} collective-permute-done((f32[2,64,128]{2,1,0:T(8,128)S(1)}, f32[2,64,128]{2,1,0:T(8,128)S(1)}, u32[]{:S(2)}, u32[]{:S(2)}) %collective-permute-start.4) | collective-permute-done | bytes 65568 | tf_op jit(solution)/shard_map/ppermute | solution.py:384
  18.6 0.0 collective-permute-done.5.refs_0_
  18.6 1.0 %last_gates.1 = f32[512,128]{1,0:T(8,128)} custom-call(f32[4,8,128]{2,1,0:T(8,128)S(1)} %get-tuple-element.14.coefs_ref, bf16[2,256,128]{2,1,0:T(8,128)(2,1)S(1)} %get-tuple-element.15.high_gate_ref, f32[256,256]{1,0:T(8,128)S(1)} %early_gate.1.early_ref, f32[2,64,128]{2,1,0:T(8,128)S(1)} %low_gate.1.own_ref, ...), custom_call_target="tpu_custom_call" | custom-call | tf_op jit(solution)/shard_map/last_gates/pallas_call | solution.py:467
  (1 shorter events, 0.0 us)
Async XLA Ops:
  2.3 11.6 %collective-permute-start = (f32[2,2,64,128]{3,2,1,0:T(8,128)S(1)}, f32[2,2,64,128]{3,2,1,0:T(8,128)S(1)}, u32[]{:S(2)}, u32[]{:S(2)}) collective-permute-start(f32[2,2,64,128]{3,2,1,0:T(8,128)S(1)} %get-tuple-element.18.near_own_ref.own_ref), channel_id=1, source_target_pairs={{0,16},{4,20},{8,24},{12,28},{16,0},{20,4},{24,8},{28,12},{1,17},{... | collective-permute-start | bytes 393224 | tf_op jit(solution)/shard_map/ppermute | solution.py:384
  6.4 4.3 %collective-permute-start.1 = (f32[2,64,128]{2,1,0:T(8,128)S(1)}, f32[2,64,128]{2,1,0:T(8,128)S(1)}, u32[]{:S(2)}, u32[]{:S(2)}) collective-permute-start(f32[2,64,128]{2,1,0:T(8,128)S(1)} %get-tuple-element.19), channel_id=1, source_target_pairs={{0,2},{1,3},{2,0},{3,1},{4,6},{5,7},{6,4},{7,5},{8,10},{9,11},{10,... | collective-permute-start | bytes 196616 | tf_op jit(solution)/shard_map/ppermute | solution.py:384
  7.9 5.2 %collective-permute-start.3 = (f32[2,64,128]{2,1,0:T(8,128)S(1)}, f32[2,64,128]{2,1,0:T(8,128)S(1)}, u32[]{:S(2)}, u32[]{:S(2)}) collective-permute-start(f32[2,64,128]{2,1,0:T(8,128)S(1)} %get-tuple-element.20), channel_id=1, source_target_pairs={{0,3},{1,2},{2,1},{3,0},{4,7},{5,6},{6,5},{7,4},{8,11},{9,10},{10,... | collective-permute-start | bytes 196616 | tf_op jit(solution)/shard_map/ppermute | solution.py:384
  10.7 7.1 %collective-permute-start.2 = (f32[2,64,128]{2,1,0:T(8,128)S(1)}, f32[2,64,128]{2,1,0:T(8,128)S(1)}, u32[]{:S(2)}, u32[]{:S(2)}) collective-permute-start(f32[2,64,128]{2,1,0:T(8,128)S(1)} %collective-permute-done.1.refs_0_), channel_id=1, source_target_pairs={{0,16},{4,20},{8,24},{12,28},{16,0},{20,4},{24,8},{28,12},{1,17},{... | collective-permute-start | bytes 196616 | tf_op jit(solution)/shard_map/ppermute | solution.py:384
  13.3 5.4 %collective-permute-start.4 = (f32[2,64,128]{2,1,0:T(8,128)S(1)}, f32[2,64,128]{2,1,0:T(8,128)S(1)}, u32[]{:S(2)}, u32[]{:S(2)}) collective-permute-start(f32[2,64,128]{2,1,0:T(8,128)S(1)} %low_gate.1.own_ref), channel_id=1, source_target_pairs={{0,16},{4,20},{8,24},{12,28},{16,0},{20,4},{24,8},{28,12},{1,17},{... | collective-permute-start | bytes 196616 | tf_op jit(solution)/shard_map/ppermute | solution.py:384
  14.0 4.6 %collective-permute-start.5 = (f32[2,64,128]{2,1,0:T(8,128)S(1)}, f32[2,64,128]{2,1,0:T(8,128)S(1)}, u32[]{:S(2)}, u32[]{:S(2)}) collective-permute-start(f32[2,64,128]{2,1,0:T(8,128)S(1)} %mix_pair.1), channel_id=1, source_target_pairs={{0,1},{1,0},{2,3},{3,2},{4,5},{5,4},{6,7},{7,6},{8,9},{9,8},{10,11... | collective-permute-start | bytes 196616 | tf_op jit(solution)/shard_map/ppermute | solution.py:384

commit v8 on v7

--- a/solution.py
+++ b/solution.py
@@ -126,6 +126,8 @@
 
     butterfly(before)
     for i, lanes in enumerate(index):
+        if lanes is None:
+            continue
         values[i] = jnp.take_along_axis(values[i], lanes, axis=1, mode="promise_in_bounds")
     butterfly(after)
     return values
@@ -216,7 +218,7 @@
         for v, value in enumerate(crossed(values, before, after, index)):
             work[c, pl.ds(8 * v, 8), :] = value
     masks = masks_of(lane, crosses[:3], slots[:3])
-    index = lanes_of(lane, crosses[:3], slots[:3])
+    index = [None] + lanes_of(lane, crosses[:3], slots[:3])[1:]
     for c in range(2):
         for group in range(4):
             places = [pl.ds(group * 64 + o, 8, stride=8) for o in range(8)]
@@ -355,8 +357,8 @@
     high, low = halves(for_high(values))
     state = jnp.concatenate([low, high, high], axis=0)
     sends = []
-    half = WIDTH // 2
-    for i in range(2):
+    half = WIDTH // 4
+    for i in range(4):
         matrix = [
             jnp.concatenate(
                 [high_gate_ref[j, c * WIDTH + i * half : c * WIDTH + (i + 1) * half] for c in range(2)], axis=0
@@ -367,12 +369,12 @@
         for c in range(2):
             for m in range(2):
                 at = c * WIDTH + i * half
-                out_ref[pl.ds(i * 256 + m * 2 + c, half, stride=4), :] = (
+                out_ref[pl.ds(i * 128 + m * 2 + c, half, stride=4), :] = (
                     early_ref[at : at + half, m * WIDTH : (m + 1) * WIDTH]
                     + result[c * half : (c + 1) * half, m * WIDTH : (m + 1) * WIDTH]
                 )
         sends.append(
-            pltpu.make_async_copy(out_ref.at[pl.ds(i * 256, 256)], out_hbm.at[pl.ds(i * 256, 256)], sems.at[i])
+            pltpu.make_async_copy(out_ref.at[pl.ds(i * 128, 128)], out_hbm.at[pl.ds(i * 128, 128)], sems.at[i])
         )
         sends[-1].start()
     for send in sends:
@@ -469,7 +471,7 @@
         out_shape=jax.ShapeDtypeStruct((512, WIDTH), F32),
         in_specs=[VMEM] * (5 + len(mixes)),
         out_specs=HBM,
-        scratch_shapes=[pltpu.VMEM((512, WIDTH), F32), pltpu.SemaphoreType.DMA((2,))],
+        scratch_shapes=[pltpu.VMEM((512, WIDTH), F32), pltpu.SemaphoreType.DMA((4,))],
         compiler_params=PARAMS,
         name="last_gates",
     )(coefs, late_weights, early, far_own[-1], far_other[-1], *mixes)

time: 19.8 us -> 19.8 us (level)
  no operation moved by 1% of the time
where the time goes in v8:
time: 19.8 us; the launch traced here: 19.6 us
  starting transfers between devices  9.53 us (48%)
  Pallas kernels  6.98 us (35%)
  waiting for transfers between devices  3.03 us (15%)
    ppermute x6, starting transfers between devices, swapped(): return lax.ppermute(block, axis, [(i, i ^ distance) for i in range(count)])  9.53 us
    ppermute x6, waiting for transfers between devices, swapped(): return lax.ppermute(block, axis, [(i, i ^ distance) for i in range(count)])  3.03 us
    pallas_call x1, Pallas kernels, on_device(): pl.pallas_call(functools.partial(first_kernel, lo_bits), out_shape=[pltpu...  2.26 us
    pallas_call x1, Pallas kernels, on_device(): pl.pallas_call(functools.partial(high_weights_kernel, lo_bits), out_shape...  1.61 us
    pallas_call x1, Pallas kernels, on_device(): pl.pallas_call(low_weights_kernel, out_shape=[pltpu.VMEM((2, 256, 256), B...  1.23 us
    pallas_call x1, Pallas kernels, on_device(): pl.pallas_call(last_kernel, out_shape=jax.ShapeDtypeStruct((512, WIDTH),...  0.97 us
    pallas_call x1, Pallas kernels, on_device(): pl.pallas_call(early_kernel, out_shape=pltpu.VMEM((256, 256), F32), in_sp...  0.53 us
  transfers between devices with their start and end apart: 6, of which 4 were waited for; matrix products, arithmetic and copies ran while one was open for 0% of the time, Pallas kernels for 19%

profile of v8, /device:TPU:0, one launch (start us, length us, event | category | flops | bytes accessed | tf_op | source)
XLA Modules:
  0.0 19.6 jit_solution(3231077793825602743)
XLA Ops:
  0.0 2.3 %first_gates.1 = (f32[2,2,64,128]{3,2,1,0:T(8,128)S(1)}, f32[2,64,128]{2,1,0:T(8,128)S(1)}, f32[2,64,128]{2,1,0:T(8,128)S(1)}, s32[2,8,128]{2,1,0:T(8,128)S(1)}) custom-call(s32[15]{0:T(128)} %order_hbm.1, f32[512,128]{1,0:T(8,128)} %bitcast.10, f32[5,2,128,128]{3,2,1,0:T(8,128)} %gates_hbm.5), custom_call_target="tpu_custom_call" | custom-call | tf_op jit(solution)/shard_map/first_gates/pallas_call | solution.py:406
  2.3 4.1 %collective-permute-start = (f32[2,2,64,128]{3,2,1,0:T(8,128)S(1)}, f32[2,2,64,128]{3,2,1,0:T(8,128)S(1)}, u32[]{:S(2)}, u32[]{:S(2)}) collective-permute-start(f32[2,2,64,128]{3,2,1,0:T(8,128)S(1)} %get-tuple-element.18.near_own_ref.own_ref), channel_id=1, source_target_pairs={{0,16},{4,20},{8,24},{12,28},{16,0},{20,4},{24,8},{28,12},{1,17},{... | collective-permute-start | bytes 393224 | tf_op jit(solution)/shard_map/ppermute | solution.py:386
  6.4 1.5 %collective-permute-start.1 = (f32[2,64,128]{2,1,0:T(8,128)S(1)}, f32[2,64,128]{2,1,0:T(8,128)S(1)}, u32[]{:S(2)}, u32[]{:S(2)}) collective-permute-start(f32[2,64,128]{2,1,0:T(8,128)S(1)} %get-tuple-element.19), channel_id=1, source_target_pairs={{0,2},{1,3},{2,0},{3,1},{4,6},{5,7},{6,4},{7,5},{8,10},{9,11},{10,... | collective-permute-start | bytes 196616 | tf_op jit(solution)/shard_map/ppermute | solution.py:386
  7.9 1.4 %collective-permute-start.3 = (f32[2,64,128]{2,1,0:T(8,128)S(1)}, f32[2,64,128]{2,1,0:T(8,128)S(1)}, u32[]{:S(2)}, u32[]{:S(2)}) collective-permute-start(f32[2,64,128]{2,1,0:T(8,128)S(1)} %get-tuple-element.20), channel_id=1, source_target_pairs={{0,3},{1,2},{2,1},{3,0},{4,7},{5,6},{6,5},{7,4},{8,11},{9,10},{10,... | collective-permute-start | bytes 196616 | tf_op jit(solution)/shard_map/ppermute | solution.py:386
  9.3 1.2 %low_weights.1 = (bf16[2,256,256]{2,1,0:T(8,128)(2,1)S(1)}, f32[4,8,128]{2,1,0:T(8,128)S(1)}) custom-call(s32[2,8,128]{2,1,0:T(8,128)S(1)} %get-tuple-element.13.orders_ref, f32[2,2,2]{2,1,0:T(2,128)} %gate_hbm.1, f32[5,2,128,128]{3,2,1,0:T(8,128)} %gates_hbm.5), custom_call_target="tpu_custom_call" | custom-call | tf_op jit(solution)/shard_map/low_weights/pallas_call | solution.py:426
  10.6 0.1 collective-permute-done.1.refs_0_
  10.6 0.3 %collective-permute-start.2 = (f32[2,64,128]{2,1,0:T(8,128)S(1)}, f32[2,64,128]{2,1,0:T(8,128)S(1)}, u32[]{:S(2)}, u32[]{:S(2)}) collective-permute-start(f32[2,64,128]{2,1,0:T(8,128)S(1)} %collective-permute-done.1.refs_0_), channel_id=1, source_target_pairs={{0,16},{4,20},{8,24},{12,28},{16,0},{20,4},{24,8},{28,12},{1,17},{... | collective-permute-start | bytes 196616 | tf_op jit(solution)/shard_map/ppermute | solution.py:386
  11.0 2.1 %collective-permute-done.3.in_ref = f32[2,64,128]{2,1,0:T(8,128)S(1)} collective-permute-done((f32[2,64,128]{2,1,0:T(8,128)S(1)}, f32[2,64,128]{2,1,0:T(8,128)S(1)}, u32[]{:S(2)}, u32[]{:S(2)}) %collective-permute-start.3) | collective-permute-done | bytes 65568 | tf_op jit(solution)/shard_map/ppermute | solution.py:386
  13.1 0.2 low_gate.1.own_ref
  13.2 0.6 %collective-permute-start.4 = (f32[2,64,128]{2,1,0:T(8,128)S(1)}, f32[2,64,128]{2,1,0:T(8,128)S(1)}, u32[]{:S(2)}, u32[]{:S(2)}) collective-permute-start(f32[2,64,128]{2,1,0:T(8,128)S(1)} %low_gate.1.own_ref), channel_id=1, source_target_pairs={{0,16},{4,20},{8,24},{12,28},{16,0},{20,4},{24,8},{28,12},{1,17},{... | collective-permute-start | bytes 196616 | tf_op jit(solution)/shard_map/ppermute | solution.py:386
  13.8 0.0 collective-permute-done.near_other_ref.other_ref
  13.8 0.2 mix_pair.1
  14.0 1.6 %collective-permute-start.5 = (f32[2,64,128]{2,1,0:T(8,128)S(1)}, f32[2,64,128]{2,1,0:T(8,128)S(1)}, u32[]{:S(2)}, u32[]{:S(2)}) collective-permute-start(f32[2,64,128]{2,1,0:T(8,128)S(1)} %mix_pair.1), channel_id=1, source_target_pairs={{0,1},{1,0},{2,3},{3,2},{4,5},{5,4},{6,7},{7,6},{8,9},{9,8},{10,11... | collective-permute-start | bytes 196616 | tf_op jit(solution)/shard_map/ppermute | solution.py:386
  15.6 1.6 %high_weights.1 = (bf16[2,256,128]{2,1,0:T(8,128)(2,1)S(1)}, bf16[2,256,128]{2,1,0:T(8,128)(2,1)S(1)}) custom-call(s32[2,8,128]{2,1,0:T(8,128)S(1)} %get-tuple-element.13.orders_ref, f32[5,2,128,128]{3,2,1,0:T(8,128)} %gates_hbm.5), custom_call_target="tpu_custom_call" | custom-call | tf_op jit(solution)/shard_map/high_weights/pallas_call | solution.py:435
  17.2 0.6 %collective-permute-done.2.in_ref = f32[2,64,128]{2,1,0:T(8,128)S(1)} collective-permute-done((f32[2,64,128]{2,1,0:T(8,128)S(1)}, f32[2,64,128]{2,1,0:T(8,128)S(1)}, u32[]{:S(2)}, u32[]{:S(2)}) %collective-permute-start.2) | collective-permute-done | bytes 65568 | tf_op jit(solution)/shard_map/ppermute | solution.py:386
  17.8 0.5 %early_gate.1.early_ref = f32[256,256]{1,0:T(8,128)S(1)} custom-call(f32[4,8,128]{2,1,0:T(8,128)S(1)} %get-tuple-element.14.coefs_ref, bf16[2,256,256]{2,1,0:T(8,128)(2,1)S(1)} %get-tuple-element.16.low_gate_ref.matrix_ref, bf16[2,256,128]{2,1,0:T(8,128)(2,1)S(1)} %get-tuple-element.17.high_gate_ref, ...), custom_call_target="tpu_custom_call" | custom-call | tf_op jit(solution)/shard_map/early_gate/pallas_call | solution.py:461
  18.3 0.3 %collective-permute-done.4.other_ref = f32[2,64,128]{2,1,0:T(8,128)S(1)} collective-permute-done((f32[2,64,128]{2,1,0:T(8,128)S(1)}, f32[2,64,128]{2,1,0:T(8,128)S(1)}, u32[]{:S(2)}, u32[]{:S(2)}) %collective-permute-start.4) | collective-permute-done | bytes 65568 | tf_op jit(solution)/shard_map/ppermute | solution.py:386
  18.6 0.0 collective-permute-done.5.refs_0_
  18.6 1.0 %last_gates.1 = f32[512,128]{1,0:T(8,128)} custom-call(f32[4,8,128]{2,1,0:T(8,128)S(1)} %get-tuple-element.14.coefs_ref, bf16[2,256,128]{2,1,0:T(8,128)(2,1)S(1)} %get-tuple-element.15.high_gate_ref, f32[256,256]{1,0:T(8,128)S(1)} %early_gate.1.early_ref, f32[2,64,128]{2,1,0:T(8,128)S(1)} %low_gate.1.own_ref, ...), custom_call_target="tpu_custom_call" | custom-call | tf_op jit(solution)/shard_map/last_gates/pallas_call | solution.py:469
  (1 shorter events, 0.0 us)
Async XLA Ops:
  2.3 11.6 %collective-permute-start = (f32[2,2,64,128]{3,2,1,0:T(8,128)S(1)}, f32[2,2,64,128]{3,2,1,0:T(8,128)S(1)}, u32[]{:S(2)}, u32[]{:S(2)}) collective-permute-start(f32[2,2,64,128]{3,2,1,0:T(8,128)S(1)} %get-tuple-element.18.near_own_ref.own_ref), channel_id=1, source_target_pairs={{0,16},{4,20},{8,24},{12,28},{16,0},{20,4},{24,8},{28,12},{1,17},{... | collective-permute-start | bytes 393224 | tf_op jit(solution)/shard_map/ppermute | solution.py:386
  6.4 4.3 %collective-permute-start.1 = (f32[2,64,128]{2,1,0:T(8,128)S(1)}, f32[2,64,128]{2,1,0:T(8,128)S(1)}, u32[]{:S(2)}, u32[]{:S(2)}) collective-permute-start(f32[2,64,128]{2,1,0:T(8,128)S(1)} %get-tuple-element.19), channel_id=1, source_target_pairs={{0,2},{1,3},{2,0},{3,1},{4,6},{5,7},{6,4},{7,5},{8,10},{9,11},{10,... | collective-permute-start | bytes 196616 | tf_op jit(solution)/shard_map/ppermute | solution.py:386
  7.9 5.2 %collective-permute-start.3 = (f32[2,64,128]{2,1,0:T(8,128)S(1)}, f32[2,64,128]{2,1,0:T(8,128)S(1)}, u32[]{:S(2)}, u32[]{:S(2)}) collective-permute-start(f32[2,64,128]{2,1,0:T(8,128)S(1)} %get-tuple-element.20), channel_id=1, source_target_pairs={{0,3},{1,2},{2,1},{3,0},{4,7},{5,6},{6,5},{7,4},{8,11},{9,10},{10,... | collective-permute-start | bytes 196616 | tf_op jit(solution)/shard_map/ppermute | solution.py:386
  10.6 7.1 %collective-permute-start.2 = (f32[2,64,128]{2,1,0:T(8,128)S(1)}, f32[2,64,128]{2,1,0:T(8,128)S(1)}, u32[]{:S(2)}, u32[]{:S(2)}) collective-permute-start(f32[2,64,128]{2,1,0:T(8,128)S(1)} %collective-permute-done.1.refs_0_), channel_id=1, source_target_pairs={{0,16},{4,20},{8,24},{12,28},{16,0},{20,4},{24,8},{28,12},{1,17},{... | collective-permute-start | bytes 196616 | tf_op jit(solution)/shard_map/ppermute | solution.py:386
  13.2 5.4 %collective-permute-start.4 = (f32[2,64,128]{2,1,0:T(8,128)S(1)}, f32[2,64,128]{2,1,0:T(8,128)S(1)}, u32[]{:S(2)}, u32[]{:S(2)}) collective-permute-start(f32[2,64,128]{2,1,0:T(8,128)S(1)} %low_gate.1.own_ref), channel_id=1, source_target_pairs={{0,16},{4,20},{8,24},{12,28},{16,0},{20,4},{24,8},{28,12},{1,17},{... | collective-permute-start | bytes 196616 | tf_op jit(solution)/shard_map/ppermute | solution.py:386
  14.0 4.6 %collective-permute-start.5 = (f32[2,64,128]{2,1,0:T(8,128)S(1)}, f32[2,64,128]{2,1,0:T(8,128)S(1)}, u32[]{:S(2)}, u32[]{:S(2)}) collective-permute-start(f32[2,64,128]{2,1,0:T(8,128)S(1)} %mix_pair.1), channel_id=1, source_target_pairs={{0,1},{1,0},{2,3},{3,2},{4,5},{5,4},{6,7},{7,6},{8,9},{9,8},{10,11... | collective-permute-start | bytes 196616 | tf_op jit(solution)/shard_map/ppermute | solution.py:386

commit v9 on v8

--- a/solution.py
+++ b/solution.py
@@ -283,10 +283,7 @@
         out_ref[i] = block_matrix(real, -imag).astype(BF16)
 
 
-def high_weights_kernel(lo_bits, orders_ref, gates_hbm, early_ref, late_ref, gates_ref, sems):
-    fetches = [pltpu.make_async_copy(gates_hbm.at[2 + 2 * g], gates_ref.at[g], sems.at[g]) for g in range(2)]
-    for fetch in fetches:
-        fetch.start()
+def high_weights_kernel(lo_bits, orders_ref, gates_ref, early_ref, late_ref):
     parts = 1 << lo_bits
     kept = WIDTH // parts
     me = lax.axis_index("lo")
@@ -296,15 +293,13 @@
     for place, step in enumerate(early + late):
         source = source + jnp.where(index // kept == place, jnp.bitwise_xor(me, step) * kept, 0)
     rows = one_hot(WIDTH, source)
-    for fetch in fetches:
-        fetch.wait()
 
     def exact(left, right):
         return lax.dot_general(
             left, right, (((1,), (0,)), ((), ())), precision=lax.Precision.HIGHEST, preferred_element_type=F32
         )
 
-    first, last = [[gates_ref[g, c] for c in range(2)] for g in range(2)]
+    first, last = [[gates_ref[g, c] for c in range(2)] for g in (2, 4)]
     real = halves(exact(last[0], first[0]) - exact(last[1], first[1]))
     imag = halves(exact(last[0], first[1]) + exact(last[1], first[0]))
     half = len(early) * kept
@@ -435,12 +430,11 @@
     early_weights, late_weights = pl.pallas_call(
         functools.partial(high_weights_kernel, lo_bits),
         out_shape=[pltpu.VMEM((2, 256, count), BF16) for count in counts],
-        in_specs=[VMEM, HBM],
+        in_specs=[VMEM, VMEM],
         out_specs=[VMEM] * 2,
-        scratch_shapes=[pltpu.VMEM((2, 2, WIDTH, WIDTH), F32), pltpu.SemaphoreType.DMA((2,))],
         compiler_params=PARAMS,
         name="high_weights",
-    )(orders, in_hbm(gate_mats))
+    )(orders, gate_mats)
     far_own[-1] = pl.pallas_call(
         low_kernel, out_shape=block, in_specs=[VMEM] * 2, out_specs=VMEM, compiler_params=PARAMS, name="low_gate"
     )(low_weights, far_own[-1])

time: 19.8 us -> 19.8 us (level)
  Pallas kernels: 6.98 us -> 5.98 us
  waiting for transfers between devices: 3.03 us -> 4.01 us
    pallas_call x1, Pallas kernels: 1.61 us -> 0.62 us  [on_device(): pl.pallas_call(functools.partial(high_weights_kernel, lo_bits), out_shape...]
    ppermute x6, waiting for transfers between devices: 3.03 us -> 4.01 us  [swapped(): return lax.ppermute(block, axis, [(i, i ^ distance) for i in range(count)])]
  transfers between devices with their start and end apart: 6 -> 6, of which waited for: 4 -> 4; matrix products, arithmetic and copies ran while one was open for 0% -> 0% of each run, Pallas kernels for 19% -> 14%
where the time goes in v9:
time: 19.8 us; the launch traced here: 19.6 us
  starting transfers between devices  9.54 us (48%)
  Pallas kernels  5.98 us (30%)
  waiting for transfers between devices  4.01 us (20%)
    ppermute x6, starting transfers between devices, swapped(): return lax.ppermute(block, axis, [(i, i ^ distance) for i in range(count)])  9.54 us
    ppermute x6, waiting for transfers between devices, swapped(): return lax.ppermute(block, axis, [(i, i ^ distance) for i in range(count)])  4.01 us
    pallas_call x1, Pallas kernels, on_device(): pl.pallas_call(functools.partial(first_kernel, lo_bits), out_shape=[pltpu...  2.26 us
    pallas_call x1, Pallas kernels, on_device(): pl.pallas_call(low_weights_kernel, out_shape=[pltpu.VMEM((2, 256, 256), B...  1.23 us
    pallas_call x1, Pallas kernels, on_device(): pl.pallas_call(last_kernel, out_shape=jax.ShapeDtypeStruct((512, WIDTH),...  0.97 us
    pallas_call x1, Pallas kernels, on_device(): pl.pallas_call(functools.partial(high_weights_kernel, lo_bits), out_shape...  0.62 us
    pallas_call x1, Pallas kernels, on_device(): pl.pallas_call(early_kernel, out_shape=pltpu.VMEM((256, 256), F32), in_sp...  0.54 us
  transfers between devices with their start and end apart: 6, of which 4 were waited for; matrix products, arithmetic and copies ran while one was open for 0% of the time, Pallas kernels for 14%

profile of v9, /device:TPU:0, one launch (start us, length us, event | category | flops | bytes accessed | tf_op | source)
XLA Modules:
  0.0 19.6 jit_solution(10367531100119900111)
XLA Ops:
  0.0 2.3 %first_gates.1 = (f32[2,2,64,128]{3,2,1,0:T(8,128)S(1)}, f32[2,64,128]{2,1,0:T(8,128)S(1)}, f32[2,64,128]{2,1,0:T(8,128)S(1)}, s32[2,8,128]{2,1,0:T(8,128)S(1)}) custom-call(s32[15]{0:T(128)} %order_hbm.1, f32[512,128]{1,0:T(8,128)} %bitcast.10, f32[5,2,128,128]{3,2,1,0:T(8,128)} %gates_ref.1), custom_call_target="tpu_custom_call" | custom-call | tf_op jit(solution)/shard_map/first_gates/pallas_call | solution.py:401
  2.3 4.1 %collective-permute-start = (f32[2,2,64,128]{3,2,1,0:T(8,128)S(1)}, f32[2,2,64,128]{3,2,1,0:T(8,128)S(1)}, u32[]{:S(2)}, u32[]{:S(2)}) collective-permute-start(f32[2,2,64,128]{3,2,1,0:T(8,128)S(1)} %get-tuple-element.18.near_own_ref.own_ref), channel_id=1, source_target_pairs={{0,16},{4,20},{8,24},{12,28},{16,0},{20,4},{24,8},{28,12},{1,17},{... | collective-permute-start | bytes 393224 | tf_op jit(solution)/shard_map/ppermute | solution.py:381
  6.4 1.5 %collective-permute-start.1 = (f32[2,64,128]{2,1,0:T(8,128)S(1)}, f32[2,64,128]{2,1,0:T(8,128)S(1)}, u32[]{:S(2)}, u32[]{:S(2)}) collective-permute-start(f32[2,64,128]{2,1,0:T(8,128)S(1)} %get-tuple-element.19), channel_id=1, source_target_pairs={{0,2},{1,3},{2,0},{3,1},{4,6},{5,7},{6,4},{7,5},{8,10},{9,11},{10,... | collective-permute-start | bytes 196616 | tf_op jit(solution)/shard_map/ppermute | solution.py:381
  7.9 1.4 %collective-permute-start.3 = (f32[2,64,128]{2,1,0:T(8,128)S(1)}, f32[2,64,128]{2,1,0:T(8,128)S(1)}, u32[]{:S(2)}, u32[]{:S(2)}) collective-permute-start(f32[2,64,128]{2,1,0:T(8,128)S(1)} %get-tuple-element.20), channel_id=1, source_target_pairs={{0,3},{1,2},{2,1},{3,0},{4,7},{5,6},{6,5},{7,4},{8,11},{9,10},{10,... | collective-permute-start | bytes 196616 | tf_op jit(solution)/shard_map/ppermute | solution.py:381
  9.3 1.2 %low_weights.1 = (bf16[2,256,256]{2,1,0:T(8,128)(2,1)S(1)}, f32[4,8,128]{2,1,0:T(8,128)S(1)}) custom-call(s32[2,8,128]{2,1,0:T(8,128)S(1)} %get-tuple-element.13.orders_ref, f32[2,2,2]{2,1,0:T(2,128)} %gate_hbm.1, f32[5,2,128,128]{3,2,1,0:T(8,128)} %gates_ref.1), custom_call_target="tpu_custom_call" | custom-call | tf_op jit(solution)/shard_map/low_weights/pallas_call | solution.py:421
  10.6 0.0 copy-start
  10.6 0.1 collective-permute-done.1.refs_0_
  10.6 0.3 %collective-permute-start.2 = (f32[2,64,128]{2,1,0:T(8,128)S(1)}, f32[2,64,128]{2,1,0:T(8,128)S(1)}, u32[]{:S(2)}, u32[]{:S(2)}) collective-permute-start(f32[2,64,128]{2,1,0:T(8,128)S(1)} %collective-permute-done.1.refs_0_), channel_id=1, source_target_pairs={{0,16},{4,20},{8,24},{12,28},{16,0},{20,4},{24,8},{28,12},{1,17},{... | collective-permute-start | bytes 196616 | tf_op jit(solution)/shard_map/ppermute | solution.py:381
  11.0 2.1 %collective-permute-done.3.in_ref = f32[2,64,128]{2,1,0:T(8,128)S(1)} collective-permute-done((f32[2,64,128]{2,1,0:T(8,128)S(1)}, f32[2,64,128]{2,1,0:T(8,128)S(1)}, u32[]{:S(2)}, u32[]{:S(2)}) %collective-permute-start.3) | collective-permute-done | bytes 65568 | tf_op jit(solution)/shard_map/ppermute | solution.py:381
  13.1 0.2 low_gate.1.own_ref
  13.2 0.6 %collective-permute-start.4 = (f32[2,64,128]{2,1,0:T(8,128)S(1)}, f32[2,64,128]{2,1,0:T(8,128)S(1)}, u32[]{:S(2)}, u32[]{:S(2)}) collective-permute-start(f32[2,64,128]{2,1,0:T(8,128)S(1)} %low_gate.1.own_ref), channel_id=1, source_target_pairs={{0,16},{4,20},{8,24},{12,28},{16,0},{20,4},{24,8},{28,12},{1,17},{... | collective-permute-start | bytes 196616 | tf_op jit(solution)/shard_map/ppermute | solution.py:381
  13.8 0.0 collective-permute-done.near_other_ref.other_ref
  13.8 0.2 mix_pair.1
  14.0 1.5 %collective-permute-start.5 = (f32[2,64,128]{2,1,0:T(8,128)S(1)}, f32[2,64,128]{2,1,0:T(8,128)S(1)}, u32[]{:S(2)}, u32[]{:S(2)}) collective-permute-start(f32[2,64,128]{2,1,0:T(8,128)S(1)} %mix_pair.1), channel_id=1, source_target_pairs={{0,1},{1,0},{2,3},{3,2},{4,5},{5,4},{6,7},{7,6},{8,9},{9,8},{10,11... | collective-permute-start | bytes 196616 | tf_op jit(solution)/shard_map/ppermute | solution.py:381
  15.6 0.0 copy-done
  15.6 0.6 %high_weights.1 = (bf16[2,256,128]{2,1,0:T(8,128)(2,1)S(1)}, bf16[2,256,128]{2,1,0:T(8,128)(2,1)S(1)}) custom-call(s32[2,8,128]{2,1,0:T(8,128)S(1)} %get-tuple-element.13.orders_ref, f32[5,2,128,128]{3,2,1,0:T(8,128)S(1)} %copy-done), custom_call_target="tpu_custom_call" | custom-call | tf_op jit(solution)/shard_map/high_weights/pallas_call | solution.py:430
  16.2 1.6 %collective-permute-done.2.in_ref = f32[2,64,128]{2,1,0:T(8,128)S(1)} collective-permute-done((f32[2,64,128]{2,1,0:T(8,128)S(1)}, f32[2,64,128]{2,1,0:T(8,128)S(1)}, u32[]{:S(2)}, u32[]{:S(2)}) %collective-permute-start.2) | collective-permute-done | bytes 65568 | tf_op jit(solution)/shard_map/ppermute | solution.py:381
  17.8 0.5 %early_gate.1.early_ref = f32[256,256]{1,0:T(8,128)S(1)} custom-call(f32[4,8,128]{2,1,0:T(8,128)S(1)} %get-tuple-element.14.coefs_ref, bf16[2,256,256]{2,1,0:T(8,128)(2,1)S(1)} %get-tuple-element.16.low_gate_ref.matrix_ref, bf16[2,256,128]{2,1,0:T(8,128)(2,1)S(1)} %get-tuple-element.17.high_gate_ref, ...), custom_call_target="tpu_custom_call" | custom-call | tf_op jit(solution)/shard_map/early_gate/pallas_call | solution.py:455
  18.4 0.3 %collective-permute-done.4.other_ref = f32[2,64,128]{2,1,0:T(8,128)S(1)} collective-permute-done((f32[2,64,128]{2,1,0:T(8,128)S(1)}, f32[2,64,128]{2,1,0:T(8,128)S(1)}, u32[]{:S(2)}, u32[]{:S(2)}) %collective-permute-start.4) | collective-permute-done | bytes 65568 | tf_op jit(solution)/shard_map/ppermute | solution.py:381
  18.6 0.0 collective-permute-done.5.refs_0_
  18.6 1.0 %last_gates.1 = f32[512,128]{1,0:T(8,128)} custom-call(f32[4,8,128]{2,1,0:T(8,128)S(1)} %get-tuple-element.14.coefs_ref, bf16[2,256,128]{2,1,0:T(8,128)(2,1)S(1)} %get-tuple-element.15.high_gate_ref, f32[256,256]{1,0:T(8,128)S(1)} %early_gate.1.early_ref, f32[2,64,128]{2,1,0:T(8,128)S(1)} %low_gate.1.own_ref, ...), custom_call_target="tpu_custom_call" | custom-call | tf_op jit(solution)/shard_map/last_gates/pallas_call | solution.py:463
  (1 shorter events, 0.0 us)
Async XLA Ops:
  2.3 11.6 %collective-permute-start = (f32[2,2,64,128]{3,2,1,0:T(8,128)S(1)}, f32[2,2,64,128]{3,2,1,0:T(8,128)S(1)}, u32[]{:S(2)}, u32[]{:S(2)}) collective-permute-start(f32[2,2,64,128]{3,2,1,0:T(8,128)S(1)} %get-tuple-element.18.near_own_ref.own_ref), channel_id=1, source_target_pairs={{0,16},{4,20},{8,24},{12,28},{16,0},{20,4},{24,8},{28,12},{1,17},{... | collective-permute-start | bytes 393224 | tf_op jit(solution)/shard_map/ppermute | solution.py:381
  6.4 4.3 %collective-permute-start.1 = (f32[2,64,128]{2,1,0:T(8,128)S(1)}, f32[2,64,128]{2,1,0:T(8,128)S(1)}, u32[]{:S(2)}, u32[]{:S(2)}) collective-permute-start(f32[2,64,128]{2,1,0:T(8,128)S(1)} %get-tuple-element.19), channel_id=1, source_target_pairs={{0,2},{1,3},{2,0},{3,1},{4,6},{5,7},{6,4},{7,5},{8,10},{9,11},{10,... | collective-permute-start | bytes 196616 | tf_op jit(solution)/shard_map/ppermute | solution.py:381
  7.9 5.2 %collective-permute-start.3 = (f32[2,64,128]{2,1,0:T(8,128)S(1)}, f32[2,64,128]{2,1,0:T(8,128)S(1)}, u32[]{:S(2)}, u32[]{:S(2)}) collective-permute-start(f32[2,64,128]{2,1,0:T(8,128)S(1)} %get-tuple-element.20), channel_id=1, source_target_pairs={{0,3},{1,2},{2,1},{3,0},{4,7},{5,6},{6,5},{7,4},{8,11},{9,10},{10,... | collective-permute-start | bytes 196616 | tf_op jit(solution)/shard_map/ppermute | solution.py:381
  10.6 5.0 %copy-start = (f32[5,2,128,128]{3,2,1,0:T(8,128)S(1)}, f32[5,2,128,128]{3,2,1,0:T(8,128)}, u32[]{:S(2)}) copy-start(f32[5,2,128,128]{3,2,1,0:T(8,128)} %gates_ref.1) | copy-start | bytes 1966084
  10.6 7.2 %collective-permute-start.2 = (f32[2,64,128]{2,1,0:T(8,128)S(1)}, f32[2,64,128]{2,1,0:T(8,128)S(1)}, u32[]{:S(2)}, u32[]{:S(2)}) collective-permute-start(f32[2,64,128]{2,1,0:T(8,128)S(1)} %collective-permute-done.1.refs_0_), channel_id=1, source_target_pairs={{0,16},{4,20},{8,24},{12,28},{16,0},{20,4},{24,8},{28,12},{1,17},{... | collective-permute-start | bytes 196616 | tf_op jit(solution)/shard_map/ppermute | solution.py:381
  13.2 5.4 %collective-permute-start.4 = (f32[2,64,128]{2,1,0:T(8,128)S(1)}, f32[2,64,128]{2,1,0:T(8,128)S(1)}, u32[]{:S(2)}, u32[]{:S(2)}) collective-permute-start(f32[2,64,128]{2,1,0:T(8,128)S(1)} %low_gate.1.own_ref), channel_id=1, source_target_pairs={{0,16},{4,20},{8,24},{12,28},{16,0},{20,4},{24,8},{28,12},{1,17},{... | collective-permute-start | bytes 196616 | tf_op jit(solution)/shard_map/ppermute | solution.py:381
  14.0 4.6 %collective-permute-start.5 = (f32[2,64,128]{2,1,0:T(8,128)S(1)}, f32[2,64,128]{2,1,0:T(8,128)S(1)}, u32[]{:S(2)}, u32[]{:S(2)}) collective-permute-start(f32[2,64,128]{2,1,0:T(8,128)S(1)} %mix_pair.1), channel_id=1, source_target_pairs={{0,1},{1,0},{2,3},{3,2},{4,5},{5,4},{6,7},{7,6},{8,9},{9,8},{10,11... | collective-permute-start | bytes 196616 | tf_op jit(solution)/shard_map/ppermute | solution.py:381
